TPU v7x, 128 devices: a whole 4x4x4 slice. The times are simulated.
128 devices in a mesh: dp: 16 (over y, x), owner: 8 (over z, core).
Axes of the slice: x: 4, y: 4, z: 4, core: 2. Of those that a mesh axis runs over, the one named last changes fastest.
Arguments:
- grad_part: bfloat16 [16, 16, 64, 12288], P('dp', None, 'owner'), may hold values from -0.29882812 to 0.29882812
- block_slot: int32 [12], replicated, may hold values from 0 to 23, as said below
- left_factor: float32 [24, 1024, 1024], P('owner', 'dp'), may hold values from -6 to 6
- right_factor: float32 [24, 1024, 1024], P('owner', 'dp'), may hold values from -6 to 6
- first_moment: bfloat16 [24, 1024, 1024], P('owner', 'dp'), may hold values from -0.59765625 to 0.59765625
- second_moment: bfloat16 [24, 1024, 1024], P('owner', 'dp'), may hold values from 0.0009994507 to 0.029907227
- left_basis: bfloat16 [24, 1024, 1024], P('owner'), may hold values from -0.1875 to 0.1875
- right_basis: bfloat16 [24, 1024, 1024], P('owner'), may hold values from -0.1875 to 0.1875
Outputs:
- new_left: float32 [24, 1024, 1024], P('owner', 'dp')
- new_right: float32 [24, 1024, 1024], P('owner', 'dp')
- new_first: bfloat16 [24, 1024, 1024], P('owner', 'dp')
- new_second: bfloat16 [24, 1024, 1024], P('owner', 'dp')
- update: bfloat16 [1024, 12288], P(('dp', 'owner'))
Inputs may be any that keep to these rules, and one draw needn't show every extreme that they name: `block_slot`: the numbers are distinct; slot q belongs to owner q // 3; in every draw one owner holds 3 blocks.
All inputs are finite; a program needn't handle non-finite values.
Results may differ from a plain program's by a relative error of at most 0.02.
Values may be sent and summed in bfloat16 or wider, within the bound.
No kernel may reach another device: no remote copies, remote signals or barrier semaphores. Data moves between devices by JAX's collectives and lax.ppermute only.
A program may use at most 128 MiB of HBM per device.

v0:
```python
import jax
import jax.numpy as jnp
from jax import lax
from jax.sharding import PartitionSpec as P

BETA_FIRST = 0.9
BETA_SECOND = 0.95
BETA_FACTOR = 0.95
EPSILON = 1e-08


def rotate_back(direction, basis_left, basis_right, mine_dp, slab_rows):
    back_half = lax.dot_general(
        direction, basis_right, (((1,), (1,)), ((), ())), preferred_element_type=jnp.float32
    ).astype(jnp.bfloat16)
    whole_half = lax.all_gather(back_half, "dp", axis=0, tiled=True)
    basis_rows = lax.dynamic_slice_in_dim(basis_left, mine_dp * slab_rows, slab_rows, 0)
    return jnp.dot(basis_rows, whole_half, preferred_element_type=jnp.float32)


def on_device(
    grad_part,
    block_slot,
    left_factor,
    right_factor,
    first_moment,
    second_moment,
    left_basis,
    right_basis,
):
    owners = lax.axis_size("owner")
    mine_dp = lax.axis_index("dp")
    mine_owner = lax.axis_index("owner")
    slot_count, slab_rows, block_order = left_factor.shape
    part_rows = grad_part.shape[2]
    strip_width = grad_part.shape[3]
    block_total = strip_width // block_order
    summed = lax.psum_scatter(
        grad_part[0].astype(jnp.float32).astype(jnp.bfloat16), "dp", scatter_dimension=0, tiled=True
    ).astype(jnp.float32)
    gradient = summed[0].astype(jnp.bfloat16).reshape(part_rows, block_total, block_order)
    slot_ids = jnp.arange(owners * slot_count, dtype=jnp.int32)
    matches = block_slot[None, :] == slot_ids[:, None]
    filled = jnp.any(matches, axis=1)
    holder = jnp.sum(
        jnp.where(matches, jnp.arange(block_total, dtype=jnp.int32)[None, :], 0), axis=1
    )
    outgoing = jnp.where(
        filled[None, :, None], jnp.take(gradient, holder, axis=1), jnp.zeros((), jnp.bfloat16)
    )
    outgoing = outgoing.reshape(part_rows, owners, slot_count, block_order)
    incoming = lax.all_to_all(outgoing, "owner", split_axis=1, concat_axis=0, tiled=True).reshape(
        slab_rows, slot_count, block_order
    )
    occupied = lax.dynamic_slice_in_dim(filled, mine_owner * slot_count, slot_count)
    grad_slabs = [incoming[:, position, :] for position in range(slot_count)]
    moment_slabs = [
        (
            BETA_FIRST * first_moment[position].astype(jnp.float32)
            + (1.0 - BETA_FIRST) * grad_slabs[position].astype(jnp.float32)
        ).astype(jnp.bfloat16)
        for position in range(slot_count)
    ]
    gathered = [
        (
            lax.all_gather(grad_slabs[position], "dp", axis=0, tiled=True),
            lax.all_gather(moment_slabs[position], "dp", axis=0, tiled=True),
        )
        for position in range(slot_count)
    ]
    lefts = []
    rights = []
    firsts = []
    seconds = []
    step_slabs = []
    col_start = mine_dp * slab_rows
    for position in range(slot_count):
        grad_rows = grad_slabs[position]
        full_grad, full_moment = gathered[position]
        basis_left = left_basis[position]
        basis_right = right_basis[position]
        gram_left = lax.dot_general(
            grad_rows, full_grad, (((1,), (1,)), ((), ())), preferred_element_type=jnp.float32
        )
        grad_cols = lax.dynamic_slice_in_dim(full_grad, col_start, slab_rows, 1)
        gram_right = lax.dot_general(
            grad_cols, full_grad, (((0,), (0,)), ((), ())), preferred_element_type=jnp.float32
        )
        basis_cols = lax.dynamic_slice_in_dim(basis_left, col_start, slab_rows, 1)
        half_grad = lax.dot_general(
            basis_cols, full_grad, (((0,), (0,)), ((), ())), preferred_element_type=jnp.float32
        ).astype(jnp.bfloat16)
        rot_grad = jnp.dot(half_grad, basis_right, preferred_element_type=jnp.float32)
        half_mom = lax.dot_general(
            basis_cols, full_moment, (((0,), (0,)), ((), ())), preferred_element_type=jnp.float32
        ).astype(jnp.bfloat16)
        rot_mom = jnp.dot(half_mom, basis_right, preferred_element_type=jnp.float32)
        variance = (
            BETA_SECOND * second_moment[position].astype(jnp.float32)
            + (1.0 - BETA_SECOND) * rot_grad * rot_grad
        )
        direction = (rot_mom / (jnp.sqrt(variance) + EPSILON)).astype(jnp.bfloat16)
        step_rows = rotate_back(direction, basis_left, basis_right, mine_dp, slab_rows).astype(
            jnp.bfloat16
        )
        is_used = occupied[position]
        lefts.append(
            jnp.where(
                is_used,
                BETA_FACTOR * left_factor[position] + (1.0 - BETA_FACTOR) * gram_left,
                jnp.zeros((), jnp.float32),
            )
        )
        rights.append(
            jnp.where(
                is_used,
                BETA_FACTOR * right_factor[position] + (1.0 - BETA_FACTOR) * gram_right,
                jnp.zeros((), jnp.float32),
            )
        )
        firsts.append(jnp.where(is_used, moment_slabs[position], jnp.zeros((), jnp.bfloat16)))
        seconds.append(
            jnp.where(is_used, variance.astype(jnp.bfloat16), jnp.zeros((), jnp.bfloat16))
        )
        step_slabs.append(step_rows)
    step_stack = jnp.stack(step_slabs).reshape(slot_count, owners, part_rows, block_order)
    returned = lax.all_to_all(step_stack, "owner", split_axis=1, concat_axis=0, tiled=True)
    picked = jnp.take(returned[:, 0], block_slot, axis=0)
    update = jnp.transpose(picked, (1, 0, 2)).reshape(part_rows, strip_width)
    return (jnp.stack(lefts), jnp.stack(rights), jnp.stack(firsts), jnp.stack(seconds), update)


def solution(mesh):
    placed = (
        P("dp", None, "owner", None),
        P(),
        P("owner", "dp", None),
        P("owner", "dp", None),
        P("owner", "dp", None),
        P("owner", "dp", None),
        P("owner", None, None),
        P("owner", None, None),
    )
    return jax.shard_map(
        on_device,
        mesh=mesh,
        in_specs=placed,
        out_specs=(
            P("owner", "dp", None),
            P("owner", "dp", None),
            P("owner", "dp", None),
            P("owner", "dp", None),
            P(("dp", "owner"), None),
        ),
        check_vma=False,
    )
```

profile of v0, /device:TPU:1, one launch (start us, length us, event | category | flops | bytes accessed | tf_op | source)
XLA Modules:
  0.0 546.4 jit_solution(5530618619533273662)
XLA Ops:
  7.2 0.7 reduce-scatter.4.cloned.1.call-update
  7.9 0.0 all-gather.13.cloned.1.call-start
  8.0 0.1 select_reduce_fusion
  8.1 0.1 reduce_sum.14
  8.1 0.1 fusion.252
  8.2 0.1 broadcast_in_dim.72
  8.4 80.3 %reduce-scatter.4.cloned.1.call-done = bf16[1,8,12288]{2,1,0:T(8,128)(2,1)} async-done(((bf16[16,8,12288]{2,1,0:T(8,128)(2,1)}), bf16[1,8,12288]{2,1,0:T(8,128)(2,1)}) %reduce-scatter.4.cloned.1.call-update) | async-done | bytes 196624
  88.6 1.5 gather_fusion
  90.1 0.1 select_select_fusion
  90.3 14.6 %all_to_all.30 = bf16[8,8,3,1024]{3,0,2,1:T(8,128)(2,1)S(1)} all-to-all(bf16[8,8,3,1024]{3,0,2,1:T(8,128)(2,1)S(1)} %select_select_fusion), channel_id=1, replica_groups=mesh['dp'=16,'owner'=8] {'owner'}, dimensions={1} | all-to-all | bytes 786432 | tf_op jit(solution)/shard_map/all_to_all | solution.py:52
  105.0 0.8 fusion.203
  105.8 0.0 all-gather.25.cloned.1.call-start
  105.9 0.8 fusion.276
  106.7 0.0 all-gather.17.cloned.1.call-start
  106.7 0.5 all-gather.17.cloned.1.call-update
  107.3 0.5 all-gather.27.cloned.1.call-update
  107.9 0.5 all-gather.21.cloned.1.call-update
  108.4 0.7 all-gather.29.cloned.1.call-update
  109.1 0.0 all-gather.15.cloned.1.call-start
  109.2 5.9 %fusion.275 = (bf16[1,1024,1024]{2,1,0:T(8,128)(2,1)}, bf16[1,1024,1024]{2,1,0:T(8,128)(2,1)S(1)}, bf16[1,1024,1024]{2,1,0:T(8,128)(2,1)}) fusion(bf16[3,1024,1024]{2,1,0:T(8,128)(2,1)} %param.14), kind=kLoop, calls=%fused_computation.192 | loop fusion | bytes 12582912 | tf_op jit(solution)/shard_map/slice | solution.py:80
  115.1 32.4 %all-gather.13.cloned.1.call-done = bf16[1024,1024]{1,0:T(8,128)(2,1)} async-done(((bf16[64,1024]{1,0:T(8,128)(2,1)}), bf16[1024,1024]{1,0:T(8,128)(2,1)}) %all-gather.13.cloned.1.call-update) | async-done | bytes 2097168 | tf_op jit(solution)/shard_map/all_gather | solution.py:67
  147.5 2.3 convolution_convert_fusion.2
  149.8 44.6 %all-gather.25.cloned.1.call-done = bf16[1024,1,1024]{2,0,1:T(8,128)(2,1)} async-done(((bf16[64,1,1024]{2,0,1:T(8,128)(2,1)}), bf16[1024,1,1024]{2,0,1:T(8,128)(2,1)}) %all-gather.25.cloned.1.call-update) | async-done | bytes 2097168 | tf_op jit(solution)/shard_map/all_gather | solution.py:66
  194.4 3.3 fusion.196
  197.7 4.0 fusion.150
  201.8 0.0 all-gather.19.cloned.1.call-start
  201.8 39.4 %all-gather.17.cloned.1.call-done = bf16[1024,1024]{1,0:T(8,128)(2,1)} async-done(((bf16[64,1024]{1,0:T(8,128)(2,1)}), bf16[1024,1024]{1,0:T(8,128)(2,1)}) %all-gather.17.cloned.1.call-update) | async-done | bytes 2097168 | tf_op jit(solution)/shard_map/all_gather | solution.py:67
  241.2 2.3 convolution_convert_fusion.1
  243.5 44.5 %all-gather.27.cloned.1.call-done = bf16[1024,1,1024]{2,0,1:T(8,128)(2,1)} async-done(((bf16[64,1,1024]{2,0,1:T(8,128)(2,1)}), bf16[1024,1,1024]{2,0,1:T(8,128)(2,1)}) %all-gather.27.cloned.1.call-update) | async-done | bytes 2097168 | tf_op jit(solution)/shard_map/all_gather | solution.py:66
  288.0 3.3 fusion.187
  291.3 4.0 fusion.155
  295.4 0.0 all-gather.23.cloned.1.call-start
  295.4 38.8 %all-gather.21.cloned.1.call-done = bf16[1024,1024]{1,0:T(8,128)(2,1)} async-done(((bf16[64,1024]{1,0:T(8,128)(2,1)}), bf16[1024,1024]{1,0:T(8,128)(2,1)}) %all-gather.21.cloned.1.call-update) | async-done | bytes 2097168 | tf_op jit(solution)/shard_map/all_gather | solution.py:67
  334.2 2.2 convolution_convert_fusion
  336.4 44.7 %all-gather.29.cloned.1.call-done = bf16[1024,1,1024]{2,0,1:T(8,128)(2,1)} async-done(((bf16[64,1,1024]{2,0,1:T(8,128)(2,1)}), bf16[1024,1,1024]{2,0,1:T(8,128)(2,1)}) %all-gather.29.cloned.1.call-update) | async-done | bytes 2097168 | tf_op jit(solution)/shard_map/all_gather | solution.py:66
  381.1 4.0 fusion.178
  385.1 4.1 fusion.160
  389.3 0.1 dynamic_slice.42
  389.3 0.7 fusion.277
  390.0 2.2 fusion.237
  392.2 0.8 pad_maximum_fusion.2
  393.0 1.6 select_bitcast_fusion
  394.7 0.8 select_bitcast_fusion.1
  395.5 0.7 select_bitcast_fusion.2
  396.2 0.8 pad_maximum_fusion.3
  397.0 1.5 fusion.111
  398.5 1.3 fusion.117
  399.8 1.4 fusion.123
  401.2 1.0 pad_maximum_fusion.1
  402.1 1.5 fusion.54
  403.6 1.4 fusion.72
  405.0 22.6 %all-gather.15.cloned.1.call-done = bf16[1024,1024]{1,0:T(8,128)(2,1)} async-done(((bf16[64,1024]{1,0:T(8,128)(2,1)}), bf16[1024,1024]{1,0:T(8,128)(2,1)}) %all-gather.15.cloned.1.call-update) | async-done | bytes 2097168 | tf_op jit(solution)/shard_map/all_gather | solution.py:16
  427.5 2.1 fusion.171
  429.7 44.8 %all-gather.19.cloned.1.call-done = bf16[1024,1024]{1,0:T(8,128)(2,1)} async-done(((bf16[64,1024]{1,0:T(8,128)(2,1)}), bf16[1024,1024]{1,0:T(8,128)(2,1)}) %all-gather.19.cloned.1.call-update) | async-done | bytes 2097168 | tf_op jit(solution)/shard_map/all_gather | solution.py:16
  474.5 2.1 fusion.172
  476.6 44.6 %all-gather.23.cloned.1.call-done = bf16[1024,1024]{1,0:T(8,128)(2,1)} async-done(((bf16[64,1024]{1,0:T(8,128)(2,1)}), bf16[1024,1024]{1,0:T(8,128)(2,1)}) %all-gather.23.cloned.1.call-update) | async-done | bytes 2097168 | tf_op jit(solution)/shard_map/all_gather | solution.py:16
  521.2 2.1 fusion.173
  523.4 0.8 pad_maximum_fusion.4
  524.2 5.9 %all-to-all-start.1 = ((bf16[3,8,8,1024]{3,2,0,1:T(8,128)(2,1)}), bf16[3,8,8,1024]{3,2,0,1:T(8,128)(2,1)S(1)}, u32[]{:S(2)}, u32[]{:S(2)}) async-start(bf16[3,8,8,1024]{3,2,0,1:T(8,128)(2,1)} %pad_maximum_fusion.4), calls=%async_computation.1 | async-start | bytes 786432 | tf_op jit(solution)/shard_map/all_to_all | solution.py:127
  530.1 2.4 fusion.90
  532.5 0.9 pad_maximum_fusion
  533.5 4.7 all-to-all-done.1
  538.2 0.6 gather_fusion.1
  538.8 0.8 broadcast_select_fusion
  (32 shorter events, 0.3 us)
Async XLA Ops:
  7.2 0.8 copy-start.7
  7.2 81.5 %reduce-scatter.4.cloned.1.call-start = ((), (), s32[]{:S(2)}) async-start(), calls=%async_computation.12 | async-start | bytes 3342336
  7.9 97.0 %copy-start.4 = (bf16[3,64,1024]{2,1,0:T(8,128)(2,1)S(1)}, bf16[3,64,1024]{2,1,0:T(8,128)(2,1)}, u32[]{:S(2)}) copy-start(bf16[3,64,1024]{2,1,0:T(8,128)(2,1)} %param.12) | copy-start | bytes 1179652
  7.9 139.5 %all-gather.13.cloned.1.call-start = ((), (), s32[]{:S(2)}) async-start(), calls=%async_computation.3 | async-start | bytes 2228224 | tf_op jit(solution)/shard_map/all_gather | solution.py:67
  105.8 88.6 %all-gather.25.cloned.1.call-start = ((), (), s32[]{:S(2)}) async-start(), calls=%async_computation.9 | async-start | bytes 2228224 | tf_op jit(solution)/shard_map/all_gather | solution.py:66
  106.7 134.5 %all-gather.17.cloned.1.call-start = ((), (), s32[]{:S(2)}) async-start(), calls=%async_computation.5 | async-start | bytes 2228224 | tf_op jit(solution)/shard_map/all_gather | solution.py:67
  107.2 180.7 %all-gather.27.cloned.1.call-start = ((), (), s32[]{:S(2)}) async-start(), calls=%async_computation.10 | async-start | bytes 2228224 | tf_op jit(solution)/shard_map/all_gather | solution.py:66
  107.8 226.4 %all-gather.21.cloned.1.call-start = ((), (), s32[]{:S(2)}) async-start(), calls=%async_computation.7 | async-start | bytes 2228224 | tf_op jit(solution)/shard_map/all_gather | solution.py:67
  108.4 272.7 %all-gather.29.cloned.1.call-start = ((), (), s32[]{:S(2)}) async-start(), calls=%async_computation.11 | async-start | bytes 2228224 | tf_op jit(solution)/shard_map/all_gather | solution.py:66
  109.1 318.4 %all-gather.15.cloned.1.call-start = ((), (), s32[]{:S(2)}) async-start(), calls=%async_computation.4 | async-start | bytes 2228224 | tf_op jit(solution)/shard_map/all_gather | solution.py:16
  115.1 266.1 %copy-start.3 = (bf16[1,1024,1024]{2,1,0:T(8,128)(2,1)}, bf16[1,1024,1024]{2,1,0:T(8,128)(2,1)S(1)}, u32[]{:S(2)}) copy-start(bf16[1,1024,1024]{2,1,0:T(8,128)(2,1)S(1)} %get-tuple-element.6) | copy-start | bytes 6291460
  201.8 272.7 %all-gather.19.cloned.1.call-start = ((), (), s32[]{:S(2)}) async-start(), calls=%async_computation.6 | async-start | bytes 2228224 | tf_op jit(solution)/shard_map/all_gather | solution.py:16
  295.4 225.9 %all-gather.23.cloned.1.call-start = ((), (), s32[]{:S(2)}) async-start(), calls=%async_computation.8 | async-start | bytes 2228224 | tf_op jit(solution)/shard_map/all_gather | solution.py:16
  389.2 7.8 %copy-start.1 = (bf16[1024,1,1024]{2,0,1:T(8,128)(2,1)S(1)}, bf16[1024,1,1024]{2,0,1:T(8,128)(2,1)}, u32[]{:S(2)}) copy-start(bf16[1024,1,1024]{2,0,1:T(8,128)(2,1)} %all-gather.29.cloned.1.call-done) | copy-start | bytes 6291460
  389.2 7.8 %copy-start.5 = (f32[3,64,1024]{2,1,0:T(8,128)S(1)}, f32[3,64,1024]{2,1,0:T(8,128)}, u32[]{:S(2)}) copy-start(f32[3,64,1024]{2,1,0:T(8,128)} %param.11) | copy-start | bytes 2359300
  394.7 3.8 copy-start.2
  397.0 2.7 copy-start
  399.7 2.4 copy-start.6
  524.2 14.0 %all-to-all-start.1 = ((bf16[3,8,8,1024]{3,2,0,1:T(8,128)(2,1)}), bf16[3,8,8,1024]{3,2,0,1:T(8,128)(2,1)S(1)}, u32[]{:S(2)}, u32[]{:S(2)}) async-start(bf16[3,8,8,1024]{3,2,0,1:T(8,128)(2,1)} %pad_maximum_fusion.4), calls=%async_computation.1 | async-start | bytes 786432 | tf_op jit(solution)/shard_map/all_to_all | solution.py:127
Sparse Core Ops, SparseCore 0:
  11.3 77.2 reduce-scatter.3
  105.9 41.4 all-gather.12
  150.2 44.1 all-gather.24
  197.0 44.1 all-gather.16
  243.8 44.1 all-gather.26
  290.0 44.1 all-gather.20
  336.9 44.1 all-gather.28
  383.3 44.1 all-gather.14
  430.2 44.1 all-gather.18
  477.0 44.1 all-gather.22
where the time goes:
time: 547 us; the launch traced here: 546 us
  waiting for transfers between devices  444 us (81%)
  matrix products  45.4 us (8%)
  blocking collectives  14.6 us (3%)
  between operations  14.4 us (3%)
  other arithmetic  11.6 us (2%)
  local copies, waits for them, and re-layouts  9.65 us (2%)
  starting transfers between devices  6.32 us (1%)
    all_gather x3, waiting for transfers between devices, on_device(): lax.all_gather(grad_slabs[position], 'dp', axis=0, tiled=True)  134 us
    all_gather x3, waiting for transfers between devices, rotate_back(): whole_half = lax.all_gather(back_half, 'dp', axis=0, tiled=True)  112 us
    all_gather x3, waiting for transfers between devices, on_device(): lax.all_gather(moment_slabs[position], 'dp', axis=0, tiled=True)  111 us
    unnamed x11, waiting for transfers between devices  83.3 us
    all_to_all x1, blocking collectives, on_device(): lax.all_to_all(outgoing, 'owner', split_axis=1, concat_axis=0, tiled=True)  14.6 us
    dot_general x3, matrix products, rotate_back(): lax.dot_general(direction, basis_right, (((1,), (1,)), ((), ())), preferr...  12.1 us
  transfers between devices with their start and end apart: 11, of which 11 were waited for; matrix products, arithmetic and copies ran while one was open for 11% of the time, Pallas kernels for 0%

commit v1 on v0

v1 whole, which is shorter than its diff:
```python
import jax
import jax.numpy as jnp
from jax import lax
from jax.experimental import pallas as pl
from jax.experimental.pallas import tpu as pltpu
from jax.sharding import PartitionSpec as P

BETA_FIRST = 0.9
BETA_SECOND = 0.95
BETA_FACTOR = 0.95
EPSILON = 1e-08
F32 = jnp.float32
BF16 = jnp.bfloat16
HALF = 64
LANES = 128
VMEM_BYTES = 40 * 1024 * 1024

NN = (((1,), (0,)), ((), ()))
NT = (((1,), (1,)), ((), ()))
TN = (((0,), (0,)), ((), ()))


def dot(a, b, dims):
    return lax.dot_general(a, b, dims, preferred_element_type=F32)


def swap_halves(x):
    return pltpu.roll(x, HALF, 1)


def rotate_right_kernel(used_ref, grad_ref, moment_ref, second_ref, basis_ref, first_ref, packed_ref):
    slot = pl.program_id(0)
    used = used_ref[slot] > 0
    low = lax.broadcasted_iota(jnp.int32, (HALF, LANES), 1) < HALF
    grad = grad_ref[0]
    moment = (
        BETA_FIRST * moment_ref[0].astype(F32) + (1.0 - BETA_FIRST) * grad.astype(F32)
    ).astype(BF16)
    first_ref[0] = jnp.where(used, moment.astype(F32), 0.0).astype(BF16)
    both = jnp.concatenate([grad, moment], axis=0)
    turned = dot(both, basis_ref[0], NN)
    second = second_ref[0].astype(F32)
    for pair in range(packed_ref.shape[0] // 2):
        lanes = slice(pair * LANES, (pair + 1) * LANES)
        a = turned[:HALF, lanes]
        b = turned[HALF:, lanes]
        v = second[:, lanes]
        packed_ref[2 * pair, 0, :, :LANES] = jnp.where(low, a, swap_halves(b)).astype(BF16)
        packed_ref[2 * pair + 1, 0, :, :LANES] = jnp.where(low, swap_halves(a), b).astype(BF16)
        packed_ref[2 * pair, 0, :, LANES:] = v.astype(BF16)
        packed_ref[2 * pair + 1, 0, :, LANES:] = swap_halves(v).astype(BF16)


def rotate_left_kernel(packed_ref, basis_ref, out_ref):
    parts = packed_ref.shape[0]
    packed = packed_ref[...].reshape(parts * HALF, 2 * LANES)
    basis = basis_ref[0]
    turned = dot(packed[:, :LANES], basis, TN)
    second = packed[:, LANES:].astype(F32).T[:HALF]
    rot_grad = turned[:HALF]
    rot_mom = turned[HALF:]
    variance = BETA_SECOND * second + (1.0 - BETA_SECOND) * rot_grad * rot_grad
    direction = (rot_mom / (jnp.sqrt(variance) + EPSILON)).astype(BF16)
    step = dot(direction, basis, NT)
    out = jnp.concatenate([step, variance], axis=0).T.astype(BF16)
    out_ref[...] = out.reshape(out_ref.shape)


def step_kernel(used_ref, packed_ref, basis_ref, second_ref, step_ref):
    used = used_ref[pl.program_id(0)] > 0
    low = lax.broadcasted_iota(jnp.int32, (HALF, LANES), 1) < HALF
    lefts = []
    seconds = []
    for pair in range(packed_ref.shape[0] // 2):
        a = packed_ref[2 * pair, 0].astype(F32)
        b = packed_ref[2 * pair + 1, 0].astype(F32)
        lefts.append(jnp.where(low, a, swap_halves(b)).astype(BF16))
        seconds.append(jnp.where(low, swap_halves(a), b))
    second_ref[0] = jnp.where(used, jnp.concatenate(seconds, axis=1), 0.0).astype(BF16)
    left = jnp.concatenate(lefts, axis=1)
    step_ref[0] = dot(left, basis_ref[0], NT).astype(BF16)


def gram_kernel(used_ref, place_ref, whole_ref, rows_ref, left_ref, right_ref, new_left_ref, new_right_ref):
    used = used_ref[pl.program_id(0)] > 0
    place = place_ref[0]
    whole = whole_ref[...].reshape(left_ref.shape[2], left_ref.shape[2])
    gram_left = dot(rows_ref[0], whole, NT)
    start = pl.multiple_of((place // 2) * LANES, LANES)
    columns = whole_ref[:, 0, :, pl.ds(start, LANES)].reshape(left_ref.shape[2], LANES)
    gram_pair = dot(columns, whole, TN)
    gram_right = jnp.where(place % 2 == 0, gram_pair[:HALF], gram_pair[HALF:])
    new_left_ref[0] = jnp.where(
        used, BETA_FACTOR * left_ref[0] + (1.0 - BETA_FACTOR) * gram_left, 0.0
    )
    new_right_ref[0] = jnp.where(
        used, BETA_FACTOR * right_ref[0] + (1.0 - BETA_FACTOR) * gram_right, 0.0
    )


def on_device(
    grad_part,
    block_slot,
    left_factor,
    right_factor,
    first_moment,
    second_moment,
    left_basis,
    right_basis,
):
    owners = lax.axis_size("owner")
    replicas = lax.axis_size("dp")
    mine_dp = lax.axis_index("dp")
    mine_owner = lax.axis_index("owner")
    slots, slab, order = left_factor.shape
    part_rows = grad_part.shape[2]
    width = grad_part.shape[3]
    blocks = width // order

    slot_ids = jnp.arange(owners * slots, dtype=jnp.int32)
    matches = block_slot[None, :] == slot_ids[:, None]
    filled = jnp.any(matches, axis=1).astype(jnp.int32)
    holder = jnp.sum(jnp.where(matches, jnp.arange(blocks, dtype=jnp.int32)[None, :], 0), axis=1)
    used = lax.dynamic_slice_in_dim(filled, mine_owner * slots, slots)
    place = mine_dp.astype(jnp.int32).reshape(1)

    partials = lax.all_to_all(grad_part[0], "dp", split_axis=0, concat_axis=0, tiled=True)
    flat = jnp.sum(partials.astype(F32), axis=0).astype(BF16)
    by_block = flat.reshape(part_rows, blocks, order).transpose(1, 0, 2)
    outgoing = jnp.take(by_block, holder, axis=0).reshape(owners, slots, part_rows, order)
    incoming = lax.all_to_all(outgoing, "owner", split_axis=0, concat_axis=0, tiled=True)
    rows = incoming.transpose(1, 0, 2, 3).reshape(slots, slab, order)

    whole = lax.all_gather(rows, "dp", axis=0)

    smem = pl.BlockSpec(memory_space=pltpu.SMEM)
    slab_spec = pl.BlockSpec((1, slab, order), lambda q: (q, 0, 0))
    basis_spec = pl.BlockSpec((1, order, order), lambda q: (q, 0, 0))

    def chunk_spec(lanes):
        return pl.BlockSpec((replicas, 1, slab, lanes), lambda q: (0, q, 0, 0))

    def params():
        return pltpu.CompilerParams(vmem_limit_bytes=VMEM_BYTES)

    def cost(products, moved):
        return pl.CostEstimate(
            flops=2 * slots * products * slab * order * order, bytes_accessed=moved, transcendentals=0
        )

    slab_bf16 = jax.ShapeDtypeStruct((slots, slab, order), BF16)
    slab_f32 = jax.ShapeDtypeStruct((slots, slab, order), F32)
    new_first, packed = pl.pallas_call(
        rotate_right_kernel,
        grid=(slots,),
        in_specs=[smem, slab_spec, slab_spec, slab_spec, basis_spec],
        out_specs=[slab_spec, chunk_spec(2 * LANES)],
        out_shape=[slab_bf16, jax.ShapeDtypeStruct((replicas, slots, slab, 2 * LANES), BF16)],
        compiler_params=params(),
        cost_estimate=cost(2, 10 * 2**20),
        name="rotate_right",
    )(used, rows, first_moment, second_moment, right_basis)

    packed = lax.all_to_all(packed, "dp", split_axis=0, concat_axis=0, tiled=True)

    turned = pl.pallas_call(
        rotate_left_kernel,
        grid=(slots,),
        in_specs=[chunk_spec(2 * LANES), basis_spec],
        out_specs=chunk_spec(LANES),
        out_shape=jax.ShapeDtypeStruct((replicas, slots, slab, LANES), BF16),
        compiler_params=params(),
        cost_estimate=cost(3, 10 * 2**20),
        name="rotate_left",
    )(packed, left_basis)

    turned = lax.all_to_all(turned, "dp", split_axis=0, concat_axis=0, tiled=True)

    new_second, step = pl.pallas_call(
        step_kernel,
        grid=(slots,),
        in_specs=[smem, chunk_spec(LANES), basis_spec],
        out_specs=[slab_spec, slab_spec],
        out_shape=[slab_bf16, slab_bf16],
        compiler_params=params(),
        cost_estimate=cost(1, 8 * 2**20),
        name="step_rows",
    )(used, turned, right_basis)

    step = step.reshape(slots, owners, part_rows, order).transpose(1, 0, 2, 3)
    returned = lax.all_to_all(step, "owner", split_axis=0, concat_axis=0, tiled=True)
    picked = jnp.take(returned.reshape(owners * slots, part_rows, order), block_slot, axis=0)
    update = picked.transpose(1, 0, 2).reshape(part_rows, width)

    new_left, new_right = pl.pallas_call(
        gram_kernel,
        grid=(slots,),
        in_specs=[smem, smem, chunk_spec(order), slab_spec, slab_spec, slab_spec],
        out_specs=[slab_spec, slab_spec],
        out_shape=[slab_f32, slab_f32],
        compiler_params=params(),
        cost_estimate=cost(3, 10 * 2**20),
        name="factor_rows",
    )(used, place, whole, rows, left_factor, right_factor)

    return new_left, new_right, new_first, new_second, update


def solution(mesh):
    slabs = P("owner", "dp", None)
    whole_slots = P("owner", None, None)
    return jax.shard_map(
        on_device,
        mesh=mesh,
        in_specs=(
            P("dp", None, "owner", None),
            P(),
            slabs,
            slabs,
            slabs,
            slabs,
            whole_slots,
            whole_slots,
        ),
        out_specs=(slabs, slabs, slabs, slabs, P(("dp", "owner"), None)),
        check_vma=False,
    )
```

time: 547 us -> 183 us (0.33)
  waiting for transfers between devices: 444 us -> 54.5 us
  blocking collectives: 14.6 us -> 70.8 us
  matrix products: 45.4 us -> 0 us
  Pallas kernels: 0 us -> 14.8 us
  starting transfers between devices: 6.32 us -> 14.5 us
  other arithmetic: 11.6 us -> 4.45 us
    all_gather x9 -> x1, waiting for transfers between devices: 356 us -> 0.01 us  [on_device(): whole = lax.all_gather(rows, 'dp', axis=0)]
    unnamed x11 -> x1, waiting for transfers between devices: 83.3 us -> 0.02 us
    all_to_all x1 -> x3, blocking collectives: 14.6 us -> 70.8 us  [the longest x1 30.5 us: on_device(): lax.all_to_all(packed, 'dp', split_axis=0, concat_axis=0, tiled=True)]
    all_to_all x1 -> x2, waiting for transfers between devices: 4.74 us -> 54.4 us  [the longest x1 46.4 us: on_device(): lax.all_to_all(grad_part[0], 'dp', split_axis=0, concat_axis=0, tiled=True)]
    dot_general x18 -> x0, matrix products: 45.4 us -> none  [the longest x3 12.1 us: rotate_back(): lax.dot_general(direction, basis_right, (((1,), (1,)), ((), ())), preferr...]
    pallas_call x0 -> x4, Pallas kernels: none -> 14.8 us  [the longest x1 4.87 us: on_device(): pl.pallas_call(gram_kernel, grid=(slots,), in_specs=[smem, smem, chunk_sp...]
    all_to_all x1 -> x2, starting transfers between devices: 5.92 us -> 14.4 us  [the longest x1 7.64 us: on_device(): lax.all_to_all(grad_part[0], 'dp', split_axis=0, concat_axis=0, tiled=True)]
    another operation x8 -> x0, other arithmetic: 7.41 us -> none  [the longest x4 3.93 us: on_device(): jnp.stack(seconds)]
  transfers between devices with their start and end apart: 11 -> 3, of which waited for: 11 -> 2; matrix products, arithmetic and copies ran while one was open for 11% -> 1% of each run, Pallas kernels for 0% -> 5%
where the time goes in v1:
time: 183 us; the launch traced here: 182 us
  blocking collectives  70.8 us (39%)
  waiting for transfers between devices  54.5 us (30%)
  Pallas kernels  14.8 us (8%)
  starting transfers between devices  14.5 us (8%)
  between operations  14.2 us (8%)
  local copies, waits for them, and re-layouts  9.27 us (5%)
  other arithmetic  4.45 us (2%)
    all_to_all x1, waiting for transfers between devices, on_device(): lax.all_to_all(grad_part[0], 'dp', split_axis=0, concat_axis=0, tiled=True)  46.4 us
    all_to_all x1, blocking collectives, on_device(): lax.all_to_all(packed, 'dp', split_axis=0, concat_axis=0, tiled=True)  30.5 us
    all_to_all x1, blocking collectives, on_device(): lax.all_to_all(turned, 'dp', split_axis=0, concat_axis=0, tiled=True)  25.3 us
    all_to_all x1, blocking collectives, on_device(): lax.all_to_all(outgoing, 'owner', split_axis=0, concat_axis=0, tiled=True)  15 us
    all_to_all x1, waiting for transfers between devices, on_device(): lax.all_to_all(step, 'owner', split_axis=0, concat_axis=0, tiled=True)  8.05 us
    all_to_all x1, starting transfers between devices, on_device(): lax.all_to_all(grad_part[0], 'dp', split_axis=0, concat_axis=0, tiled=True)  7.64 us
    all_to_all x1, starting transfers between devices, on_device(): lax.all_to_all(step, 'owner', split_axis=0, concat_axis=0, tiled=True)  6.8 us
    unnamed x22, local copies, waits for them, and re-layouts  5.61 us
  transfers between devices with their start and end apart: 3, of which 2 were waited for; matrix products, arithmetic and copies ran while one was open for 1% of the time, Pallas kernels for 5%

profile of v1, /device:TPU:1, one launch (start us, length us, event | category | flops | bytes accessed | tf_op | source)
XLA Modules:
  0.0 182.4 jit_solution(18329461265196595770)
XLA Ops:
  7.2 0.0 copy-start.6
  7.2 7.6 %all-to-all-start = ((bf16[16,8,12288]{2,1,0:T(8,128)(2,1)}), bf16[16,8,12288]{2,1,0:T(8,128)(2,1)}, u32[]{:S(2)}, u32[]{:S(2)}) async-start(bf16[16,8,12288]{2,1,0:T(8,128)(2,1)} %bitcast.30), calls=%async_computation | async-start | bytes 6291456 | tf_op jit(solution)/shard_map/all_to_all | solution.py:127
  14.8 0.0 all-gather.2.cloned.1.call-start
  14.9 0.0 copy-done.6
  14.9 0.1 select_reduce_fusion
  15.0 0.1 reduce_sum.26
  15.1 0.0 copy-start.4
  15.1 0.0 copy-start.5
  15.1 46.4 %all-to-all-done = bf16[16,8,12288]{2,1,0:T(8,128)(2,1)} async-done(((bf16[16,8,12288]{2,1,0:T(8,128)(2,1)}), bf16[16,8,12288]{2,1,0:T(8,128)(2,1)}, u32[]{:S(2)}, u32[]{:S(2)}) %all-to-all-start) | async-done | bytes 3145760 | tf_op jit(solution)/shard_map/all_to_all | solution.py:127
  61.5 2.4 %reduce_sum.27 = bf16[8,12288]{1,0:T(8,128)(2,1)S(1)} reduce(bf16[16,8,12288]{2,1,0:T(8,128)(2,1)} %all-to-all-done, bf16[]{:T(256)} %constant.45.clone.1), dimensions={0}, to_apply=%region_2.3 | reduce | flops 1474560 | bytes 3342338 | tf_op jit(solution)/shard_map/reduce_sum | solution.py:128
  63.9 0.0 slice-start.2
  63.9 1.3 gather_fusion
  65.2 1.1 broadcast_select_fusion
  66.3 15.0 %all_to_all.25 = bf16[8,3,8,1024]{3,2,1,0:T(8,128)(2,1)S(1)} all-to-all(bf16[8,3,8,1024]{3,2,1,0:T(8,128)(2,1)S(1)} %broadcast_select_fusion), channel_id=1, replica_groups=mesh['dp'=16,'owner'=8] {'owner'}, dimensions={0} | all-to-all | bytes 786432 | tf_op jit(solution)/shard_map/all_to_all | solution.py:131
  81.3 0.8 copy_bitcast_fusion.1
  82.2 0.0 all-gather.2.cloned.1.call-update
  82.2 0.1 fusion
  82.3 0.1 dynamic_slice.3.used_ref
  82.4 0.0 copy-done.4
  82.4 0.0 copy-done.5
  82.4 0.0 copy-start
  82.4 2.8 %copy-done = bf16[3,1024,1024]{2,1,0:T(8,128)(2,1)S(1)} copy-done((bf16[3,1024,1024]{2,1,0:T(8,128)(2,1)S(1)}, bf16[3,1024,1024]{2,1,0:T(8,128)(2,1)}, u32[]{:S(2)}) %copy-start) | copy-done | bytes 6291480
  85.2 0.0 slice-start.3
  85.2 2.7 %rotate_right.1 = (bf16[3,64,1024]{2,1,0:T(8,128)(2,1)}, bf16[16,3,64,256]{3,2,1,0:T(8,128)(2,1)S(1)}) custom-call(s32[3]{0:T(128)S(1)} %dynamic_slice.3.used_ref, bf16[3,64,1024]{2,1,0:T(8,128)(2,1)S(1)} %get-tuple-element.17.rows_ref.grad_ref, bf16[3,64,1024]{2,1,0:T(8,128)(2,1)S(1)} %copy-done.4, bf16[3,64,1024]{2,1,0:T(8,128)(2,1)S(1)} %copy-done.5, ...), custom_call_target="tpu_custom_call" | custom-call | flops 805306368 | bytes 10485760 | tf_op jit(solution)/shard_map/rotate_right/pallas_call | solution.py:153
  87.8 0.0 slice-start
  87.8 30.5 %all_to_all.26.packed_ref = bf16[16,3,64,256]{3,2,1,0:T(8,128)(2,1)S(1)} all-to-all(bf16[16,3,64,256]{3,2,1,0:T(8,128)(2,1)S(1)} %get-tuple-element.14), channel_id=1, replica_groups=mesh['dp'=16,'owner'=8] {'dp'}, dimensions={0} | all-to-all | bytes 3145728 | tf_op jit(solution)/shard_map/all_to_all | solution.py:164
  118.3 0.0 slice-done.2
  118.3 0.0 slice-done.3
  118.3 0.0 slice-start.1
  118.3 3.8 %rotate_left.1 = bf16[16,3,64,128]{3,2,1,0:T(8,128)(2,1)S(1)} custom-call(bf16[16,3,64,256]{3,2,1,0:T(8,128)(2,1)S(1)} %all_to_all.26.packed_ref, bf16[3,1024,1024]{2,1,0:T(8,128)(2,1)S(1)} %bitcast.29), custom_call_target="tpu_custom_call" | custom-call | flops 1207959552 | bytes 10485760 | tf_op jit(solution)/shard_map/rotate_left/pallas_call | solution.py:166
  122.1 25.3 %all_to_all.27.packed_ref = bf16[16,3,64,128]{3,2,1,0:T(8,128)(2,1)S(1)} all-to-all(bf16[16,3,64,128]{3,2,1,0:T(8,128)(2,1)S(1)} %rotate_left.1), channel_id=1, replica_groups=mesh['dp'=16,'owner'=8] {'dp'}, dimensions={0} | all-to-all | bytes 1572864 | tf_op jit(solution)/shard_map/all_to_all | solution.py:177
  147.4 0.0 slice-done
  147.4 0.0 slice-done.1
  147.4 0.0 copy-start.2
  147.4 0.0 copy-start.3
  147.4 3.5 %step_rows.1 = (bf16[3,64,1024]{2,1,0:T(8,128)(2,1)}, bf16[3,64,1024]{2,1,0:T(8,128)(2,1)S(1)}) custom-call(s32[3]{0:T(128)S(1)} %dynamic_slice.3.used_ref, bf16[16,3,64,128]{3,2,1,0:T(8,128)(2,1)S(1)} %all_to_all.27.packed_ref, bf16[3,1024,1024]{2,1,0:T(8,128)(2,1)S(1)} %bitcast.27), custom_call_target="tpu_custom_call" | custom-call | flops 402653184 | bytes 8388608 | tf_op jit(solution)/shard_map/step_rows/pallas_call | solution.py:179
  150.9 0.8 copy_bitcast_fusion
  151.7 6.8 %all-to-all-start.4 = ((bf16[8,3,8,1024]{3,2,1,0:T(8,128)(2,1)}), bf16[8,3,8,1024]{3,2,1,0:T(8,128)(2,1)S(1)}, u32[]{:S(2)}, u32[]{:S(2)}) async-start(bf16[8,3,8,1024]{3,2,1,0:T(8,128)(2,1)} %copy_bitcast_fusion), calls=%async_computation.4 | async-start | bytes 786432 | tf_op jit(solution)/shard_map/all_to_all | solution.py:191
  158.5 8.1 %all-to-all-done.4 = bf16[8,3,8,1024]{3,2,1,0:T(8,128)(2,1)S(1)} async-done(((bf16[8,3,8,1024]{3,2,1,0:T(8,128)(2,1)}), bf16[8,3,8,1024]{3,2,1,0:T(8,128)(2,1)S(1)}, u32[]{:S(2)}, u32[]{:S(2)}) %all-to-all-start.4) | async-done | bytes 393248 | tf_op jit(solution)/shard_map/all_to_all | solution.py:191
  166.6 0.6 gather_fusion.1
  167.1 0.8 broadcast_select_fusion.1
  167.9 0.0 all-gather.2.cloned.1.call-done.whole_ref
  167.9 0.0 copy-done.2
  167.9 0.0 copy-done.3
  167.9 0.0 copy-start.1
  167.9 2.8 %copy-done.1 = bf16[16,3,64,1024]{3,2,1,0:T(8,128)(2,1)S(1)} copy-done((bf16[16,3,64,1024]{3,2,1,0:T(8,128)(2,1)S(1)}, bf16[16,3,64,1024]{3,2,1,0:T(8,128)(2,1)}, u32[]{:S(2)}) %copy-start.1) | copy-done | bytes 6291480
  170.7 4.9 %factor_rows.1 = (f32[3,64,1024]{2,1,0:T(8,128)}, f32[3,64,1024]{2,1,0:T(8,128)}) custom-call(s32[3]{0:T(128)S(1)} %dynamic_slice.3.used_ref, s32[1]{0:T(128)} %bitcast.place_ref, bf16[16,3,64,1024]{3,2,1,0:T(8,128)(2,1)S(1)} %copy-done.1, bf16[3,64,1024]{2,1,0:T(8,128)(2,1)S(1)} %get-tuple-element.17.rows_ref.grad_ref, f32[3,64,1024]{2,1,0:T(8,128)S(1)} %copy-done.2, ...), custom_call_target="tpu_custom_call" | custom-call | flops 1207959552 | bytes 10485760 | tf_op jit(solution)/shard_map/factor_rows/pallas_call | solution.py:195
  (9 shorter events, 0.0 us)
Async XLA Ops:
  7.2 7.7 %copy-start.6 = (s32[12]{0:T(128)S(1)}, s32[12]{0:T(128)}, u32[]{:S(2)}) copy-start(s32[12]{0:T(128)} %param.9) | copy-start | bytes 148
  7.2 54.3 %all-to-all-start = ((bf16[16,8,12288]{2,1,0:T(8,128)(2,1)}), bf16[16,8,12288]{2,1,0:T(8,128)(2,1)}, u32[]{:S(2)}, u32[]{:S(2)}) async-start(bf16[16,8,12288]{2,1,0:T(8,128)(2,1)} %bitcast.30), calls=%async_computation | async-start | bytes 6291456 | tf_op jit(solution)/shard_map/all_to_all | solution.py:127
  14.8 153.1 %all-gather.2.cloned.1.call-start = ((), (), s32[]{:S(2)}) async-start(), calls=%async_computation.5 | async-start | bytes 6684672 | tf_op jit(solution)/shard_map/all_gather | solution.py:134
  15.1 67.3 %copy-start.4 = (bf16[3,64,1024]{2,1,0:T(8,128)(2,1)S(1)}, bf16[3,64,1024]{2,1,0:T(8,128)(2,1)}, u32[]{:S(2)}) copy-start(bf16[3,64,1024]{2,1,0:T(8,128)(2,1)} %moment_ref.1) | copy-start | bytes 1179652
  15.1 67.3 %copy-start.5 = (bf16[3,64,1024]{2,1,0:T(8,128)(2,1)S(1)}, bf16[3,64,1024]{2,1,0:T(8,128)(2,1)}, u32[]{:S(2)}) copy-start(bf16[3,64,1024]{2,1,0:T(8,128)(2,1)} %second_ref.1) | copy-start | bytes 1179652
  63.9 54.4 %slice-start.2 = ((s8[6291456]{0:T(1024)(128)(4,1)}), s8[2097152]{0:T(1024)(128)(4,1)S(1)}, s32[]{:S(2)}) async-start(s8[6291456]{0:T(1024)(128)(4,1)} %bitcast.28), calls=%async_computation.8 | async-start | bytes 4194304
  82.4 2.8 %copy-start = (bf16[3,1024,1024]{2,1,0:T(8,128)(2,1)S(1)}, bf16[3,1024,1024]{2,1,0:T(8,128)(2,1)}, u32[]{:S(2)}) copy-start(bf16[3,1024,1024]{2,1,0:T(8,128)(2,1)} %basis_ref.5) | copy-start | bytes 18874372
  85.2 33.1 %slice-start.3 = ((s8[6291456]{0:T(1024)(128)(4,1)}), s8[4194304]{0:T(1024)(128)(4,1)S(1)}, s32[]{:S(2)}) async-start(s8[6291456]{0:T(1024)(128)(4,1)} %bitcast.28), calls=%async_computation.9 | async-start | bytes 8388608
  87.8 59.5 %slice-start = ((s8[6291456]{0:T(1024)(128)(4,1)}), s8[4194304]{0:T(1024)(128)(4,1)S(1)}, s32[]{:S(2)}) async-start(s8[6291456]{0:T(1024)(128)(4,1)} %bitcast.26), calls=%async_computation.6 | async-start | bytes 8388608
  118.3 29.1 %slice-start.1 = ((s8[6291456]{0:T(1024)(128)(4,1)}), s8[2097152]{0:T(1024)(128)(4,1)S(1)}, s32[]{:S(2)}) async-start(s8[6291456]{0:T(1024)(128)(4,1)} %bitcast.26), calls=%async_computation.7 | async-start | bytes 4194304
  147.4 20.5 %copy-start.2 = (f32[3,64,1024]{2,1,0:T(8,128)S(1)}, f32[3,64,1024]{2,1,0:T(8,128)}, u32[]{:S(2)}) copy-start(f32[3,64,1024]{2,1,0:T(8,128)} %left_ref.1) | copy-start | bytes 2359300
  147.4 20.5 %copy-start.3 = (f32[3,64,1024]{2,1,0:T(8,128)S(1)}, f32[3,64,1024]{2,1,0:T(8,128)}, u32[]{:S(2)}) copy-start(f32[3,64,1024]{2,1,0:T(8,128)} %right_ref.1) | copy-start | bytes 2359300
  151.7 14.9 %all-to-all-start.4 = ((bf16[8,3,8,1024]{3,2,1,0:T(8,128)(2,1)}), bf16[8,3,8,1024]{3,2,1,0:T(8,128)(2,1)S(1)}, u32[]{:S(2)}, u32[]{:S(2)}) async-start(bf16[8,3,8,1024]{3,2,1,0:T(8,128)(2,1)} %copy_bitcast_fusion), calls=%async_computation.4 | async-start | bytes 786432 | tf_op jit(solution)/shard_map/all_to_all | solution.py:191
  167.9 2.8 %copy-start.1 = (bf16[16,3,64,1024]{3,2,1,0:T(8,128)(2,1)S(1)}, bf16[16,3,64,1024]{3,2,1,0:T(8,128)(2,1)}, u32[]{:S(2)}) copy-start(bf16[16,3,64,1024]{3,2,1,0:T(8,128)(2,1)} %all-gather.2.cloned.1.call-done.whole_ref) | copy-start | bytes 18874372
Sparse Core Ops, SparseCore 0:
  82.3 79.9 all-gather.1

commit v2 on v1

v2 whole, which is shorter than its diff:
```python
import jax
import jax.numpy as jnp
from jax import lax
from jax.experimental import pallas as pl
from jax.experimental.pallas import tpu as pltpu
from jax.sharding import PartitionSpec as P

BETA_FIRST = 0.9
BETA_SECOND = 0.95
BETA_FACTOR = 0.95
EPSILON = 1e-08
F32 = jnp.float32
BF16 = jnp.bfloat16
HALF = 64
LANES = 128
VMEM_BYTES = 32 * 1024 * 1024
SMEM, VMEM, HBM, ANY = pltpu.SMEM, pltpu.VMEM, pltpu.HBM, pl.ANY
SIDE = 4

NN = (((1,), (0,)), ((), ()))
NT = (((1,), (1,)), ((), ()))
TN = (((0,), (0,)), ((), ()))


def dot(a, b, dims):
    return lax.dot_general(a, b, dims, preferred_element_type=F32)


def swap_halves(x):
    return pltpu.roll(x, HALF, 1)


def low_lanes(rows):
    return lax.broadcasted_iota(jnp.int32, (rows, LANES), 1) < HALF


def turn(index, by):
    return lax.rem(index + by, SIDE)


def start_all(copies):
    for copy in copies:
        copy.start()
    return copies


def wait_all(copies):
    for copy in copies:
        copy.wait()


def add(*terms):
    total = terms[0].astype(F32)
    for term in terms[1:]:
        total = total + term.astype(F32)
    return total.astype(BF16)


def first_send_kernel(here, grad, a1, b1, a3, b3, a2, b2, sems):
    y, x = here[0], here[1]
    half = grad.shape[3] // 2
    copies = []
    for by, a_out, b_out in ((1, a1, b1), (3, a3, b3), (2, a2, b2)):
        for source, target in (
            (grad.at[:, turn(x, by), :, pl.ds(0, half)], a_out),
            (grad.at[turn(y, by), :, :, pl.ds(half, half)], b_out),
        ):
            copies.append(pltpu.make_async_copy(source, target, sems.at[len(copies)]))
    wait_all(start_all(copies))


def fetch(source, target, sems):
    return start_all(
        [
            pltpu.make_async_copy(source.at[slot], target.at[slot], sems.at[slot])
            for slot in range(source.shape[0])
        ]
    )


def second_send_kernel(here, grad, a1, b1, a3, b3, a2, b2, p0, p1, p2, p3, q0, q1, q2, q3, a0, b0, sems):
    y, x = here[0], here[1]
    half = grad.shape[3] // 2
    own = [
        pltpu.make_async_copy(grad.at[:, x, :, pl.ds(0, half)], a0, sems.at[0]),
        pltpu.make_async_copy(grad.at[y, :, :, pl.ds(half, half)], b0, sems.at[1]),
    ]
    wait_all(start_all(own))
    for by, (p_out, q_out) in enumerate(((p0, q0), (p1, q1), (p2, q2), (p3, q3))):
        to_y = turn(y, by)
        to_x = turn(x, by)
        p_out[...] = add(a0[to_y], a1[to_y], a3[to_y], a2[to_y])
        q_out[...] = add(b0[to_x], b1[to_x], b3[to_x], b2[to_x])


def outgoing_kernel(holder, p0, p1, p2, p3, q0, q1, q2, q3, out, flat):
    order = out.shape[2]
    half_blocks = p0.shape[1] // order
    for block in range(half_blocks):
        lanes = slice(block * order, (block + 1) * order)
        flat[block] = add(p0[:, lanes], p1[:, lanes], p2[:, lanes], p3[:, lanes])
        flat[block + half_blocks] = add(q0[:, lanes], q1[:, lanes], q2[:, lanes], q3[:, lanes])
    for slot in range(out.shape[0]):
        out[slot] = flat[holder[slot]]


def moment_right_kernel(moment_hbm, second_hbm, basis_hbm, packed, moment, second, basis, small_sems, sems):
    small = start_all(
        [
            pltpu.make_async_copy(moment_hbm, moment, small_sems.at[0]),
            pltpu.make_async_copy(second_hbm, second, small_sems.at[1]),
        ]
    )
    arrivals = fetch(basis_hbm, basis, sems)
    wait_all(small)
    low = low_lanes(HALF)
    for slot in range(moment.shape[0]):
        arrivals[slot].wait()
        turned = dot(moment[slot], basis[slot], NN)
        for pair in range(packed.shape[0] // 2):
            lanes = slice(pair * LANES, (pair + 1) * LANES)
            a = turned[:, lanes]
            b = second[slot, :, lanes].astype(F32)
            packed[2 * pair, slot] = jnp.where(low, a, swap_halves(b)).astype(BF16)
            packed[2 * pair + 1, slot] = jnp.where(low, swap_halves(a), b).astype(BF16)


def moment_left_kernel(packed, basis_hbm, out, basis, sems):
    arrivals = fetch(basis_hbm, basis, sems)
    order = basis.shape[1]
    for slot in range(out.shape[0]):
        both = packed[:, slot].reshape(order, LANES)
        out[slot, HALF:] = both.astype(F32).T[HALF:]
        arrivals[slot].wait()
        out[slot, :HALF] = dot(both[:, :HALF], basis[slot], TN)


def rotate_right_kernel(used, rows, moment_hbm, basis_hbm, first, packed, moment, basis, small_sems, sems):
    small = pltpu.make_async_copy(moment_hbm, moment, small_sems.at[0])
    arrivals = fetch(basis_hbm, basis, sems)
    small.start()
    small.wait()
    half = HALF // 2
    low = low_lanes(half)
    for slot in range(rows.shape[0]):
        grad = rows[slot]
        mixed = BETA_FIRST * moment[slot].astype(F32) + (1.0 - BETA_FIRST) * grad.astype(F32)
        first[slot] = jnp.where(used[slot] > 0, mixed, 0.0).astype(BF16)
    for slot in range(rows.shape[0]):
        arrivals[slot].wait()
        turned = dot(rows[slot], basis[slot], NN)
        for pair in range(packed.shape[0] // 2):
            lanes = slice(pair * LANES, (pair + 1) * LANES)
            a = turned[:half, lanes]
            b = turned[half:, lanes]
            packed[2 * pair, slot] = jnp.where(low, a, swap_halves(b)).astype(BF16)
            packed[2 * pair + 1, slot] = jnp.where(low, swap_halves(a), b).astype(BF16)


def rotate_left_kernel(packed, basis_hbm, ready, out, basis, sems):
    arrivals = fetch(basis_hbm, basis, sems)
    order = basis.shape[1]
    parts, half = packed.shape[0], packed.shape[2]
    for slot in range(out.shape[1]):
        both = packed[:, slot].reshape(parts * half, LANES)
        arrivals[slot].wait()
        cut = basis[slot].reshape(parts, 2, half, order)
        rot_grad = dot(both[:, :HALF], cut[:, 0].reshape(parts * half, order), TN) + dot(
            both[:, HALF:], cut[:, 1].reshape(parts * half, order), TN
        )
        rot_mom = BETA_FIRST * ready[slot, :HALF] + (1.0 - BETA_FIRST) * rot_grad
        variance = BETA_SECOND * ready[slot, HALF:] + (1.0 - BETA_SECOND) * rot_grad * rot_grad
        direction = (rot_mom / (jnp.sqrt(variance) + EPSILON)).astype(BF16)
        step = dot(direction, basis[slot], NT)
        joined = jnp.concatenate([step, variance], axis=0).T.astype(BF16)
        out[:, slot] = joined.reshape(parts, HALF, LANES)


def step_kernel(used, packed, basis_hbm, second, step, basis, sems):
    arrivals = fetch(basis_hbm, basis, sems)
    low = low_lanes(HALF)
    for slot in range(second.shape[0]):
        lefts = []
        for pair in range(packed.shape[0] // 2):
            lanes = slice(pair * LANES, (pair + 1) * LANES)
            a = packed[2 * pair, slot].astype(F32)
            b = packed[2 * pair + 1, slot].astype(F32)
            lefts.append(jnp.where(low, a, swap_halves(b)).astype(BF16))
            v = jnp.where(low, swap_halves(a), b)
            second[slot, :, lanes] = jnp.where(used[slot] > 0, v, 0.0).astype(BF16)
        arrivals[slot].wait()
        moved = dot(jnp.concatenate(lefts, axis=1), basis[slot], NT)
        step[:, slot] = moved.reshape(step.shape[0], step.shape[2], step.shape[3]).astype(BF16)


def gram_tiles_kernel(
    here, rows, x1, y1, x3, y3, x2, y2,
    left0, left1, left2, left3, right0, right1, right2, right3,
    across, down, grams, sems,
):
    y, x = here[0], here[1]
    slots, slab, order = rows.shape
    lines = SIDE * slab
    start = pl.multiple_of(y * lines, lines)
    copies = []
    for back, (ref_x, ref_y) in enumerate(((rows, rows), (x1, y1), (x2, y2), (x3, y3))):
        copies.append(pltpu.make_async_copy(ref_x, across.at[turn(x, SIDE - back)], sems.at[0, back]))
        copies.append(pltpu.make_async_copy(ref_y, down.at[back], sems.at[1, back]))
    wait_all(start_all(copies))
    for slot in range(slots):
        panel = down[:, slot].reshape(lines, order)
        tile = dot(panel, across[:, slot].reshape(lines, order), NT)
        for back, out in enumerate((left0, left1, left2, left3)):
            out[slot] = tile[back * slab : (back + 1) * slab].astype(out.dtype)
        columns = down[:, slot, :, pl.ds(start, lines)].reshape(lines, lines)
        grams[...] = dot(columns, panel, TN).reshape(grams.shape)
        for by, out in enumerate((right0, right1, right2, right3)):
            out[slot] = grams[turn(x, by)].astype(out.dtype)


def gram_sum_kernel(
    here, used, left0, left1, left2, left3, right0, right1, right2, right3, left_hbm, right_hbm,
    new_left, new_right, left, right, sems,
):
    y = here[0]
    old = start_all(
        [pltpu.make_async_copy(left_hbm, left, sems.at[0]), pltpu.make_async_copy(right_hbm, right, sems.at[1])]
    )
    wait_all(old)
    lines = left0.shape[2]
    for slot in range(left.shape[0]):
        is_used = used[slot] > 0
        for ahead, tile in enumerate((left0, left1, left2, left3)):
            lanes = pl.ds(pl.multiple_of(turn(y, ahead) * lines, lines), lines)
            new_left[slot, :, lanes] = jnp.where(
                is_used, BETA_FACTOR * left[slot, :, lanes] + (1.0 - BETA_FACTOR) * tile[slot].astype(F32), 0.0
            )
        gram = right0[slot] + right1[slot].astype(F32) + right2[slot].astype(F32) + right3[slot].astype(F32)
        new_right[slot] = jnp.where(is_used, BETA_FACTOR * right[slot] + (1.0 - BETA_FACTOR) * gram, 0.0)


def along_x(value, by):
    pairs = [
        (y * SIDE + x, y * SIDE + (x + by) % SIDE) for y in range(SIDE) for x in range(SIDE)
    ]
    return lax.ppermute(value, "dp", pairs)


def along_y(value, by):
    pairs = [
        (y * SIDE + x, ((y + by) % SIDE) * SIDE + x) for y in range(SIDE) for x in range(SIDE)
    ]
    return lax.ppermute(value, "dp", pairs)


def call(kernel, name, ins, outs, scratch, products, moved):
    arrays = [pltpu.with_memory_space_constraint(array, space) if space == HBM else array for array, space in ins]
    return pl.pallas_call(
        kernel,
        in_specs=[pl.BlockSpec(memory_space=space) for _, space in ins],
        out_specs=[pl.BlockSpec(memory_space=space or VMEM) for _, _, space in outs],
        out_shape=[
            space(shape, dtype) if space == VMEM else jax.ShapeDtypeStruct(shape, dtype) for shape, dtype, space in outs
        ],
        scratch_shapes=scratch,
        compiler_params=pltpu.CompilerParams(vmem_limit_bytes=VMEM_BYTES),
        cost_estimate=pl.CostEstimate(flops=products * 2**27, bytes_accessed=moved * 2**20, transcendentals=0),
        name=name,
    )(*arrays)


def sum_replicas(grad, here, holder, slot_total, order, beside, between):
    rows, width = grad.shape[1], grad.shape[2]
    half = width // 2
    grad = grad.reshape(SIDE, SIDE, rows, width)
    line = (SIDE, rows, half)
    sent = call(
        first_send_kernel, "first_send", [(here, SMEM), (grad, HBM)], [(line, BF16, VMEM)] * 6,
        [pltpu.SemaphoreType.DMA((6,))], 0, 5,
    )
    got = []
    for k, by in enumerate((1, 3, 2)):
        got += [along_x(sent[2 * k], by), along_y(sent[2 * k + 1], by)]
    got, early = lax.optimization_barrier((got, beside()))
    pieces = call(
        second_send_kernel, "second_send", [(here, SMEM), (grad, HBM)] + [(value, VMEM) for value in got],
        [((rows, half), BF16, None if by % SIDE == 0 else VMEM) for by in range(2 * SIDE)],
        [pltpu.VMEM(line, BF16), pltpu.VMEM(line, BF16), pltpu.SemaphoreType.DMA((2,))], 0, 4,
    )
    early = between(early)
    p, q = [pieces[0]], [pieces[4]]
    for by in (1, 3, 2):
        p.append(along_y(pieces[by], by))
        q.append(along_x(pieces[4 + by], by))
    p, q, early = lax.optimization_barrier((p, q, early))
    outgoing = call(
        outgoing_kernel, "outgoing", [(holder, SMEM)] + [(value, VMEM) for value in p + q],
        [((slot_total, rows, order), BF16, VMEM)], [pltpu.VMEM((width // order, rows, order), BF16)], 0, 1,
    )[0]
    return outgoing, early


def on_device(
    grad_part,
    block_slot,
    left_factor,
    right_factor,
    first_moment,
    second_moment,
    left_basis,
    right_basis,
):
    owners = lax.axis_size("owner")
    replicas = lax.axis_size("dp")
    mine_dp = lax.axis_index("dp").astype(jnp.int32)
    mine_owner = lax.axis_index("owner")
    slots, slab, order = left_factor.shape
    part_rows = grad_part.shape[2]
    width = grad_part.shape[3]
    blocks = width // order

    slot_ids = jnp.arange(owners * slots, dtype=jnp.int32)
    matches = block_slot[None, :] == slot_ids[:, None]
    filled = jnp.any(matches, axis=1).astype(jnp.int32)
    holder = jnp.sum(jnp.where(matches, jnp.arange(blocks, dtype=jnp.int32)[None, :], 0), axis=1)
    used = lax.dynamic_slice_in_dim(filled, mine_owner * slots, slots)
    here = jnp.stack([mine_dp // SIDE, mine_dp % SIDE])

    slabs = (slots, slab, order)

    def exchange(value, axis):
        return lax.all_to_all(value, axis, split_axis=0, concat_axis=0, tiled=True)

    basis_scratch = [pltpu.VMEM((slots, order, order), BF16), pltpu.SemaphoreType.DMA((slots,))]
    chunks = (replicas, slots, slab, LANES)

    def moment_right():
        return call(
            moment_right_kernel, "moment_right",
            [(first_moment, HBM), (second_moment, HBM), (right_basis, HBM)], [(chunks, BF16, VMEM)],
            [pltpu.VMEM(slabs, BF16), pltpu.VMEM(slabs, BF16), basis_scratch[0], pltpu.SemaphoreType.DMA((2,)), basis_scratch[1]],
            3, 8,
        )[0]

    outgoing, early = sum_replicas(
        grad_part[0], here, holder, owners * slots, order, moment_right, lambda value: exchange(value, "dp")
    )
    incoming = exchange(outgoing.reshape(owners, slots, part_rows, order), "owner")
    rows = incoming.transpose(1, 0, 2, 3).reshape(slabs)

    new_first, packed = call(
        rotate_right_kernel, "rotate_right",
        [(used, SMEM), (rows, VMEM), (first_moment, HBM), (right_basis, HBM)],
        [(slabs, BF16, None), ((replicas, slots, slab // 2, LANES), BF16, VMEM)],
        [pltpu.VMEM(slabs, BF16), basis_scratch[0], pltpu.SemaphoreType.DMA((1,)), basis_scratch[1]], 3, 8,
    )
    rows, packed, early = lax.optimization_barrier((rows, packed, early))
    packed = exchange(packed, "dp")
    near = []
    for by in (1, 3):
        near += [along_x(rows, by), along_y(rows, by)]
    near.append(along_x(rows, 2))
    ready = call(
        moment_left_kernel, "moment_left", [(early, VMEM), (left_basis, HBM)],
        [((slots, 2 * slab, order), F32, VMEM)], basis_scratch, 3, 8,
    )[0]
    rows, ready = lax.optimization_barrier((rows, ready))
    near.append(along_y(rows, 2))
    turned = call(
        rotate_left_kernel, "rotate_left", [(packed, VMEM), (left_basis, HBM), (ready, VMEM)],
        [(chunks, BF16, VMEM)], basis_scratch, 9, 8,
    )[0]
    near, turned = lax.optimization_barrier((near, turned))
    turned = exchange(turned, "dp")
    tiles = call(
        gram_tiles_kernel, "gram_tiles", [(here, SMEM)] + [(value, ANY) for value in [rows] + near],
        [((slots, slab, SIDE * slab), F32 if k == 0 else BF16, VMEM) for k in range(SIDE)]
        + [(slabs, F32 if k == 0 else BF16, VMEM) for k in range(SIDE)],
        [
            pltpu.VMEM((SIDE, slots, slab, order), BF16), pltpu.VMEM((SIDE, slots, slab, order), BF16),
            pltpu.VMEM((SIDE, slab, order), F32), pltpu.SemaphoreType.DMA((2, SIDE)),
        ],
        9, 6,
    )
    lefts = [tiles[0]] + [along_y(tiles[back], SIDE - back) for back in (1, 2, 3)]
    rights = [tiles[SIDE]] + [along_x(tiles[SIDE + by], by) for by in (1, 2, 3)]
    lefts, turned = lax.optimization_barrier((lefts, turned))
    new_second, step = call(
        step_kernel, "step_rows", [(used, SMEM), (turned, VMEM), (right_basis, HBM)],
        [(slabs, BF16, None), ((owners, slots, part_rows, order), BF16, VMEM)], basis_scratch, 3, 8,
    )
    returned = exchange(step, "owner")
    rights, step = lax.optimization_barrier((rights, step))
    new_left, new_right = call(
        gram_sum_kernel, "gram_sum",
        [(here, SMEM), (used, SMEM)] + [(value, VMEM) for value in lefts + rights]
        + [(left_factor, HBM), (right_factor, HBM)],
        [(slabs, F32, None)] * 2,
        [pltpu.VMEM(slabs, F32), pltpu.VMEM(slabs, F32), pltpu.SemaphoreType.DMA((2,))], 0, 8,
    )

    picked = returned.reshape(owners * slots, part_rows, order).at[block_slot].get(mode="promise_in_bounds")
    update = picked.transpose(1, 0, 2).reshape(part_rows, width)
    return new_left, new_right, new_first, new_second, update


def solution(mesh):
    slabs = P("owner", "dp", None)
    whole_slots = P("owner", None, None)
    return jax.shard_map(
        on_device,
        mesh=mesh,
        in_specs=(
            P("dp", None, "owner", None),
            P(),
            slabs,
            slabs,
            slabs,
            slabs,
            whole_slots,
            whole_slots,
        ),
        out_specs=(slabs, slabs, slabs, slabs, P(("dp", "owner"), None)),
        check_vma=False,
    )
```

time: 183 us -> 148 us (0.81)
  blocking collectives: 70.8 us -> 0 us
  starting transfers between devices: 14.5 us -> 67.4 us
  Pallas kernels: 14.8 us -> 40.3 us
  waiting for transfers between devices: 54.5 us -> 35.9 us
  between operations: 14.2 us -> 0.83 us
  local copies, waits for them, and re-layouts: 9.27 us -> 2.34 us
  other arithmetic: 4.45 us -> 0.27 us
    all_to_all x3 -> x0, blocking collectives: 70.8 us -> none  [the longest x1 30.5 us: on_device(): lax.all_to_all(packed, 'dp', split_axis=0, concat_axis=0, tiled=True)]
    all_to_all x2 -> x5, waiting for transfers between devices: 54.4 us -> 12.8 us  [exchange(): return lax.all_to_all(value, axis, split_axis=0, concat_axis=0, tiled=True)]
    ppermute x0 -> x24, starting transfers between devices: none -> 37.9 us  [the longest x12 19.4 us: along_y(): return lax.ppermute(value, 'dp', pairs)]
    pallas_call x4 -> x10, Pallas kernels: 14.8 us -> 40.3 us  [call(): pl.pallas_call(kernel, in_specs=[pl.BlockSpec(memory_space=space) for _,...]
    ppermute x0 -> x24, waiting for transfers between devices: none -> 23.1 us  [the longest x12 13.3 us: along_x(): return lax.ppermute(value, 'dp', pairs)]
    all_to_all x2 -> x5, starting transfers between devices: 14.4 us -> 29.5 us  [exchange(): return lax.all_to_all(value, axis, split_axis=0, concat_axis=0, tiled=True)]
    unnamed x22 -> x6, local copies, waits for them, and re-layouts: 5.61 us -> 1 us
    reduce_sum x1 -> x0, other arithmetic: 2.36 us -> none  [on_device(): flat = jnp.sum(partials.astype(F32), axis=0).astype(BF16)]
  transfers between devices with their start and end apart: 3 -> 29, of which waited for: 2 -> 17; matrix products, arithmetic and copies ran while one was open for 1% -> 0% of each run, Pallas kernels for 5% -> 19%
where the time goes in v2:
time: 148 us; the launch traced here: 147 us
  starting transfers between devices  67.4 us (46%)
  Pallas kernels  40.3 us (27%)
  waiting for transfers between devices  35.9 us (24%)
  local copies, waits for them, and re-layouts  2.34 us (2%)
    pallas_call x10, Pallas kernels, call(): pl.pallas_call(kernel, in_specs=[pl.BlockSpec(memory_space=space) for _,...  40.3 us
    all_to_all x5, starting transfers between devices, exchange(): return lax.all_to_all(value, axis, split_axis=0, concat_axis=0, tiled=True)  29.5 us
    ppermute x12, starting transfers between devices, along_y(): return lax.ppermute(value, 'dp', pairs)  19.4 us
    ppermute x12, starting transfers between devices, along_x(): return lax.ppermute(value, 'dp', pairs)  18.5 us
    ppermute x12, waiting for transfers between devices, along_x(): return lax.ppermute(value, 'dp', pairs)  13.3 us
    all_to_all x5, waiting for transfers between devices, exchange(): return lax.all_to_all(value, axis, split_axis=0, concat_axis=0, tiled=True)  12.8 us
    ppermute x12, waiting for transfers between devices, along_y(): return lax.ppermute(value, 'dp', pairs)  9.86 us
  transfers between devices with their start and end apart: 29, of which 17 were waited for; matrix products, arithmetic and copies ran while one was open for 0% of the time, Pallas kernels for 19%

profile of v2, /device:TPU:1, one launch (start us, length us, event | category | flops | bytes accessed | tf_op | source)
XLA Modules:
  0.0 147.0 jit_solution(10046968859527793862)
XLA Ops:
  0.7 0.1 pad_add_fusion.here
  0.7 2.2 %first_send.1 = (bf16[4,8,6144]{2,1,0:T(8,128)(2,1)S(1)}, bf16[4,8,6144]{2,1,0:T(8,128)(2,1)S(1)}, bf16[4,8,6144]{2,1,0:T(8,128)(2,1)S(1)}, bf16[4,8,6144]{2,1,0...) custom-call(s32[2]{0:T(128)S(1)} %pad_add_fusion.here, bf16[4,4,8,12288]{3,2,1,0:T(8,128)(2,1)} %bitcast.13), custom_call_target="tpu_custom_call" | custom-call | bytes 5242880 | tf_op jit(solution)/shard_map/first_send/pallas_call | solution.py:258
  2.9 2.1 %collective-permute-start = (bf16[4,8,6144]{2,1,0:T(8,128)(2,1)S(1)}, bf16[4,8,6144]{2,1,0:T(8,128)(2,1)S(1)}, u32[]{:S(2)}, u32[]{:S(2)}) collective-permute-start(bf16[4,8,6144]{2,1,0:T(8,128)(2,1)S(1)} %get-tuple-element.70), channel_id=1, source_target_pairs={{0,8},{8,16},{16,24},{24,0},{32,40},{40,48},{48,56},{56,32},{64,72... | collective-permute-start | bytes 1179656 | tf_op jit(solution)/shard_map/ppermute | solution.py:246
  5.0 1.3 collective-permute-start.1
  6.3 1.5 collective-permute-start.2
  7.8 1.4 collective-permute-start.3
  9.2 1.5 %collective-permute-start.4 = (bf16[4,8,6144]{2,1,0:T(8,128)(2,1)S(1)}, bf16[4,8,6144]{2,1,0:T(8,128)(2,1)S(1)}, u32[]{:S(2)}, u32[]{:S(2)}) collective-permute-start(bf16[4,8,6144]{2,1,0:T(8,128)(2,1)S(1)} %get-tuple-element.74), channel_id=1, source_target_pairs={{0,16},{8,24},{16,0},{24,8},{32,48},{40,56},{48,32},{56,40},{64,80... | collective-permute-start | bytes 1179656 | tf_op jit(solution)/shard_map/ppermute | solution.py:246
  10.8 3.9 %collective-permute-done.a1 = bf16[4,8,6144]{2,1,0:T(8,128)(2,1)S(1)} collective-permute-done((bf16[4,8,6144]{2,1,0:T(8,128)(2,1)S(1)}, bf16[4,8,6144]{2,1,0:T(8,128)(2,1)S(1)}, u32[]{:S(2)}, u32[]{:S(2)}) %collective-permute-start) | collective-permute-done | bytes 393248 | tf_op jit(solution)/shard_map/ppermute | solution.py:246
  14.7 3.2 %collective-permute-start.5 = (bf16[4,8,6144]{2,1,0:T(8,128)(2,1)S(1)}, bf16[4,8,6144]{2,1,0:T(8,128)(2,1)S(1)}, u32[]{:S(2)}, u32[]{:S(2)}) collective-permute-start(bf16[4,8,6144]{2,1,0:T(8,128)(2,1)S(1)} %get-tuple-element.75), channel_id=1, source_target_pairs={{0,64},{8,72},{16,80},{24,88},{32,96},{40,104},{48,112},{56,120},{... | collective-permute-start | bytes 1179656 | tf_op jit(solution)/shard_map/ppermute | solution.py:253
  17.9 5.0 %moment_right.1 = bf16[16,3,64,128]{3,2,1,0:T(8,128)(2,1)} custom-call(bf16[3,64,1024]{2,1,0:T(8,128)(2,1)} %moment_hbm.3, bf16[3,64,1024]{2,1,0:T(8,128)(2,1)} %second_hbm.1, bf16[3,1024,1024]{2,1,0:T(8,128)(2,1)} %basis_hbm.9), custom_call_target="tpu_custom_call" | custom-call | flops 402653184 | bytes 8388608 | tf_op jit(solution)/shard_map/moment_right/pallas_call | solution.py:258
  22.9 0.0 collective-permute-done.2.a3
  23.0 1.5 %collective-permute-done.4.a2 = bf16[4,8,6144]{2,1,0:T(8,128)(2,1)S(1)} collective-permute-done((bf16[4,8,6144]{2,1,0:T(8,128)(2,1)S(1)}, bf16[4,8,6144]{2,1,0:T(8,128)(2,1)S(1)}, u32[]{:S(2)}, u32[]{:S(2)}) %collective-permute-start.4) | collective-permute-done | bytes 393248 | tf_op jit(solution)/shard_map/ppermute | solution.py:246
  24.4 1.2 collective-permute-done.5.b2
  25.7 4.6 %all-to-all-start = ((bf16[16,3,64,128]{3,2,1,0:T(8,128)(2,1)}), bf16[16,3,64,128]{3,2,1,0:T(8,128)(2,1)S(1)}, u32[]{:S(2)}, u32[]{:S(2)}) async-start(bf16[16,3,64,128]{3,2,1,0:T(8,128)(2,1)} %moment_right.1), calls=%async_computation | async-start | bytes 1572864 | tf_op jit(solution)/shard_map/all_to_all | solution.py:332
  30.3 2.1 %second_send.1 = (bf16[8,6144]{1,0:T(8,128)(2,1)S(1)}, bf16[8,6144]{1,0:T(8,128)(2,1)S(1)}, bf16[8,6144]{1,0:T(8,128)(2,1)S(1)}, bf16[8,6144]{1,0:T(8,128)(2,1)S...) custom-call(s32[2]{0:T(128)S(1)} %pad_add_fusion.here, ...), custom_call_target="tpu_custom_call" | custom-call | bytes 4194304 | tf_op jit(solution)/shard_map/second_send/pallas_call | solution.py:258
  32.4 2.6 %collective-permute-start.10 = (bf16[8,6144]{1,0:T(8,128)(2,1)S(1)}, bf16[8,6144]{1,0:T(8,128)(2,1)S(1)}, u32[]{:S(2)}, u32[]{:S(2)}) collective-permute-start(bf16[8,6144]{1,0:T(8,128)(2,1)S(1)} %get-tuple-element.88), channel_id=1, source_target_pairs={{0,24},{8,0},{16,8},{24,16},{32,56},{40,32},{48,40},{56,48},{64,88... | collective-permute-start | bytes 294920 | tf_op jit(solution)/shard_map/ppermute | solution.py:246
  35.0 0.6 collective-permute-start.11
  35.6 1.2 collective-permute-start.6
  36.8 1.5 %collective-permute-start.7 = (bf16[8,6144]{1,0:T(8,128)(2,1)S(1)}, bf16[8,6144]{1,0:T(8,128)(2,1)S(1)}, u32[]{:S(2)}, u32[]{:S(2)}) collective-permute-start(bf16[8,6144]{1,0:T(8,128)(2,1)S(1)} %get-tuple-element.84), channel_id=1, source_target_pairs={{0,96},{8,104},{16,112},{24,120},{32,0},{40,8},{48,16},{56,24},{64... | collective-permute-start | bytes 294920 | tf_op jit(solution)/shard_map/ppermute | solution.py:253
  38.3 1.5 %collective-permute-start.8 = (bf16[8,6144]{1,0:T(8,128)(2,1)S(1)}, bf16[8,6144]{1,0:T(8,128)(2,1)S(1)}, u32[]{:S(2)}, u32[]{:S(2)}) collective-permute-start(bf16[8,6144]{1,0:T(8,128)(2,1)S(1)} %get-tuple-element.85), channel_id=1, source_target_pairs={{0,64},{8,72},{16,80},{24,88},{32,96},{40,104},{48,112},{56,120},{... | collective-permute-start | bytes 294920 | tf_op jit(solution)/shard_map/ppermute | solution.py:253
  39.7 0.4 collective-permute-done.10.q2
  40.1 1.1 collective-permute-start.9
  41.3 0.1 select_reduce_fusion.holder
  41.4 3.5 %collective-permute-done.6.p1 = bf16[8,6144]{1,0:T(8,128)(2,1)S(1)} collective-permute-done((bf16[8,6144]{1,0:T(8,128)(2,1)S(1)}, bf16[8,6144]{1,0:T(8,128)(2,1)S(1)}, u32[]{:S(2)}, u32[]{:S(2)}) %collective-permute-start.6) | collective-permute-done | bytes 98336 | tf_op jit(solution)/shard_map/ppermute | solution.py:253
  44.8 1.0 collective-permute-done.8.p3
  45.8 0.5 collective-permute-done.9.q1
  46.3 1.4 outgoing.1
  47.7 10.0 %all-to-all-start.1 = ((bf16[8,3,8,1024]{3,2,1,0:T(8,128)(2,1)}), bf16[8,3,8,1024]{3,2,1,0:T(8,128)(2,1)S(1)}, u32[]{:S(2)}, u32[]{:S(2)}) async-start(bf16[8,3,8,1024]{3,2,1,0:T(8,128)(2,1)} %bitcast.3), calls=%async_computation.1 | async-start | bytes 786432 | tf_op jit(solution)/shard_map/all_to_all | solution.py:332
  57.8 0.1 fusion
  57.9 0.1 dynamic_slice.3.used
  58.0 7.9 %all-to-all-done.1 = bf16[8,3,8,1024]{3,2,1,0:T(8,128)(2,1)S(1)} async-done(((bf16[8,3,8,1024]{3,2,1,0:T(8,128)(2,1)}), bf16[8,3,8,1024]{3,2,1,0:T(8,128)(2,1)S(1)}, u32[]{:S(2)}, u32[]{:S(2)}) %all-to-all-start.1) | async-done | bytes 393248 | tf_op jit(solution)/shard_map/all_to_all | solution.py:332
  65.9 6.0 %rotate_right.1 = (bf16[3,64,1024]{2,1,0:T(8,128)(2,1)}, bf16[16,3,32,128]{3,2,1,0:T(8,128)(2,1)}) custom-call(s32[3]{0:T(128)S(1)} %dynamic_slice.3.used, bf16[3,64,1024]{2,1,0:T(8,128)(2,1)S(1)} %copy_bitcast_fusion.rows, bf16[3,64,1024]{2,1,0:T(8,128)(2,1)} %moment_hbm.3, bf16[3,1024,1024]{2,1,0:T(8,128)(2,1)} %basis_hbm.9), custom_call_target="tpu_custom_call" | custom-call | flops 402653184 | bytes 8388608 | tf_op jit(solution)/shard_map/rotate_right/pallas_call | solution.py:258
  71.9 3.4 %moment_left.1.ready = f32[3,128,1024]{2,1,0:T(8,128)S(1)} custom-call(bf16[16,3,64,128]{3,2,1,0:T(8,128)(2,1)S(1)} %all-to-all-done.packed, bf16[3,1024,1024]{2,1,0:T(8,128)(2,1)} %basis_hbm.8), custom_call_target="tpu_custom_call" | custom-call | flops 402653184 | bytes 8388608 | tf_op jit(solution)/shard_map/moment_left/pallas_call | solution.py:258
  75.3 2.8 %collective-permute-start.17 = (bf16[3,64,1024]{2,1,0:T(8,128)(2,1)S(1)}, bf16[3,64,1024]{2,1,0:T(8,128)(2,1)S(1)}, u32[]{:S(2)}, u32[]{:S(2)}) collective-permute-start(bf16[3,64,1024]{2,1,0:T(8,128)(2,1)S(1)} %copy_bitcast_fusion.rows), channel_id=1, source_target_pairs={{0,64},{8,72},{16,80},{24,88},{32,96},{40,104},{48,112},{56,120},{... | collective-permute-start | bytes 1179656 | tf_op jit(solution)/shard_map/ppermute | solution.py:253
  78.1 3.6 %all-to-all-start.2 = ((bf16[16,3,32,128]{3,2,1,0:T(8,128)(2,1)}), bf16[16,3,32,128]{3,2,1,0:T(8,128)(2,1)S(1)}, u32[]{:S(2)}, u32[]{:S(2)}) async-start(bf16[16,3,32,128]{3,2,1,0:T(8,128)(2,1)} %get-tuple-element.104), calls=%async_computation.2 | async-start | bytes 786432 | tf_op jit(solution)/shard_map/all_to_all | solution.py:332
  81.7 1.2 collective-permute-start.12
  82.9 1.2 collective-permute-start.13
  84.1 1.5 %collective-permute-start.14 = (bf16[3,64,1024]{2,1,0:T(8,128)(2,1)S(1)}, bf16[3,64,1024]{2,1,0:T(8,128)(2,1)}, u32[]{:S(2)}, u32[]{:S(2)}) collective-permute-start(bf16[3,64,1024]{2,1,0:T(8,128)(2,1)S(1)} %copy_bitcast_fusion.rows), channel_id=1, source_target_pairs={{0,24},{8,0},{16,8},{24,16},{32,56},{40,32},{48,40},{56,48},{64,88... | collective-permute-start | bytes 1179656 | tf_op jit(solution)/shard_map/ppermute | solution.py:246
  85.6 1.5 %collective-permute-start.15 = (bf16[3,64,1024]{2,1,0:T(8,128)(2,1)S(1)}, bf16[3,64,1024]{2,1,0:T(8,128)(2,1)}, u32[]{:S(2)}, u32[]{:S(2)}) collective-permute-start(bf16[3,64,1024]{2,1,0:T(8,128)(2,1)S(1)} %copy_bitcast_fusion.rows), channel_id=1, source_target_pairs={{0,96},{8,104},{16,112},{24,120},{32,0},{40,8},{48,16},{56,24},{64... | collective-permute-start | bytes 1179656 | tf_op jit(solution)/shard_map/ppermute | solution.py:253
  87.1 1.3 collective-permute-done.17.y2
  88.4 0.8 collective-permute-start.16
  89.1 2.0 %all-to-all-done.2.packed = bf16[16,3,32,128]{3,2,1,0:T(8,128)(2,1)S(1)} async-done(((bf16[16,3,32,128]{3,2,1,0:T(8,128)(2,1)}), bf16[16,3,32,128]{3,2,1,0:T(8,128)(2,1)S(1)}, u32[]{:S(2)}, u32[]{:S(2)}) %all-to-all-start.2) | async-done | bytes 393248 | tf_op jit(solution)/shard_map/all_to_all | solution.py:332
  91.1 6.5 %rotate_left.1 = bf16[16,3,64,128]{3,2,1,0:T(8,128)(2,1)} custom-call(bf16[16,3,32,128]{3,2,1,0:T(8,128)(2,1)S(1)} %all-to-all-done.2.packed, bf16[3,1024,1024]{2,1,0:T(8,128)(2,1)} %basis_hbm.8, f32[3,128,1024]{2,1,0:T(8,128)S(1)} %moment_left.1.ready), custom_call_target="tpu_custom_call" | custom-call | flops 1207959552 | bytes 8388608 | tf_op jit(solution)/shard_map/rotate_left/pallas_call | solution.py:258
  97.7 0.3 collective-permute-done.12.x1
  97.9 2.6 %collective-permute-done.13.y1 = bf16[3,64,1024]{2,1,0:T(8,128)(2,1)} collective-permute-done((bf16[3,64,1024]{2,1,0:T(8,128)(2,1)S(1)}, bf16[3,64,1024]{2,1,0:T(8,128)(2,1)}, u32[]{:S(2)}, u32[]{:S(2)}) %collective-permute-start.13) | collective-permute-done | bytes 393248 | tf_op jit(solution)/shard_map/ppermute | solution.py:253
  100.5 4.8 %collective-permute-done.16.x2 = bf16[3,64,1024]{2,1,0:T(8,128)(2,1)} collective-permute-done((bf16[3,64,1024]{2,1,0:T(8,128)(2,1)S(1)}, bf16[3,64,1024]{2,1,0:T(8,128)(2,1)}, u32[]{:S(2)}, u32[]{:S(2)}) %collective-permute-start.16) | collective-permute-done | bytes 393248 | tf_op jit(solution)/shard_map/ppermute | solution.py:246
  105.4 4.7 %all-to-all-start.3 = ((bf16[16,3,64,128]{3,2,1,0:T(8,128)(2,1)}), bf16[16,3,64,128]{3,2,1,0:T(8,128)(2,1)S(1)}, u32[]{:S(2)}, u32[]{:S(2)}) async-start(bf16[16,3,64,128]{3,2,1,0:T(8,128)(2,1)} %rotate_left.1), calls=%async_computation.3 | async-start | bytes 1572864 | tf_op jit(solution)/shard_map/all_to_all | solution.py:332
  110.1 0.0 copy-start.1
  110.1 1.0 copy-done.1
  111.1 5.1 %gram_tiles.1 = (f32[3,64,256]{2,1,0:T(8,128)S(1)}, bf16[3,64,256]{2,1,0:T(8,128)(2,1)S(1)}, bf16[3,64,256]{2,1,0:T(8,128)(2,1)S(1)}, bf16[3,64,256]{2,1,0:T(8,1...) custom-call(s32[2]{0:T(128)S(1)} %pad_add_fusion.here, ...), custom_call_target="tpu_custom_call" | custom-call | flops 1207959552 | bytes 6291456 | tf_op jit(solution)/shard_map/gram_tiles/pallas_call | solution.py:258
  116.2 2.7 %collective-permute-start.18 = (bf16[3,64,256]{2,1,0:T(8,128)(2,1)S(1)}, bf16[3,64,256]{2,1,0:T(8,128)(2,1)S(1)}, u32[]{:S(2)}, u32[]{:S(2)}) collective-permute-start(bf16[3,64,256]{2,1,0:T(8,128)(2,1)S(1)} %get-tuple-element.113), channel_id=1, source_target_pairs={{0,96},{8,104},{16,112},{24,120},{32,0},{40,8},{48,16},{56,24},{64... | collective-permute-start | bytes 294920 | tf_op jit(solution)/shard_map/ppermute | solution.py:253
  118.8 0.6 collective-permute-start.19
  119.4 0.6 collective-permute-start.20
  120.0 1.2 collective-permute-start.21
  121.2 2.4 %collective-permute-start.22 = (bf16[3,64,1024]{2,1,0:T(8,128)(2,1)}, bf16[3,64,1024]{2,1,0:T(8,128)(2,1)S(1)}, u32[]{:S(2)}, u32[]{:S(2)}) collective-permute-start(bf16[3,64,1024]{2,1,0:T(8,128)(2,1)} %get-tuple-element.123), channel_id=1, source_target_pairs={{0,16},{8,24},{16,0},{24,8},{32,48},{40,56},{48,32},{56,40},{64,80... | collective-permute-start | bytes 1179656 | tf_op jit(solution)/shard_map/ppermute | solution.py:246
  123.6 0.4 collective-permute-done.18.left1
  123.9 2.0 %collective-permute-start.23 = (bf16[3,64,1024]{2,1,0:T(8,128)(2,1)}, bf16[3,64,1024]{2,1,0:T(8,128)(2,1)S(1)}, u32[]{:S(2)}, u32[]{:S(2)}) collective-permute-start(bf16[3,64,1024]{2,1,0:T(8,128)(2,1)} %get-tuple-element.124), channel_id=1, source_target_pairs={{0,24},{8,0},{16,8},{24,16},{32,56},{40,32},{48,40},{56,48},{64,88... | collective-permute-start | bytes 1179656 | tf_op jit(solution)/shard_map/ppermute | solution.py:246
  125.9 5.2 %step_rows.1 = (bf16[3,64,1024]{2,1,0:T(8,128)(2,1)}, bf16[8,3,8,1024]{3,2,1,0:T(8,128)(2,1)}) custom-call(s32[3]{0:T(128)S(1)} %dynamic_slice.3.used, bf16[16,3,64,128]{3,2,1,0:T(8,128)(2,1)S(1)} %all-to-all-done.3.packed, bf16[3,1024,1024]{2,1,0:T(8,128)(2,1)} %basis_hbm.9), custom_call_target="tpu_custom_call" | custom-call | flops 402653184 | bytes 8388608 | tf_op jit(solution)/shard_map/step_rows/pallas_call | solution.py:258
  131.2 6.5 %all-to-all-start.4 = ((bf16[8,3,8,1024]{3,2,1,0:T(8,128)(2,1)}), bf16[8,3,8,1024]{3,2,1,0:T(8,128)(2,1)S(1)}, u32[]{:S(2)}, u32[]{:S(2)}) async-start(bf16[8,3,8,1024]{3,2,1,0:T(8,128)(2,1)} %get-tuple-element.126), calls=%async_computation.4 | async-start | bytes 786432 | tf_op jit(solution)/shard_map/all_to_all | solution.py:332
  137.7 0.2 collective-permute-done.22.right2
  137.9 1.6 %collective-permute-done.23.right3 = bf16[3,64,1024]{2,1,0:T(8,128)(2,1)S(1)} collective-permute-done((bf16[3,64,1024]{2,1,0:T(8,128)(2,1)}, bf16[3,64,1024]{2,1,0:T(8,128)(2,1)S(1)}, u32[]{:S(2)}, u32[]{:S(2)}) %collective-permute-start.23) | collective-permute-done | bytes 393248 | tf_op jit(solution)/shard_map/ppermute | solution.py:246
  139.5 3.4 %gram_sum.1 = (f32[3,64,1024]{2,1,0:T(8,128)}, f32[3,64,1024]{2,1,0:T(8,128)}) custom-call(s32[2]{0:T(128)S(1)} %pad_add_fusion.here, s32[3]{0:T(128)S(1)} %dynamic_slice.3.used, f32[3,64,256]{2,1,0:T(8,128)S(1)} %get-tuple-element.117.left0, bf16[3,64,256]{2,1,0:T(8,128)(2,1)S(1)} %collective-permute-done.18.left1, ...), custom_call_target="tpu_custom_call" | custom-call | bytes 8388608 | tf_op jit(solution)/shard_map/gram_sum/pallas_call | solution.py:258
  142.9 2.9 %all-to-all-done.4 = bf16[8,3,8,1024]{3,2,1,0:T(8,128)(2,1)S(1)} async-done(((bf16[8,3,8,1024]{3,2,1,0:T(8,128)(2,1)}), bf16[8,3,8,1024]{3,2,1,0:T(8,128)(2,1)S(1)}, u32[]{:S(2)}, u32[]{:S(2)}) %all-to-all-start.4) | async-done | bytes 393248 | tf_op jit(solution)/shard_map/all_to_all | solution.py:332
  145.8 1.2 gather_fusion
  (19 shorter events, 0.1 us)
Async XLA Ops:
  2.9 11.8 %collective-permute-start = (bf16[4,8,6144]{2,1,0:T(8,128)(2,1)S(1)}, bf16[4,8,6144]{2,1,0:T(8,128)(2,1)S(1)}, u32[]{:S(2)}, u32[]{:S(2)}) collective-permute-start(bf16[4,8,6144]{2,1,0:T(8,128)(2,1)S(1)} %get-tuple-element.70), channel_id=1, source_target_pairs={{0,8},{8,16},{16,24},{24,0},{32,40},{40,48},{48,56},{56,32},{64,72... | collective-permute-start | bytes 1179656 | tf_op jit(solution)/shard_map/ppermute | solution.py:246
  5.0 17.9 %collective-permute-start.1 = (bf16[4,8,6144]{2,1,0:T(8,128)(2,1)S(1)}, bf16[4,8,6144]{2,1,0:T(8,128)(2,1)S(1)}, u32[]{:S(2)}, u32[]{:S(2)}) collective-permute-start(bf16[4,8,6144]{2,1,0:T(8,128)(2,1)S(1)} %get-tuple-element.71), channel_id=1, source_target_pairs={{0,32},{8,40},{16,48},{24,56},{32,64},{40,72},{48,80},{56,88},{64,... | collective-permute-start | bytes 1179656 | tf_op jit(solution)/shard_map/ppermute | solution.py:253
  6.3 16.6 %collective-permute-start.2 = (bf16[4,8,6144]{2,1,0:T(8,128)(2,1)S(1)}, bf16[4,8,6144]{2,1,0:T(8,128)(2,1)S(1)}, u32[]{:S(2)}, u32[]{:S(2)}) collective-permute-start(bf16[4,8,6144]{2,1,0:T(8,128)(2,1)S(1)} %get-tuple-element.72), channel_id=1, source_target_pairs={{0,24},{8,0},{16,8},{24,16},{32,56},{40,32},{48,40},{56,48},{64,88... | collective-permute-start | bytes 1179656 | tf_op jit(solution)/shard_map/ppermute | solution.py:246
  7.8 15.1 %collective-permute-start.3 = (bf16[4,8,6144]{2,1,0:T(8,128)(2,1)S(1)}, bf16[4,8,6144]{2,1,0:T(8,128)(2,1)S(1)}, u32[]{:S(2)}, u32[]{:S(2)}) collective-permute-start(bf16[4,8,6144]{2,1,0:T(8,128)(2,1)S(1)} %get-tuple-element.73), channel_id=1, source_target_pairs={{0,96},{8,104},{16,112},{24,120},{32,0},{40,8},{48,16},{56,24},{64... | collective-permute-start | bytes 1179656 | tf_op jit(solution)/shard_map/ppermute | solution.py:253
  9.2 15.2 %collective-permute-start.4 = (bf16[4,8,6144]{2,1,0:T(8,128)(2,1)S(1)}, bf16[4,8,6144]{2,1,0:T(8,128)(2,1)S(1)}, u32[]{:S(2)}, u32[]{:S(2)}) collective-permute-start(bf16[4,8,6144]{2,1,0:T(8,128)(2,1)S(1)} %get-tuple-element.74), channel_id=1, source_target_pairs={{0,16},{8,24},{16,0},{24,8},{32,48},{40,56},{48,32},{56,40},{64,80... | collective-permute-start | bytes 1179656 | tf_op jit(solution)/shard_map/ppermute | solution.py:246
  14.7 26.6 %copy-start.2 = (s32[12]{0:T(128)S(1)}, s32[12]{0:T(128)}, u32[]{:S(2)}) copy-start(s32[12]{0:T(128)} %param.9) | copy-start | bytes 148
  14.7 11.0 %collective-permute-start.5 = (bf16[4,8,6144]{2,1,0:T(8,128)(2,1)S(1)}, bf16[4,8,6144]{2,1,0:T(8,128)(2,1)S(1)}, u32[]{:S(2)}, u32[]{:S(2)}) collective-permute-start(bf16[4,8,6144]{2,1,0:T(8,128)(2,1)S(1)} %get-tuple-element.75), channel_id=1, source_target_pairs={{0,64},{8,72},{16,80},{24,88},{32,96},{40,104},{48,112},{56,120},{... | collective-permute-start | bytes 1179656 | tf_op jit(solution)/shard_map/ppermute | solution.py:253
  25.7 20.7 %all-to-all-start = ((bf16[16,3,64,128]{3,2,1,0:T(8,128)(2,1)}), bf16[16,3,64,128]{3,2,1,0:T(8,128)(2,1)S(1)}, u32[]{:S(2)}, u32[]{:S(2)}) async-start(bf16[16,3,64,128]{3,2,1,0:T(8,128)(2,1)} %moment_right.1), calls=%async_computation | async-start | bytes 1572864 | tf_op jit(solution)/shard_map/all_to_all | solution.py:332
  32.4 7.8 %collective-permute-start.10 = (bf16[8,6144]{1,0:T(8,128)(2,1)S(1)}, bf16[8,6144]{1,0:T(8,128)(2,1)S(1)}, u32[]{:S(2)}, u32[]{:S(2)}) collective-permute-start(bf16[8,6144]{1,0:T(8,128)(2,1)S(1)} %get-tuple-element.88), channel_id=1, source_target_pairs={{0,24},{8,0},{16,8},{24,16},{32,56},{40,32},{48,40},{56,48},{64,88... | collective-permute-start | bytes 294920 | tf_op jit(solution)/shard_map/ppermute | solution.py:246
  35.0 6.4 %collective-permute-start.11 = (bf16[8,6144]{1,0:T(8,128)(2,1)S(1)}, bf16[8,6144]{1,0:T(8,128)(2,1)S(1)}, u32[]{:S(2)}, u32[]{:S(2)}) collective-permute-start(bf16[8,6144]{1,0:T(8,128)(2,1)S(1)} %get-tuple-element.89), channel_id=1, source_target_pairs={{0,16},{8,24},{16,0},{24,8},{32,48},{40,56},{48,32},{56,40},{64,80... | collective-permute-start | bytes 294920 | tf_op jit(solution)/shard_map/ppermute | solution.py:246
  35.6 9.2 %collective-permute-start.6 = (bf16[8,6144]{1,0:T(8,128)(2,1)S(1)}, bf16[8,6144]{1,0:T(8,128)(2,1)S(1)}, u32[]{:S(2)}, u32[]{:S(2)}) collective-permute-start(bf16[8,6144]{1,0:T(8,128)(2,1)S(1)} %get-tuple-element.83), channel_id=1, source_target_pairs={{0,32},{8,40},{16,48},{24,56},{32,64},{40,72},{48,80},{56,88},{64,... | collective-permute-start | bytes 294920 | tf_op jit(solution)/shard_map/ppermute | solution.py:253
  36.8 8.1 %collective-permute-start.7 = (bf16[8,6144]{1,0:T(8,128)(2,1)S(1)}, bf16[8,6144]{1,0:T(8,128)(2,1)S(1)}, u32[]{:S(2)}, u32[]{:S(2)}) collective-permute-start(bf16[8,6144]{1,0:T(8,128)(2,1)S(1)} %get-tuple-element.84), channel_id=1, source_target_pairs={{0,96},{8,104},{16,112},{24,120},{32,0},{40,8},{48,16},{56,24},{64... | collective-permute-start | bytes 294920 | tf_op jit(solution)/shard_map/ppermute | solution.py:253
  38.3 7.5 %collective-permute-start.8 = (bf16[8,6144]{1,0:T(8,128)(2,1)S(1)}, bf16[8,6144]{1,0:T(8,128)(2,1)S(1)}, u32[]{:S(2)}, u32[]{:S(2)}) collective-permute-start(bf16[8,6144]{1,0:T(8,128)(2,1)S(1)} %get-tuple-element.85), channel_id=1, source_target_pairs={{0,64},{8,72},{16,80},{24,88},{32,96},{40,104},{48,112},{56,120},{... | collective-permute-start | bytes 294920 | tf_op jit(solution)/shard_map/ppermute | solution.py:253
  40.1 6.2 %collective-permute-start.9 = (bf16[8,6144]{1,0:T(8,128)(2,1)S(1)}, bf16[8,6144]{1,0:T(8,128)(2,1)S(1)}, u32[]{:S(2)}, u32[]{:S(2)}) collective-permute-start(bf16[8,6144]{1,0:T(8,128)(2,1)S(1)} %get-tuple-element.87), channel_id=1, source_target_pairs={{0,8},{8,16},{16,24},{24,0},{32,40},{40,48},{48,56},{56,32},{64,72... | collective-permute-start | bytes 294920 | tf_op jit(solution)/shard_map/ppermute | solution.py:246
  47.7 18.1 %all-to-all-start.1 = ((bf16[8,3,8,1024]{3,2,1,0:T(8,128)(2,1)}), bf16[8,3,8,1024]{3,2,1,0:T(8,128)(2,1)S(1)}, u32[]{:S(2)}, u32[]{:S(2)}) async-start(bf16[8,3,8,1024]{3,2,1,0:T(8,128)(2,1)} %bitcast.3), calls=%async_computation.1 | async-start | bytes 786432 | tf_op jit(solution)/shard_map/all_to_all | solution.py:332
  75.3 13.0 %collective-permute-start.17 = (bf16[3,64,1024]{2,1,0:T(8,128)(2,1)S(1)}, bf16[3,64,1024]{2,1,0:T(8,128)(2,1)S(1)}, u32[]{:S(2)}, u32[]{:S(2)}) collective-permute-start(bf16[3,64,1024]{2,1,0:T(8,128)(2,1)S(1)} %copy_bitcast_fusion.rows), channel_id=1, source_target_pairs={{0,64},{8,72},{16,80},{24,88},{32,96},{40,104},{48,112},{56,120},{... | collective-permute-start | bytes 1179656 | tf_op jit(solution)/shard_map/ppermute | solution.py:253
  78.1 13.0 %all-to-all-start.2 = ((bf16[16,3,32,128]{3,2,1,0:T(8,128)(2,1)}), bf16[16,3,32,128]{3,2,1,0:T(8,128)(2,1)S(1)}, u32[]{:S(2)}, u32[]{:S(2)}) async-start(bf16[16,3,32,128]{3,2,1,0:T(8,128)(2,1)} %get-tuple-element.104), calls=%async_computation.2 | async-start | bytes 786432 | tf_op jit(solution)/shard_map/all_to_all | solution.py:332
  81.7 16.3 %collective-permute-start.12 = (bf16[3,64,1024]{2,1,0:T(8,128)(2,1)S(1)}, bf16[3,64,1024]{2,1,0:T(8,128)(2,1)S(1)}, u32[]{:S(2)}, u32[]{:S(2)}) collective-permute-start(bf16[3,64,1024]{2,1,0:T(8,128)(2,1)S(1)} %copy_bitcast_fusion.rows), channel_id=1, source_target_pairs={{0,8},{8,16},{16,24},{24,0},{32,40},{40,48},{48,56},{56,32},{64,72... | collective-permute-start | bytes 1179656 | tf_op jit(solution)/shard_map/ppermute | solution.py:246
  82.9 17.6 %collective-permute-start.13 = (bf16[3,64,1024]{2,1,0:T(8,128)(2,1)S(1)}, bf16[3,64,1024]{2,1,0:T(8,128)(2,1)}, u32[]{:S(2)}, u32[]{:S(2)}) collective-permute-start(bf16[3,64,1024]{2,1,0:T(8,128)(2,1)S(1)} %copy_bitcast_fusion.rows), channel_id=1, source_target_pairs={{0,32},{8,40},{16,48},{24,56},{32,64},{40,72},{48,80},{56,88},{64,... | collective-permute-start | bytes 1179656 | tf_op jit(solution)/shard_map/ppermute | solution.py:253
  84.1 16.4 %collective-permute-start.14 = (bf16[3,64,1024]{2,1,0:T(8,128)(2,1)S(1)}, bf16[3,64,1024]{2,1,0:T(8,128)(2,1)}, u32[]{:S(2)}, u32[]{:S(2)}) collective-permute-start(bf16[3,64,1024]{2,1,0:T(8,128)(2,1)S(1)} %copy_bitcast_fusion.rows), channel_id=1, source_target_pairs={{0,24},{8,0},{16,8},{24,16},{32,56},{40,32},{48,40},{56,48},{64,88... | collective-permute-start | bytes 1179656 | tf_op jit(solution)/shard_map/ppermute | solution.py:246
  85.6 14.9 %collective-permute-start.15 = (bf16[3,64,1024]{2,1,0:T(8,128)(2,1)S(1)}, bf16[3,64,1024]{2,1,0:T(8,128)(2,1)}, u32[]{:S(2)}, u32[]{:S(2)}) collective-permute-start(bf16[3,64,1024]{2,1,0:T(8,128)(2,1)S(1)} %copy_bitcast_fusion.rows), channel_id=1, source_target_pairs={{0,96},{8,104},{16,112},{24,120},{32,0},{40,8},{48,16},{56,24},{64... | collective-permute-start | bytes 1179656 | tf_op jit(solution)/shard_map/ppermute | solution.py:253
  88.4 17.0 %collective-permute-start.16 = (bf16[3,64,1024]{2,1,0:T(8,128)(2,1)S(1)}, bf16[3,64,1024]{2,1,0:T(8,128)(2,1)}, u32[]{:S(2)}, u32[]{:S(2)}) collective-permute-start(bf16[3,64,1024]{2,1,0:T(8,128)(2,1)S(1)} %copy_bitcast_fusion.rows), channel_id=1, source_target_pairs={{0,16},{8,24},{16,0},{24,8},{32,48},{40,56},{48,32},{56,40},{64,80... | collective-permute-start | bytes 1179656 | tf_op jit(solution)/shard_map/ppermute | solution.py:246
  97.9 7.4 %copy-start = (bf16[3,64,1024]{2,1,0:T(8,128)(2,1)}, bf16[3,64,1024]{2,1,0:T(8,128)(2,1)S(1)}, u32[]{:S(2)}) copy-start(bf16[3,64,1024]{2,1,0:T(8,128)(2,1)S(1)} %collective-permute-done.12.x1) | copy-start | bytes 1179652
  105.4 20.6 %all-to-all-start.3 = ((bf16[16,3,64,128]{3,2,1,0:T(8,128)(2,1)}), bf16[16,3,64,128]{3,2,1,0:T(8,128)(2,1)S(1)}, u32[]{:S(2)}, u32[]{:S(2)}) async-start(bf16[16,3,64,128]{3,2,1,0:T(8,128)(2,1)} %rotate_left.1), calls=%async_computation.3 | async-start | bytes 1572864 | tf_op jit(solution)/shard_map/all_to_all | solution.py:332
  110.1 1.0 copy-start.1
  116.2 7.7 %collective-permute-start.18 = (bf16[3,64,256]{2,1,0:T(8,128)(2,1)S(1)}, bf16[3,64,256]{2,1,0:T(8,128)(2,1)S(1)}, u32[]{:S(2)}, u32[]{:S(2)}) collective-permute-start(bf16[3,64,256]{2,1,0:T(8,128)(2,1)S(1)} %get-tuple-element.113), channel_id=1, source_target_pairs={{0,96},{8,104},{16,112},{24,120},{32,0},{40,8},{48,16},{56,24},{64... | collective-permute-start | bytes 294920 | tf_op jit(solution)/shard_map/ppermute | solution.py:253
  118.8 7.1 %collective-permute-start.19 = (bf16[3,64,256]{2,1,0:T(8,128)(2,1)S(1)}, bf16[3,64,256]{2,1,0:T(8,128)(2,1)S(1)}, u32[]{:S(2)}, u32[]{:S(2)}) collective-permute-start(bf16[3,64,256]{2,1,0:T(8,128)(2,1)S(1)} %get-tuple-element.114), channel_id=1, source_target_pairs={{0,64},{8,72},{16,80},{24,88},{32,96},{40,104},{48,112},{56,120},{... | collective-permute-start | bytes 294920 | tf_op jit(solution)/shard_map/ppermute | solution.py:253
  119.4 6.5 %collective-permute-start.20 = (bf16[3,64,256]{2,1,0:T(8,128)(2,1)S(1)}, bf16[3,64,256]{2,1,0:T(8,128)(2,1)S(1)}, u32[]{:S(2)}, u32[]{:S(2)}) collective-permute-start(bf16[3,64,256]{2,1,0:T(8,128)(2,1)S(1)} %get-tuple-element.115), channel_id=1, source_target_pairs={{0,32},{8,40},{16,48},{24,56},{32,64},{40,72},{48,80},{56,88},{64,... | collective-permute-start | bytes 294920 | tf_op jit(solution)/shard_map/ppermute | solution.py:253
  120.0 17.7 %collective-permute-start.21 = (bf16[3,64,1024]{2,1,0:T(8,128)(2,1)}, bf16[3,64,1024]{2,1,0:T(8,128)(2,1)S(1)}, u32[]{:S(2)}, u32[]{:S(2)}) collective-permute-start(bf16[3,64,1024]{2,1,0:T(8,128)(2,1)} %get-tuple-element.122), channel_id=1, source_target_pairs={{0,8},{8,16},{16,24},{24,0},{32,40},{40,48},{48,56},{56,32},{64,72... | collective-permute-start | bytes 1179656 | tf_op jit(solution)/shard_map/ppermute | solution.py:246
  121.2 16.7 %collective-permute-start.22 = (bf16[3,64,1024]{2,1,0:T(8,128)(2,1)}, bf16[3,64,1024]{2,1,0:T(8,128)(2,1)S(1)}, u32[]{:S(2)}, u32[]{:S(2)}) collective-permute-start(bf16[3,64,1024]{2,1,0:T(8,128)(2,1)} %get-tuple-element.123), channel_id=1, source_target_pairs={{0,16},{8,24},{16,0},{24,8},{32,48},{40,56},{48,32},{56,40},{64,80... | collective-permute-start | bytes 1179656 | tf_op jit(solution)/shard_map/ppermute | solution.py:246
  123.9 15.6 %collective-permute-start.23 = (bf16[3,64,1024]{2,1,0:T(8,128)(2,1)}, bf16[3,64,1024]{2,1,0:T(8,128)(2,1)S(1)}, u32[]{:S(2)}, u32[]{:S(2)}) collective-permute-start(bf16[3,64,1024]{2,1,0:T(8,128)(2,1)} %get-tuple-element.124), channel_id=1, source_target_pairs={{0,24},{8,0},{16,8},{24,16},{32,56},{40,32},{48,40},{56,48},{64,88... | collective-permute-start | bytes 1179656 | tf_op jit(solution)/shard_map/ppermute | solution.py:246
  131.2 14.6 %all-to-all-start.4 = ((bf16[8,3,8,1024]{3,2,1,0:T(8,128)(2,1)}), bf16[8,3,8,1024]{3,2,1,0:T(8,128)(2,1)S(1)}, u32[]{:S(2)}, u32[]{:S(2)}) async-start(bf16[8,3,8,1024]{3,2,1,0:T(8,128)(2,1)} %get-tuple-element.126), calls=%async_computation.4 | async-start | bytes 786432 | tf_op jit(solution)/shard_map/all_to_all | solution.py:332

commit v3 on v2

--- a/solution.py
+++ b/solution.py
@@ -194,8 +194,8 @@
 
 
 def gram_tiles_kernel(
-    here, rows, x1, y1, x3, y3, x2, y2,
-    left0, left1, left2, left3, right0, right1, right2, right3,
+    here, rows, x2, y2, x1, y1, y3,
+    own, left0, left1, left2, left3, right0, right1, right2, right3,
     across, down, grams, sems,
 ):
     y, x = here[0], here[1]
@@ -203,39 +203,61 @@
     lines = SIDE * slab
     start = pl.multiple_of(y * lines, lines)
     copies = []
-    for back, (ref_x, ref_y) in enumerate(((rows, rows), (x1, y1), (x2, y2), (x3, y3))):
-        copies.append(pltpu.make_async_copy(ref_x, across.at[turn(x, SIDE - back)], sems.at[0, back]))
-        copies.append(pltpu.make_async_copy(ref_y, down.at[back], sems.at[1, back]))
+    for back, ref in enumerate((x1, x2)):
+        copies.append(pltpu.make_async_copy(ref, across.at[back], sems.at[0, back]))
+    for back, ref in enumerate((rows, y1, y2, y3)):
+        copies.append(pltpu.make_async_copy(ref, down.at[back], sems.at[1, back]))
     wait_all(start_all(copies))
     for slot in range(slots):
         panel = down[:, slot].reshape(lines, order)
-        tile = dot(panel, across[:, slot].reshape(lines, order), NT)
+        tile = dot(panel, across[:, slot].reshape(2 * slab, order), NT)
+        own[slot] = dot(down[0, slot], panel, NT)
         for back, out in enumerate((left0, left1, left2, left3)):
             out[slot] = tile[back * slab : (back + 1) * slab].astype(out.dtype)
         columns = down[:, slot, :, pl.ds(start, lines)].reshape(lines, lines)
         grams[...] = dot(columns, panel, TN).reshape(grams.shape)
         for by, out in enumerate((right0, right1, right2, right3)):
-            out[slot] = grams[turn(x, by)].astype(out.dtype)
+            out[slot, :, :order] = grams[turn(x, by)].astype(out.dtype)
+        right3[slot, :, order:] = dot(across[0, slot], panel, NT).astype(BF16)
+
+
+def spread(pair, which):
+    other = swap_halves(pair)
+    low = low_lanes(pair.shape[0])
+    twice = jnp.where(low, pair, other) if which == 0 else jnp.where(low, other, pair)
+    return jnp.concatenate([twice, twice], axis=1)
 
 
 def gram_sum_kernel(
-    here, used, left0, left1, left2, left3, right0, right1, right2, right3, left_hbm, right_hbm,
+    here, used, own, left0, left1, left2, left3, right0, right1, right2, right3, left_hbm, right_hbm,
     new_left, new_right, left, right, sems,
 ):
-    y = here[0]
+    y, x = here[0], here[1]
     old = start_all(
         [pltpu.make_async_copy(left_hbm, left, sems.at[0]), pltpu.make_async_copy(right_hbm, right, sems.at[1])]
     )
+    slots, slab, order = left.shape
+    lines = own.shape[2]
+    column = lax.broadcasted_iota(jnp.int32, (slab, lines), 1) // HALF
     wait_all(old)
-    lines = left0.shape[2]
-    for slot in range(left.shape[0]):
+    for slot in range(slots):
         is_used = used[slot] > 0
         for ahead, tile in enumerate((left0, left1, left2, left3)):
+            back = (SIDE - ahead) % SIDE
+            same = spread(own[slot, :, back // 2 * LANES :][:, :LANES], back % 2)
+            first = order + back // 2 * LANES
+            ahead_x = spread(right3[slot, :, first : first + LANES].astype(F32), back % 2)
+            tile = tile[slot].astype(F32)
+            gram = jnp.where(column == turn(x, 1), ahead_x, same)
+            gram = jnp.where(column == turn(x, 3), spread(tile, 0), gram)
+            gram = jnp.where(column == turn(x, 2), spread(tile, 1), gram)
             lanes = pl.ds(pl.multiple_of(turn(y, ahead) * lines, lines), lines)
             new_left[slot, :, lanes] = jnp.where(
-                is_used, BETA_FACTOR * left[slot, :, lanes] + (1.0 - BETA_FACTOR) * tile[slot].astype(F32), 0.0
+                is_used, BETA_FACTOR * left[slot, :, lanes] + (1.0 - BETA_FACTOR) * gram, 0.0
             )
-        gram = right0[slot] + right1[slot].astype(F32) + right2[slot].astype(F32) + right3[slot].astype(F32)
+        gram = right0[slot]
+        for term in (right1, right2, right3):
+            gram = gram + term[slot, :, :order].astype(F32)
         new_right[slot] = jnp.where(is_used, BETA_FACTOR * right[slot] + (1.0 - BETA_FACTOR) * gram, 0.0)
 
 
@@ -282,12 +304,12 @@
     for k, by in enumerate((1, 3, 2)):
         got += [along_x(sent[2 * k], by), along_y(sent[2 * k + 1], by)]
     got, early = lax.optimization_barrier((got, beside()))
+    early = between(early)
     pieces = call(
         second_send_kernel, "second_send", [(here, SMEM), (grad, HBM)] + [(value, VMEM) for value in got],
         [((rows, half), BF16, None if by % SIDE == 0 else VMEM) for by in range(2 * SIDE)],
         [pltpu.VMEM(line, BF16), pltpu.VMEM(line, BF16), pltpu.SemaphoreType.DMA((2,))], 0, 4,
     )
-    early = between(early)
     p, q = [pieces[0]], [pieces[4]]
     for by in (1, 3, 2):
         p.append(along_y(pieces[by], by))
@@ -346,6 +368,11 @@
         grad_part[0], here, holder, owners * slots, order, moment_right, lambda value: exchange(value, "dp")
     )
     incoming = exchange(outgoing.reshape(owners, slots, part_rows, order), "owner")
+    ready = call(
+        moment_left_kernel, "moment_left", [(early, VMEM), (left_basis, HBM)],
+        [((slots, 2 * slab, order), F32, VMEM)], basis_scratch, 3, 8,
+    )[0]
+    incoming, ready = lax.optimization_barrier((incoming, ready))
     rows = incoming.transpose(1, 0, 2, 3).reshape(slabs)
 
     new_first, packed = call(
@@ -354,18 +381,12 @@
         [(slabs, BF16, None), ((replicas, slots, slab // 2, LANES), BF16, VMEM)],
         [pltpu.VMEM(slabs, BF16), basis_scratch[0], pltpu.SemaphoreType.DMA((1,)), basis_scratch[1]], 3, 8,
     )
-    rows, packed, early = lax.optimization_barrier((rows, packed, early))
+    rows, packed = lax.optimization_barrier((rows, packed))
     packed = exchange(packed, "dp")
     near = []
-    for by in (1, 3):
+    for by in (2, 1):
         near += [along_x(rows, by), along_y(rows, by)]
-    near.append(along_x(rows, 2))
-    ready = call(
-        moment_left_kernel, "moment_left", [(early, VMEM), (left_basis, HBM)],
-        [((slots, 2 * slab, order), F32, VMEM)], basis_scratch, 3, 8,
-    )[0]
-    rows, ready = lax.optimization_barrier((rows, ready))
-    near.append(along_y(rows, 2))
+    near.append(along_y(rows, 3))
     turned = call(
         rotate_left_kernel, "rotate_left", [(packed, VMEM), (left_basis, HBM), (ready, VMEM)],
         [(chunks, BF16, VMEM)], basis_scratch, 9, 8,
@@ -373,18 +394,18 @@
     near, turned = lax.optimization_barrier((near, turned))
     turned = exchange(turned, "dp")
     tiles = call(
-        gram_tiles_kernel, "gram_tiles", [(here, SMEM)] + [(value, ANY) for value in [rows] + near],
-        [((slots, slab, SIDE * slab), F32 if k == 0 else BF16, VMEM) for k in range(SIDE)]
-        + [(slabs, F32 if k == 0 else BF16, VMEM) for k in range(SIDE)],
+        gram_tiles_kernel, "gram_tiles", [(here, SMEM)] + [(value, HBM) for value in [rows] + near],
+        [((slots, slab, SIDE * slab), F32, VMEM)]
+        + [((slots, slab, 2 * slab), F32 if k == 0 else BF16, VMEM) for k in range(SIDE)]
+        + [(slabs, F32, VMEM), (slabs, BF16, VMEM), (slabs, BF16, VMEM), ((slots, slab, order + SIDE * slab), BF16, VMEM)],
         [
-            pltpu.VMEM((SIDE, slots, slab, order), BF16), pltpu.VMEM((SIDE, slots, slab, order), BF16),
+            pltpu.VMEM((2, slots, slab, order), BF16), pltpu.VMEM((SIDE, slots, slab, order), BF16),
             pltpu.VMEM((SIDE, slab, order), F32), pltpu.SemaphoreType.DMA((2, SIDE)),
         ],
         9, 6,
     )
-    lefts = [tiles[0]] + [along_y(tiles[back], SIDE - back) for back in (1, 2, 3)]
-    rights = [tiles[SIDE]] + [along_x(tiles[SIDE + by], by) for by in (1, 2, 3)]
-    lefts, turned = lax.optimization_barrier((lefts, turned))
+    lefts = [tiles[1]] + [along_y(tiles[1 + back], SIDE - back) for back in (1, 2, 3)]
+    rights = [tiles[1 + SIDE]] + [along_x(tiles[1 + SIDE + by], by) for by in (1, 2, 3)]
     new_second, step = call(
         step_kernel, "step_rows", [(used, SMEM), (turned, VMEM), (right_basis, HBM)],
         [(slabs, BF16, None), ((owners, slots, part_rows, order), BF16, VMEM)], basis_scratch, 3, 8,
@@ -393,7 +414,7 @@
     rights, step = lax.optimization_barrier((rights, step))
     new_left, new_right = call(
         gram_sum_kernel, "gram_sum",
-        [(here, SMEM), (used, SMEM)] + [(value, VMEM) for value in lefts + rights]
+        [(here, SMEM), (used, SMEM)] + [(value, VMEM) for value in [tiles[0]] + lefts + rights]
         + [(left_factor, HBM), (right_factor, HBM)],
         [(slabs, F32, None)] * 2,
         [pltpu.VMEM(slabs, F32), pltpu.VMEM(slabs, F32), pltpu.SemaphoreType.DMA((2,))], 0, 8,

time: 148 us -> 144 us (0.973)
  starting transfers between devices: 67.4 us -> 63.9 us
    all_to_all x5, waiting for transfers between devices: 12.8 us -> 8.48 us  [exchange(): return lax.all_to_all(value, axis, split_axis=0, concat_axis=0, tiled=True)]
    ppermute x12 -> x11, waiting for transfers between devices: 13.3 us -> 15.8 us  [along_x(): return lax.ppermute(value, 'dp', pairs)]
    ppermute x12, starting transfers between devices: 19.4 us -> 17 us  [along_y(): return lax.ppermute(value, 'dp', pairs)]
    ppermute x12, waiting for transfers between devices: 9.86 us -> 12.1 us  [along_y(): return lax.ppermute(value, 'dp', pairs)]
    ppermute x12 -> x11, starting transfers between devices: 18.5 us -> 17 us  [along_x(): return lax.ppermute(value, 'dp', pairs)]
  transfers between devices with their start and end apart: 29 -> 28, of which waited for: 17 -> 17; matrix products, arithmetic and copies ran while one was open for 0% -> 0% of each run, Pallas kernels for 19% -> 22%
where the time goes in v3:
time: 144 us
  starting transfers between devices  63.9 us (44%)
  Pallas kernels  40.8 us (28%)
  waiting for transfers between devices  36.4 us (25%)
    pallas_call x10, Pallas kernels, call(): pl.pallas_call(kernel, in_specs=[pl.BlockSpec(memory_space=space) for _,...  40.8 us
    all_to_all x5, starting transfers between devices, exchange(): return lax.all_to_all(value, axis, split_axis=0, concat_axis=0, tiled=True)  29.9 us
    ppermute x11, starting transfers between devices, along_x(): return lax.ppermute(value, 'dp', pairs)  17 us
    ppermute x12, starting transfers between devices, along_y(): return lax.ppermute(value, 'dp', pairs)  17 us
    ppermute x11, waiting for transfers between devices, along_x(): return lax.ppermute(value, 'dp', pairs)  15.8 us
    ppermute x12, waiting for transfers between devices, along_y(): return lax.ppermute(value, 'dp', pairs)  12.1 us
    all_to_all x5, waiting for transfers between devices, exchange(): return lax.all_to_all(value, axis, split_axis=0, concat_axis=0, tiled=True)  8.48 us
  transfers between devices with their start and end apart: 28, of which 17 were waited for; matrix products, arithmetic and copies ran while one was open for 0% of the time, Pallas kernels for 22%

profile of v3, /device:TPU:1, one launch (start us, length us, event | category | flops | bytes accessed | tf_op | source)
XLA Modules:
  0.0 143.5 jit_solution(12013145165579754878)
XLA Ops:
  0.7 0.1 pad_add_fusion.here
  0.7 2.2 %first_send.1 = (bf16[4,8,6144]{2,1,0:T(8,128)(2,1)S(1)}, bf16[4,8,6144]{2,1,0:T(8,128)(2,1)S(1)}, bf16[4,8,6144]{2,1,0:T(8,128)(2,1)S(1)}, bf16[4,8,6144]{2,1,0...) custom-call(s32[2]{0:T(128)S(1)} %pad_add_fusion.here, bf16[4,4,8,12288]{3,2,1,0:T(8,128)(2,1)} %bitcast.13), custom_call_target="tpu_custom_call" | custom-call | bytes 5242880 | tf_op jit(solution)/shard_map/first_send/pallas_call | solution.py:280
  2.9 2.1 %collective-permute-start = (bf16[4,8,6144]{2,1,0:T(8,128)(2,1)S(1)}, bf16[4,8,6144]{2,1,0:T(8,128)(2,1)S(1)}, u32[]{:S(2)}, u32[]{:S(2)}) collective-permute-start(bf16[4,8,6144]{2,1,0:T(8,128)(2,1)S(1)} %get-tuple-element.64), channel_id=1, source_target_pairs={{0,8},{8,16},{16,24},{24,0},{32,40},{40,48},{48,56},{56,32},{64,72... | collective-permute-start | bytes 1179656 | tf_op jit(solution)/shard_map/ppermute | solution.py:268
  5.0 1.3 collective-permute-start.1
  6.3 1.5 %collective-permute-start.2 = (bf16[4,8,6144]{2,1,0:T(8,128)(2,1)S(1)}, bf16[4,8,6144]{2,1,0:T(8,128)(2,1)S(1)}, u32[]{:S(2)}, u32[]{:S(2)}) collective-permute-start(bf16[4,8,6144]{2,1,0:T(8,128)(2,1)S(1)} %get-tuple-element.66), channel_id=1, source_target_pairs={{0,24},{8,0},{16,8},{24,16},{32,56},{40,32},{48,40},{56,48},{64,88... | collective-permute-start | bytes 1179656 | tf_op jit(solution)/shard_map/ppermute | solution.py:268
  7.8 1.4 %collective-permute-start.3 = (bf16[4,8,6144]{2,1,0:T(8,128)(2,1)S(1)}, bf16[4,8,6144]{2,1,0:T(8,128)(2,1)S(1)}, u32[]{:S(2)}, u32[]{:S(2)}) collective-permute-start(bf16[4,8,6144]{2,1,0:T(8,128)(2,1)S(1)} %get-tuple-element.67), channel_id=1, source_target_pairs={{0,96},{8,104},{16,112},{24,120},{32,0},{40,8},{48,16},{56,24},{64... | collective-permute-start | bytes 1179656 | tf_op jit(solution)/shard_map/ppermute | solution.py:275
  9.2 1.5 %collective-permute-start.4 = (bf16[4,8,6144]{2,1,0:T(8,128)(2,1)S(1)}, bf16[4,8,6144]{2,1,0:T(8,128)(2,1)S(1)}, u32[]{:S(2)}, u32[]{:S(2)}) collective-permute-start(bf16[4,8,6144]{2,1,0:T(8,128)(2,1)S(1)} %get-tuple-element.68), channel_id=1, source_target_pairs={{0,16},{8,24},{16,0},{24,8},{32,48},{40,56},{48,32},{56,40},{64,80... | collective-permute-start | bytes 1179656 | tf_op jit(solution)/shard_map/ppermute | solution.py:268
  10.8 3.9 %collective-permute-done.a1 = bf16[4,8,6144]{2,1,0:T(8,128)(2,1)S(1)} collective-permute-done((bf16[4,8,6144]{2,1,0:T(8,128)(2,1)S(1)}, bf16[4,8,6144]{2,1,0:T(8,128)(2,1)S(1)}, u32[]{:S(2)}, u32[]{:S(2)}) %collective-permute-start) | collective-permute-done | bytes 393248 | tf_op jit(solution)/shard_map/ppermute | solution.py:268
  14.7 3.2 %collective-permute-start.5 = (bf16[4,8,6144]{2,1,0:T(8,128)(2,1)S(1)}, bf16[4,8,6144]{2,1,0:T(8,128)(2,1)S(1)}, u32[]{:S(2)}, u32[]{:S(2)}) collective-permute-start(bf16[4,8,6144]{2,1,0:T(8,128)(2,1)S(1)} %get-tuple-element.69), channel_id=1, source_target_pairs={{0,64},{8,72},{16,80},{24,88},{32,96},{40,104},{48,112},{56,120},{... | collective-permute-start | bytes 1179656 | tf_op jit(solution)/shard_map/ppermute | solution.py:275
  17.9 5.0 %moment_right.1 = bf16[16,3,64,128]{3,2,1,0:T(8,128)(2,1)} custom-call(bf16[3,64,1024]{2,1,0:T(8,128)(2,1)} %moment_hbm.3, bf16[3,64,1024]{2,1,0:T(8,128)(2,1)} %second_hbm.1, bf16[3,1024,1024]{2,1,0:T(8,128)(2,1)} %basis_hbm.9), custom_call_target="tpu_custom_call" | custom-call | flops 402653184 | bytes 8388608 | tf_op jit(solution)/shard_map/moment_right/pallas_call | solution.py:280
  22.9 0.0 collective-permute-done.1.b1
  22.9 0.0 collective-permute-done.3.b3
  23.0 1.5 %collective-permute-done.4.a2 = bf16[4,8,6144]{2,1,0:T(8,128)(2,1)S(1)} collective-permute-done((bf16[4,8,6144]{2,1,0:T(8,128)(2,1)S(1)}, bf16[4,8,6144]{2,1,0:T(8,128)(2,1)S(1)}, u32[]{:S(2)}, u32[]{:S(2)}) %collective-permute-start.4) | collective-permute-done | bytes 393248 | tf_op jit(solution)/shard_map/ppermute | solution.py:268
  24.4 1.2 collective-permute-done.5.b2
  25.7 4.6 %all-to-all-start = ((bf16[16,3,64,128]{3,2,1,0:T(8,128)(2,1)}), bf16[16,3,64,128]{3,2,1,0:T(8,128)(2,1)S(1)}, u32[]{:S(2)}, u32[]{:S(2)}) async-start(bf16[16,3,64,128]{3,2,1,0:T(8,128)(2,1)} %moment_right.1), calls=%async_computation | async-start | bytes 1572864 | tf_op jit(solution)/shard_map/all_to_all | solution.py:354
  30.3 2.1 %second_send.1 = (bf16[8,6144]{1,0:T(8,128)(2,1)S(1)}, bf16[8,6144]{1,0:T(8,128)(2,1)S(1)}, bf16[8,6144]{1,0:T(8,128)(2,1)S(1)}, bf16[8,6144]{1,0:T(8,128)(2,1)S...) custom-call(s32[2]{0:T(128)S(1)} %pad_add_fusion.here, ...), custom_call_target="tpu_custom_call" | custom-call | bytes 4194304 | tf_op jit(solution)/shard_map/second_send/pallas_call | solution.py:280
  32.4 2.6 %collective-permute-start.10 = (bf16[8,6144]{1,0:T(8,128)(2,1)S(1)}, bf16[8,6144]{1,0:T(8,128)(2,1)S(1)}, u32[]{:S(2)}, u32[]{:S(2)}) collective-permute-start(bf16[8,6144]{1,0:T(8,128)(2,1)S(1)} %get-tuple-element.82), channel_id=1, source_target_pairs={{0,24},{8,0},{16,8},{24,16},{32,56},{40,32},{48,40},{56,48},{64,88... | collective-permute-start | bytes 294920 | tf_op jit(solution)/shard_map/ppermute | solution.py:268
  35.0 0.6 collective-permute-start.11
  35.6 1.2 collective-permute-start.6
  36.8 1.5 %collective-permute-start.7 = (bf16[8,6144]{1,0:T(8,128)(2,1)S(1)}, bf16[8,6144]{1,0:T(8,128)(2,1)S(1)}, u32[]{:S(2)}, u32[]{:S(2)}) collective-permute-start(bf16[8,6144]{1,0:T(8,128)(2,1)S(1)} %get-tuple-element.78), channel_id=1, source_target_pairs={{0,96},{8,104},{16,112},{24,120},{32,0},{40,8},{48,16},{56,24},{64... | collective-permute-start | bytes 294920 | tf_op jit(solution)/shard_map/ppermute | solution.py:275
  38.3 1.5 %collective-permute-start.8 = (bf16[8,6144]{1,0:T(8,128)(2,1)S(1)}, bf16[8,6144]{1,0:T(8,128)(2,1)S(1)}, u32[]{:S(2)}, u32[]{:S(2)}) collective-permute-start(bf16[8,6144]{1,0:T(8,128)(2,1)S(1)} %get-tuple-element.79), channel_id=1, source_target_pairs={{0,64},{8,72},{16,80},{24,88},{32,96},{40,104},{48,112},{56,120},{... | collective-permute-start | bytes 294920 | tf_op jit(solution)/shard_map/ppermute | solution.py:275
  39.7 0.4 collective-permute-done.10.q2
  40.1 1.1 collective-permute-start.9
  41.3 0.1 select_reduce_fusion.holder
  41.4 0.0 collective-permute-done.11.q3
  41.4 3.5 %collective-permute-done.6.p1 = bf16[8,6144]{1,0:T(8,128)(2,1)S(1)} collective-permute-done((bf16[8,6144]{1,0:T(8,128)(2,1)S(1)}, bf16[8,6144]{1,0:T(8,128)(2,1)S(1)}, u32[]{:S(2)}, u32[]{:S(2)}) %collective-permute-start.6) | collective-permute-done | bytes 98336 | tf_op jit(solution)/shard_map/ppermute | solution.py:275
  44.8 1.0 collective-permute-done.8.p3
  45.8 0.5 collective-permute-done.9.q1
  46.3 1.4 outgoing.1
  47.7 10.0 %all-to-all-start.1 = ((bf16[8,3,8,1024]{3,2,1,0:T(8,128)(2,1)}), bf16[8,3,8,1024]{3,2,1,0:T(8,128)(2,1)S(1)}, u32[]{:S(2)}, u32[]{:S(2)}) async-start(bf16[8,3,8,1024]{3,2,1,0:T(8,128)(2,1)} %bitcast.3), calls=%async_computation.1 | async-start | bytes 786432 | tf_op jit(solution)/shard_map/all_to_all | solution.py:354
  57.8 0.1 fusion
  57.9 0.1 dynamic_slice.3.used
  58.0 3.4 %moment_left.1.ready = f32[3,128,1024]{2,1,0:T(8,128)S(1)} custom-call(bf16[16,3,64,128]{3,2,1,0:T(8,128)(2,1)S(1)} %all-to-all-done.packed, bf16[3,1024,1024]{2,1,0:T(8,128)(2,1)} %basis_hbm.8), custom_call_target="tpu_custom_call" | custom-call | flops 402653184 | bytes 8388608 | tf_op jit(solution)/shard_map/moment_left/pallas_call | solution.py:280
  61.4 4.5 %all-to-all-done.1 = bf16[8,3,8,1024]{3,2,1,0:T(8,128)(2,1)S(1)} async-done(((bf16[8,3,8,1024]{3,2,1,0:T(8,128)(2,1)}), bf16[8,3,8,1024]{3,2,1,0:T(8,128)(2,1)S(1)}, u32[]{:S(2)}, u32[]{:S(2)}) %all-to-all-start.1) | async-done | bytes 393248 | tf_op jit(solution)/shard_map/all_to_all | solution.py:354
  65.9 0.0 copy-start
  65.9 6.0 %rotate_right.1 = (bf16[3,64,1024]{2,1,0:T(8,128)(2,1)}, bf16[16,3,32,128]{3,2,1,0:T(8,128)(2,1)}) custom-call(s32[3]{0:T(128)S(1)} %dynamic_slice.3.used, bf16[3,64,1024]{2,1,0:T(8,128)(2,1)S(1)} %copy_bitcast_fusion.rows, bf16[3,64,1024]{2,1,0:T(8,128)(2,1)} %moment_hbm.3, bf16[3,1024,1024]{2,1,0:T(8,128)(2,1)} %basis_hbm.9), custom_call_target="tpu_custom_call" | custom-call | flops 402653184 | bytes 8388608 | tf_op jit(solution)/shard_map/rotate_right/pallas_call | solution.py:280
  71.9 4.9 %all-to-all-start.2 = ((bf16[16,3,32,128]{3,2,1,0:T(8,128)(2,1)}), bf16[16,3,32,128]{3,2,1,0:T(8,128)(2,1)S(1)}, u32[]{:S(2)}, u32[]{:S(2)}) async-start(bf16[16,3,32,128]{3,2,1,0:T(8,128)(2,1)} %get-tuple-element.97), calls=%async_computation.2 | async-start | bytes 786432 | tf_op jit(solution)/shard_map/all_to_all | solution.py:354
  76.9 2.9 %collective-permute-start.12 = (bf16[3,64,1024]{2,1,0:T(8,128)(2,1)S(1)}, bf16[3,64,1024]{2,1,0:T(8,128)(2,1)S(1)}, u32[]{:S(2)}, u32[]{:S(2)}) collective-permute-start(bf16[3,64,1024]{2,1,0:T(8,128)(2,1)S(1)} %copy_bitcast_fusion.rows), channel_id=1, source_target_pairs={{0,16},{8,24},{16,0},{24,8},{32,48},{40,56},{48,32},{56,40},{64,80... | collective-permute-start | bytes 1179656 | tf_op jit(solution)/shard_map/ppermute | solution.py:268
  79.8 2.7 %collective-permute-start.13 = (bf16[3,64,1024]{2,1,0:T(8,128)(2,1)S(1)}, bf16[3,64,1024]{2,1,0:T(8,128)(2,1)S(1)}, u32[]{:S(2)}, u32[]{:S(2)}) collective-permute-start(bf16[3,64,1024]{2,1,0:T(8,128)(2,1)S(1)} %copy_bitcast_fusion.rows), channel_id=1, source_target_pairs={{0,64},{8,72},{16,80},{24,88},{32,96},{40,104},{48,112},{56,120},{... | collective-permute-start | bytes 1179656 | tf_op jit(solution)/shard_map/ppermute | solution.py:275
  82.4 0.3 collective-permute-start.14
  82.7 0.3 collective-permute-start.15
  83.0 2.4 %collective-permute-start.16 = (bf16[3,64,1024]{2,1,0:T(8,128)(2,1)S(1)}, bf16[3,64,1024]{2,1,0:T(8,128)(2,1)}, u32[]{:S(2)}, u32[]{:S(2)}) collective-permute-start(bf16[3,64,1024]{2,1,0:T(8,128)(2,1)S(1)} %copy_bitcast_fusion.rows), channel_id=1, source_target_pairs={{0,96},{8,104},{16,112},{24,120},{32,0},{40,8},{48,16},{56,24},{64... | collective-permute-start | bytes 1179656 | tf_op jit(solution)/shard_map/ppermute | solution.py:275
  85.4 0.5 all-to-all-done.2.packed
  85.9 6.5 %rotate_left.1 = bf16[16,3,64,128]{3,2,1,0:T(8,128)(2,1)} custom-call(bf16[16,3,32,128]{3,2,1,0:T(8,128)(2,1)S(1)} %all-to-all-done.2.packed, bf16[3,1024,1024]{2,1,0:T(8,128)(2,1)} %basis_hbm.8, f32[3,128,1024]{2,1,0:T(8,128)S(1)} %moment_left.1.ready), custom_call_target="tpu_custom_call" | custom-call | flops 1207959552 | bytes 8388608 | tf_op jit(solution)/shard_map/rotate_left/pallas_call | solution.py:280
  92.5 1.9 %collective-permute-done.13.y2 = bf16[3,64,1024]{2,1,0:T(8,128)(2,1)S(1)} collective-permute-done((bf16[3,64,1024]{2,1,0:T(8,128)(2,1)S(1)}, bf16[3,64,1024]{2,1,0:T(8,128)(2,1)S(1)}, u32[]{:S(2)}, u32[]{:S(2)}) %collective-permute-start.13) | collective-permute-done | bytes 393248 | tf_op jit(solution)/shard_map/ppermute | solution.py:275
  94.4 7.8 %collective-permute-done.14.x1 = bf16[3,64,1024]{2,1,0:T(8,128)(2,1)} collective-permute-done((bf16[3,64,1024]{2,1,0:T(8,128)(2,1)S(1)}, bf16[3,64,1024]{2,1,0:T(8,128)(2,1)}, u32[]{:S(2)}, u32[]{:S(2)}) %collective-permute-start.14) | collective-permute-done | bytes 393248 | tf_op jit(solution)/shard_map/ppermute | solution.py:268
  102.1 1.3 collective-permute-done.15.y1
  103.4 3.7 %all-to-all-start.3 = ((bf16[16,3,64,128]{3,2,1,0:T(8,128)(2,1)}), bf16[16,3,64,128]{3,2,1,0:T(8,128)(2,1)S(1)}, u32[]{:S(2)}, u32[]{:S(2)}) async-start(bf16[16,3,64,128]{3,2,1,0:T(8,128)(2,1)} %rotate_left.1), calls=%async_computation.3 | async-start | bytes 1572864 | tf_op jit(solution)/shard_map/all_to_all | solution.py:354
  107.1 5.4 %gram_tiles.1 = (f32[3,64,256]{2,1,0:T(8,128)S(1)}, f32[3,64,128]{2,1,0:T(8,128)S(1)}, bf16[3,64,128]{2,1,0:T(8,128)(2,1)S(1)}, bf16[3,64,128]{2,1,0:T(8,128)(2,...) custom-call(s32[2]{0:T(128)S(1)} %pad_add_fusion.here, ...), custom_call_target="tpu_custom_call" | custom-call | flops 1207959552 | bytes 6291456 | tf_op jit(solution)/shard_map/gram_tiles/pallas_call | solution.py:280
  112.5 1.4 collective-permute-start.20
  114.0 1.3 collective-permute-start.22
  115.3 1.7 %collective-permute-start.21 = (bf16[3,64,1024]{2,1,0:T(8,128)(2,1)}, bf16[3,64,1024]{2,1,0:T(8,128)(2,1)S(1)}, u32[]{:S(2)}, u32[]{:S(2)}) collective-permute-start(bf16[3,64,1024]{2,1,0:T(8,128)(2,1)} %get-tuple-element.111), channel_id=1, source_target_pairs={{0,16},{8,24},{16,0},{24,8},{32,48},{40,56},{48,32},{56,40},{64,80... | collective-permute-start | bytes 1179656 | tf_op jit(solution)/shard_map/ppermute | solution.py:268
  116.9 3.5 %all-to-all-done.3.packed = bf16[16,3,64,128]{3,2,1,0:T(8,128)(2,1)S(1)} async-done(((bf16[16,3,64,128]{3,2,1,0:T(8,128)(2,1)}), bf16[16,3,64,128]{3,2,1,0:T(8,128)(2,1)S(1)}, u32[]{:S(2)}, u32[]{:S(2)}) %all-to-all-start.3) | async-done | bytes 786464 | tf_op jit(solution)/shard_map/all_to_all | solution.py:354
  120.4 5.2 %step_rows.1 = (bf16[3,64,1024]{2,1,0:T(8,128)(2,1)}, bf16[8,3,8,1024]{3,2,1,0:T(8,128)(2,1)}) custom-call(s32[3]{0:T(128)S(1)} %dynamic_slice.3.used, bf16[16,3,64,128]{3,2,1,0:T(8,128)(2,1)S(1)} %all-to-all-done.3.packed, bf16[3,1024,1024]{2,1,0:T(8,128)(2,1)} %basis_hbm.9), custom_call_target="tpu_custom_call" | custom-call | flops 402653184 | bytes 8388608 | tf_op jit(solution)/shard_map/step_rows/pallas_call | solution.py:280
  125.6 6.7 %all-to-all-start.4 = ((bf16[8,3,8,1024]{3,2,1,0:T(8,128)(2,1)}), bf16[8,3,8,1024]{3,2,1,0:T(8,128)(2,1)S(1)}, u32[]{:S(2)}, u32[]{:S(2)}) async-start(bf16[8,3,8,1024]{3,2,1,0:T(8,128)(2,1)} %get-tuple-element.114), calls=%async_computation.4 | async-start | bytes 786432 | tf_op jit(solution)/shard_map/all_to_all | solution.py:354
  132.3 0.6 collective-permute-start.17
  132.9 0.3 collective-permute-start.18
  133.1 0.6 collective-permute-start.19
  133.8 1.7 %collective-permute-done.21.right2 = bf16[3,64,1024]{2,1,0:T(8,128)(2,1)S(1)} collective-permute-done((bf16[3,64,1024]{2,1,0:T(8,128)(2,1)}, bf16[3,64,1024]{2,1,0:T(8,128)(2,1)S(1)}, u32[]{:S(2)}, u32[]{:S(2)}) %collective-permute-start.21) | collective-permute-done | bytes 393248 | tf_op jit(solution)/shard_map/ppermute | solution.py:268
  135.4 0.1 collective-permute-done.17.left1
  135.5 1.8 %collective-permute-done.18.left2 = bf16[3,64,128]{2,1,0:T(8,128)(2,1)S(1)} collective-permute-done((bf16[3,64,128]{2,1,0:T(8,128)(2,1)S(1)}, bf16[3,64,128]{2,1,0:T(8,128)(2,1)S(1)}, u32[]{:S(2)}, u32[]{:S(2)}) %collective-permute-start.18) | collective-permute-done | bytes 49184 | tf_op jit(solution)/shard_map/ppermute | solution.py:275
  137.3 1.4 collective-permute-done.19.left3
  138.8 3.5 %gram_sum.1 = (f32[3,64,1024]{2,1,0:T(8,128)}, f32[3,64,1024]{2,1,0:T(8,128)}) custom-call(s32[2]{0:T(128)S(1)} %pad_add_fusion.here, s32[3]{0:T(128)S(1)} %dynamic_slice.3.used, f32[3,64,256]{2,1,0:T(8,128)S(1)} %get-tuple-element.104.own, f32[3,64,128]{2,1,0:T(8,128)S(1)} %get-tuple-element.105.left0, ...), custom_call_target="tpu_custom_call" | custom-call | bytes 8388608 | tf_op jit(solution)/shard_map/gram_sum/pallas_call | solution.py:280
  142.3 1.2 gather_fusion
  (19 shorter events, 0.1 us)
Async XLA Ops:
  2.9 11.8 %collective-permute-start = (bf16[4,8,6144]{2,1,0:T(8,128)(2,1)S(1)}, bf16[4,8,6144]{2,1,0:T(8,128)(2,1)S(1)}, u32[]{:S(2)}, u32[]{:S(2)}) collective-permute-start(bf16[4,8,6144]{2,1,0:T(8,128)(2,1)S(1)} %get-tuple-element.64), channel_id=1, source_target_pairs={{0,8},{8,16},{16,24},{24,0},{32,40},{40,48},{48,56},{56,32},{64,72... | collective-permute-start | bytes 1179656 | tf_op jit(solution)/shard_map/ppermute | solution.py:268
  5.0 17.9 %collective-permute-start.1 = (bf16[4,8,6144]{2,1,0:T(8,128)(2,1)S(1)}, bf16[4,8,6144]{2,1,0:T(8,128)(2,1)S(1)}, u32[]{:S(2)}, u32[]{:S(2)}) collective-permute-start(bf16[4,8,6144]{2,1,0:T(8,128)(2,1)S(1)} %get-tuple-element.65), channel_id=1, source_target_pairs={{0,32},{8,40},{16,48},{24,56},{32,64},{40,72},{48,80},{56,88},{64,... | collective-permute-start | bytes 1179656 | tf_op jit(solution)/shard_map/ppermute | solution.py:275
  6.3 16.6 %collective-permute-start.2 = (bf16[4,8,6144]{2,1,0:T(8,128)(2,1)S(1)}, bf16[4,8,6144]{2,1,0:T(8,128)(2,1)S(1)}, u32[]{:S(2)}, u32[]{:S(2)}) collective-permute-start(bf16[4,8,6144]{2,1,0:T(8,128)(2,1)S(1)} %get-tuple-element.66), channel_id=1, source_target_pairs={{0,24},{8,0},{16,8},{24,16},{32,56},{40,32},{48,40},{56,48},{64,88... | collective-permute-start | bytes 1179656 | tf_op jit(solution)/shard_map/ppermute | solution.py:268
  7.8 15.1 %collective-permute-start.3 = (bf16[4,8,6144]{2,1,0:T(8,128)(2,1)S(1)}, bf16[4,8,6144]{2,1,0:T(8,128)(2,1)S(1)}, u32[]{:S(2)}, u32[]{:S(2)}) collective-permute-start(bf16[4,8,6144]{2,1,0:T(8,128)(2,1)S(1)} %get-tuple-element.67), channel_id=1, source_target_pairs={{0,96},{8,104},{16,112},{24,120},{32,0},{40,8},{48,16},{56,24},{64... | collective-permute-start | bytes 1179656 | tf_op jit(solution)/shard_map/ppermute | solution.py:275
  9.2 15.2 %collective-permute-start.4 = (bf16[4,8,6144]{2,1,0:T(8,128)(2,1)S(1)}, bf16[4,8,6144]{2,1,0:T(8,128)(2,1)S(1)}, u32[]{:S(2)}, u32[]{:S(2)}) collective-permute-start(bf16[4,8,6144]{2,1,0:T(8,128)(2,1)S(1)} %get-tuple-element.68), channel_id=1, source_target_pairs={{0,16},{8,24},{16,0},{24,8},{32,48},{40,56},{48,32},{56,40},{64,80... | collective-permute-start | bytes 1179656 | tf_op jit(solution)/shard_map/ppermute | solution.py:268
  14.7 26.6 %copy-start.3 = (s32[12]{0:T(128)S(1)}, s32[12]{0:T(128)}, u32[]{:S(2)}) copy-start(s32[12]{0:T(128)} %param.9) | copy-start | bytes 148
  14.7 11.0 %collective-permute-start.5 = (bf16[4,8,6144]{2,1,0:T(8,128)(2,1)S(1)}, bf16[4,8,6144]{2,1,0:T(8,128)(2,1)S(1)}, u32[]{:S(2)}, u32[]{:S(2)}) collective-permute-start(bf16[4,8,6144]{2,1,0:T(8,128)(2,1)S(1)} %get-tuple-element.69), channel_id=1, source_target_pairs={{0,64},{8,72},{16,80},{24,88},{32,96},{40,104},{48,112},{56,120},{... | collective-permute-start | bytes 1179656 | tf_op jit(solution)/shard_map/ppermute | solution.py:275
  25.7 20.7 %all-to-all-start = ((bf16[16,3,64,128]{3,2,1,0:T(8,128)(2,1)}), bf16[16,3,64,128]{3,2,1,0:T(8,128)(2,1)S(1)}, u32[]{:S(2)}, u32[]{:S(2)}) async-start(bf16[16,3,64,128]{3,2,1,0:T(8,128)(2,1)} %moment_right.1), calls=%async_computation | async-start | bytes 1572864 | tf_op jit(solution)/shard_map/all_to_all | solution.py:354
  32.4 7.8 %collective-permute-start.10 = (bf16[8,6144]{1,0:T(8,128)(2,1)S(1)}, bf16[8,6144]{1,0:T(8,128)(2,1)S(1)}, u32[]{:S(2)}, u32[]{:S(2)}) collective-permute-start(bf16[8,6144]{1,0:T(8,128)(2,1)S(1)} %get-tuple-element.82), channel_id=1, source_target_pairs={{0,24},{8,0},{16,8},{24,16},{32,56},{40,32},{48,40},{56,48},{64,88... | collective-permute-start | bytes 294920 | tf_op jit(solution)/shard_map/ppermute | solution.py:268
  35.0 6.4 %collective-permute-start.11 = (bf16[8,6144]{1,0:T(8,128)(2,1)S(1)}, bf16[8,6144]{1,0:T(8,128)(2,1)S(1)}, u32[]{:S(2)}, u32[]{:S(2)}) collective-permute-start(bf16[8,6144]{1,0:T(8,128)(2,1)S(1)} %get-tuple-element.83), channel_id=1, source_target_pairs={{0,16},{8,24},{16,0},{24,8},{32,48},{40,56},{48,32},{56,40},{64,80... | collective-permute-start | bytes 294920 | tf_op jit(solution)/shard_map/ppermute | solution.py:268
  35.6 9.2 %collective-permute-start.6 = (bf16[8,6144]{1,0:T(8,128)(2,1)S(1)}, bf16[8,6144]{1,0:T(8,128)(2,1)S(1)}, u32[]{:S(2)}, u32[]{:S(2)}) collective-permute-start(bf16[8,6144]{1,0:T(8,128)(2,1)S(1)} %get-tuple-element.77), channel_id=1, source_target_pairs={{0,32},{8,40},{16,48},{24,56},{32,64},{40,72},{48,80},{56,88},{64,... | collective-permute-start | bytes 294920 | tf_op jit(solution)/shard_map/ppermute | solution.py:275
  36.8 8.1 %collective-permute-start.7 = (bf16[8,6144]{1,0:T(8,128)(2,1)S(1)}, bf16[8,6144]{1,0:T(8,128)(2,1)S(1)}, u32[]{:S(2)}, u32[]{:S(2)}) collective-permute-start(bf16[8,6144]{1,0:T(8,128)(2,1)S(1)} %get-tuple-element.78), channel_id=1, source_target_pairs={{0,96},{8,104},{16,112},{24,120},{32,0},{40,8},{48,16},{56,24},{64... | collective-permute-start | bytes 294920 | tf_op jit(solution)/shard_map/ppermute | solution.py:275
  38.3 7.5 %collective-permute-start.8 = (bf16[8,6144]{1,0:T(8,128)(2,1)S(1)}, bf16[8,6144]{1,0:T(8,128)(2,1)S(1)}, u32[]{:S(2)}, u32[]{:S(2)}) collective-permute-start(bf16[8,6144]{1,0:T(8,128)(2,1)S(1)} %get-tuple-element.79), channel_id=1, source_target_pairs={{0,64},{8,72},{16,80},{24,88},{32,96},{40,104},{48,112},{56,120},{... | collective-permute-start | bytes 294920 | tf_op jit(solution)/shard_map/ppermute | solution.py:275
  40.1 6.2 %collective-permute-start.9 = (bf16[8,6144]{1,0:T(8,128)(2,1)S(1)}, bf16[8,6144]{1,0:T(8,128)(2,1)S(1)}, u32[]{:S(2)}, u32[]{:S(2)}) collective-permute-start(bf16[8,6144]{1,0:T(8,128)(2,1)S(1)} %get-tuple-element.81), channel_id=1, source_target_pairs={{0,8},{8,16},{16,24},{24,0},{32,40},{40,48},{48,56},{56,32},{64,72... | collective-permute-start | bytes 294920 | tf_op jit(solution)/shard_map/ppermute | solution.py:268
  47.7 18.1 %all-to-all-start.1 = ((bf16[8,3,8,1024]{3,2,1,0:T(8,128)(2,1)}), bf16[8,3,8,1024]{3,2,1,0:T(8,128)(2,1)S(1)}, u32[]{:S(2)}, u32[]{:S(2)}) async-start(bf16[8,3,8,1024]{3,2,1,0:T(8,128)(2,1)} %bitcast.3), calls=%async_computation.1 | async-start | bytes 786432 | tf_op jit(solution)/shard_map/all_to_all | solution.py:354
  65.9 26.6 %copy-start = (bf16[3,64,1024]{2,1,0:T(8,128)(2,1)}, bf16[3,64,1024]{2,1,0:T(8,128)(2,1)S(1)}, u32[]{:S(2)}) copy-start(bf16[3,64,1024]{2,1,0:T(8,128)(2,1)S(1)} %copy_bitcast_fusion.rows) | copy-start | bytes 1179652
  71.9 14.0 %all-to-all-start.2 = ((bf16[16,3,32,128]{3,2,1,0:T(8,128)(2,1)}), bf16[16,3,32,128]{3,2,1,0:T(8,128)(2,1)S(1)}, u32[]{:S(2)}, u32[]{:S(2)}) async-start(bf16[16,3,32,128]{3,2,1,0:T(8,128)(2,1)} %get-tuple-element.97), calls=%async_computation.2 | async-start | bytes 786432 | tf_op jit(solution)/shard_map/all_to_all | solution.py:354
  76.9 15.6 %collective-permute-start.12 = (bf16[3,64,1024]{2,1,0:T(8,128)(2,1)S(1)}, bf16[3,64,1024]{2,1,0:T(8,128)(2,1)S(1)}, u32[]{:S(2)}, u32[]{:S(2)}) collective-permute-start(bf16[3,64,1024]{2,1,0:T(8,128)(2,1)S(1)} %copy_bitcast_fusion.rows), channel_id=1, source_target_pairs={{0,16},{8,24},{16,0},{24,8},{32,48},{40,56},{48,32},{56,40},{64,80... | collective-permute-start | bytes 1179656 | tf_op jit(solution)/shard_map/ppermute | solution.py:268
  79.8 14.6 %collective-permute-start.13 = (bf16[3,64,1024]{2,1,0:T(8,128)(2,1)S(1)}, bf16[3,64,1024]{2,1,0:T(8,128)(2,1)S(1)}, u32[]{:S(2)}, u32[]{:S(2)}) collective-permute-start(bf16[3,64,1024]{2,1,0:T(8,128)(2,1)S(1)} %copy_bitcast_fusion.rows), channel_id=1, source_target_pairs={{0,64},{8,72},{16,80},{24,88},{32,96},{40,104},{48,112},{56,120},{... | collective-permute-start | bytes 1179656 | tf_op jit(solution)/shard_map/ppermute | solution.py:275
  82.4 19.7 %collective-permute-start.14 = (bf16[3,64,1024]{2,1,0:T(8,128)(2,1)S(1)}, bf16[3,64,1024]{2,1,0:T(8,128)(2,1)}, u32[]{:S(2)}, u32[]{:S(2)}) collective-permute-start(bf16[3,64,1024]{2,1,0:T(8,128)(2,1)S(1)} %copy_bitcast_fusion.rows), channel_id=1, source_target_pairs={{0,8},{8,16},{16,24},{24,0},{32,40},{40,48},{48,56},{56,32},{64,72... | collective-permute-start | bytes 1179656 | tf_op jit(solution)/shard_map/ppermute | solution.py:268
  82.7 20.7 %collective-permute-start.15 = (bf16[3,64,1024]{2,1,0:T(8,128)(2,1)S(1)}, bf16[3,64,1024]{2,1,0:T(8,128)(2,1)}, u32[]{:S(2)}, u32[]{:S(2)}) collective-permute-start(bf16[3,64,1024]{2,1,0:T(8,128)(2,1)S(1)} %copy_bitcast_fusion.rows), channel_id=1, source_target_pairs={{0,32},{8,40},{16,48},{24,56},{32,64},{40,72},{48,80},{56,88},{64,... | collective-permute-start | bytes 1179656 | tf_op jit(solution)/shard_map/ppermute | solution.py:275
  83.0 20.4 %collective-permute-start.16 = (bf16[3,64,1024]{2,1,0:T(8,128)(2,1)S(1)}, bf16[3,64,1024]{2,1,0:T(8,128)(2,1)}, u32[]{:S(2)}, u32[]{:S(2)}) collective-permute-start(bf16[3,64,1024]{2,1,0:T(8,128)(2,1)S(1)} %copy_bitcast_fusion.rows), channel_id=1, source_target_pairs={{0,96},{8,104},{16,112},{24,120},{32,0},{40,8},{48,16},{56,24},{64... | collective-permute-start | bytes 1179656 | tf_op jit(solution)/shard_map/ppermute | solution.py:275
  92.5 14.6 %copy-start.1 = (bf16[3,64,1024]{2,1,0:T(8,128)(2,1)}, bf16[3,64,1024]{2,1,0:T(8,128)(2,1)S(1)}, u32[]{:S(2)}) copy-start(bf16[3,64,1024]{2,1,0:T(8,128)(2,1)S(1)} %collective-permute-done.12.x2) | copy-start | bytes 1179652
  94.4 9.1 %copy-start.2 = (bf16[3,64,1024]{2,1,0:T(8,128)(2,1)}, bf16[3,64,1024]{2,1,0:T(8,128)(2,1)S(1)}, u32[]{:S(2)}) copy-start(bf16[3,64,1024]{2,1,0:T(8,128)(2,1)S(1)} %collective-permute-done.13.y2) | copy-start | bytes 1179652
  103.4 17.0 %all-to-all-start.3 = ((bf16[16,3,64,128]{3,2,1,0:T(8,128)(2,1)}), bf16[16,3,64,128]{3,2,1,0:T(8,128)(2,1)S(1)}, u32[]{:S(2)}, u32[]{:S(2)}) async-start(bf16[16,3,64,128]{3,2,1,0:T(8,128)(2,1)} %rotate_left.1), calls=%async_computation.3 | async-start | bytes 1572864 | tf_op jit(solution)/shard_map/all_to_all | solution.py:354
  112.5 20.6 %collective-permute-start.20 = (bf16[3,64,1024]{2,1,0:T(8,128)(2,1)}, bf16[3,64,1024]{2,1,0:T(8,128)(2,1)S(1)}, u32[]{:S(2)}, u32[]{:S(2)}) collective-permute-start(bf16[3,64,1024]{2,1,0:T(8,128)(2,1)} %get-tuple-element.110), channel_id=1, source_target_pairs={{0,8},{8,16},{16,24},{24,0},{32,40},{40,48},{48,56},{56,32},{64,72... | collective-permute-start | bytes 1179656 | tf_op jit(solution)/shard_map/ppermute | solution.py:268
  114.0 21.5 %collective-permute-start.22 = (bf16[3,64,1280]{2,1,0:T(8,128)(2,1)}, bf16[3,64,1280]{2,1,0:T(8,128)(2,1)S(1)}, u32[]{:S(2)}, u32[]{:S(2)}) collective-permute-start(bf16[3,64,1280]{2,1,0:T(8,128)(2,1)} %get-tuple-element.112), channel_id=1, source_target_pairs={{0,24},{8,0},{16,8},{24,16},{32,56},{40,32},{48,40},{56,48},{64,88... | collective-permute-start | bytes 1474568 | tf_op jit(solution)/shard_map/ppermute | solution.py:268
  115.3 20.2 %collective-permute-start.21 = (bf16[3,64,1024]{2,1,0:T(8,128)(2,1)}, bf16[3,64,1024]{2,1,0:T(8,128)(2,1)S(1)}, u32[]{:S(2)}, u32[]{:S(2)}) collective-permute-start(bf16[3,64,1024]{2,1,0:T(8,128)(2,1)} %get-tuple-element.111), channel_id=1, source_target_pairs={{0,16},{8,24},{16,0},{24,8},{32,48},{40,56},{48,32},{56,40},{64,80... | collective-permute-start | bytes 1179656 | tf_op jit(solution)/shard_map/ppermute | solution.py:268
  125.6 16.7 %all-to-all-start.4 = ((bf16[8,3,8,1024]{3,2,1,0:T(8,128)(2,1)}), bf16[8,3,8,1024]{3,2,1,0:T(8,128)(2,1)S(1)}, u32[]{:S(2)}, u32[]{:S(2)}) async-start(bf16[8,3,8,1024]{3,2,1,0:T(8,128)(2,1)} %get-tuple-element.114), calls=%async_computation.4 | async-start | bytes 786432 | tf_op jit(solution)/shard_map/all_to_all | solution.py:354
  132.3 3.2 %collective-permute-start.17 = (bf16[3,64,128]{2,1,0:T(8,128)(2,1)S(1)}, bf16[3,64,128]{2,1,0:T(8,128)(2,1)S(1)}, u32[]{:S(2)}, u32[]{:S(2)}) collective-permute-start(bf16[3,64,128]{2,1,0:T(8,128)(2,1)S(1)} %get-tuple-element.106), channel_id=1, source_target_pairs={{0,96},{8,104},{16,112},{24,120},{32,0},{40,8},{48,16},{56,24},{64... | collective-permute-start | bytes 147464 | tf_op jit(solution)/shard_map/ppermute | solution.py:275
  132.9 4.5 %collective-permute-start.18 = (bf16[3,64,128]{2,1,0:T(8,128)(2,1)S(1)}, bf16[3,64,128]{2,1,0:T(8,128)(2,1)S(1)}, u32[]{:S(2)}, u32[]{:S(2)}) collective-permute-start(bf16[3,64,128]{2,1,0:T(8,128)(2,1)S(1)} %get-tuple-element.107), channel_id=1, source_target_pairs={{0,64},{8,72},{16,80},{24,88},{32,96},{40,104},{48,112},{56,120},{... | collective-permute-start | bytes 147464 | tf_op jit(solution)/shard_map/ppermute | solution.py:275
  133.1 5.6 %collective-permute-start.19 = (bf16[3,64,128]{2,1,0:T(8,128)(2,1)S(1)}, bf16[3,64,128]{2,1,0:T(8,128)(2,1)S(1)}, u32[]{:S(2)}, u32[]{:S(2)}) collective-permute-start(bf16[3,64,128]{2,1,0:T(8,128)(2,1)S(1)} %get-tuple-element.108), channel_id=1, source_target_pairs={{0,32},{8,40},{16,48},{24,56},{32,64},{40,72},{48,80},{56,88},{64,... | collective-permute-start | bytes 147464 | tf_op jit(solution)/shard_map/ppermute | solution.py:275

commit v4 on v3

--- a/solution.py
+++ b/solution.py
@@ -1,3 +1,5 @@
+import functools
+
 import jax
 import jax.numpy as jnp
 from jax import lax
@@ -56,16 +58,35 @@
     return total.astype(BF16)
 
 
-def first_send_kernel(here, grad, a1, b1, a3, b3, a2, b2, sems):
+def cut_for_column(grad, target, sems, y, x, by, split):
+    to_x = turn(x, by)
+    copies = [
+        pltpu.make_async_copy(
+            grad.at[k, to_x, :, pl.ds(0, split)], target.at[:, pl.ds(k * split, split)], sems.at[k]
+        )
+        for k in range(SIDE)
+    ]
+    rest = grad.shape[3] - split
+    copies.append(
+        pltpu.make_async_copy(
+            grad.at[turn(y, 2), to_x, :, pl.ds(split, rest)], target.at[:, pl.ds(SIDE * split, rest)], sems.at[SIDE]
+        )
+    )
+    return copies
+
+
+def cut_for_row(grad, target, sem, y, by, split):
+    rest = grad.shape[3] - split
+    return [pltpu.make_async_copy(grad.at[turn(y, by), :, :, pl.ds(split, rest)], target, sem)]
+
+
+def first_send_kernel(split, here, grad, a1, b1, a3, b3, a2, column_sems, row_sems):
     y, x = here[0], here[1]
-    half = grad.shape[3] // 2
     copies = []
-    for by, a_out, b_out in ((1, a1, b1), (3, a3, b3), (2, a2, b2)):
-        for source, target in (
-            (grad.at[:, turn(x, by), :, pl.ds(0, half)], a_out),
-            (grad.at[turn(y, by), :, :, pl.ds(half, half)], b_out),
-        ):
-            copies.append(pltpu.make_async_copy(source, target, sems.at[len(copies)]))
+    for k, (by, target) in enumerate(((1, a1), (3, a3), (2, a2))):
+        copies += cut_for_column(grad, target, column_sems.at[k], y, x, by, split)
+    for k, (by, target) in enumerate(((1, b1), (3, b3))):
+        copies += cut_for_row(grad, target, row_sems.at[k], y, by, split)
     wait_all(start_all(copies))
 
 
@@ -78,28 +99,33 @@
     )
 
 
-def second_send_kernel(here, grad, a1, b1, a3, b3, a2, b2, p0, p1, p2, p3, q0, q1, q2, q3, a0, b0, sems):
+def second_send_kernel(
+    split, here, grad, a1, b1, a3, b3, a2, p0, p1, p2, p3, q0, q1, q2, q3, own_a, own_b, column_sems, row_sems
+):
     y, x = here[0], here[1]
-    half = grad.shape[3] // 2
-    own = [
-        pltpu.make_async_copy(grad.at[:, x, :, pl.ds(0, half)], a0, sems.at[0]),
-        pltpu.make_async_copy(grad.at[y, :, :, pl.ds(half, half)], b0, sems.at[1]),
-    ]
-    wait_all(start_all(own))
-    for by, (p_out, q_out) in enumerate(((p0, q0), (p1, q1), (p2, q2), (p3, q3))):
-        to_y = turn(y, by)
+    column = start_all(cut_for_column(grad, own_a, column_sems, y, x, 0, split))
+    row = start_all(cut_for_row(grad, own_b, row_sems.at[0], y, 0, split))
+    wait_all(column)
+    for by, out in enumerate((p0, p1, p2, p3)):
+        lanes = pl.ds(pl.multiple_of(turn(y, by) * split, split), split)
+        out[:, :split] = add(own_a[:, lanes], a1[:, lanes], a3[:, lanes], a2[:, lanes])
+    p2[:, split:] = add(*(ref[:, SIDE * split :] for ref in (own_a, a1, a3, a2)))
+    wait_all(row)
+    for by, out in enumerate((q0, q1, q2, q3)):
         to_x = turn(x, by)
-        p_out[...] = add(a0[to_y], a1[to_y], a3[to_y], a2[to_y])
-        q_out[...] = add(b0[to_x], b1[to_x], b3[to_x], b2[to_x])
-
-
-def outgoing_kernel(holder, p0, p1, p2, p3, q0, q1, q2, q3, out, flat):
+        out[...] = add(own_b[to_x], b1[to_x], b3[to_x])
+
+
+def outgoing_kernel(holder, p0, p1, p3, p2, q0, q1, q3, q2, out, flat):
     order = out.shape[2]
-    half_blocks = p0.shape[1] // order
-    for block in range(half_blocks):
+    first_blocks = p0.shape[1] // order
+    for block in range(flat.shape[0]):
         lanes = slice(block * order, (block + 1) * order)
-        flat[block] = add(p0[:, lanes], p1[:, lanes], p2[:, lanes], p3[:, lanes])
-        flat[block + half_blocks] = add(q0[:, lanes], q1[:, lanes], q2[:, lanes], q3[:, lanes])
+        if block < first_blocks:
+            flat[block] = add(p0[:, lanes], p1[:, lanes], p2[:, lanes], p3[:, lanes])
+        else:
+            rest = slice((block - first_blocks) * order, (block - first_blocks + 1) * order)
+            flat[block] = add(q0[:, rest], q1[:, rest], q2[:, rest], q3[:, rest], p2[:, lanes])
     for slot in range(out.shape[0]):
         out[slot] = flat[holder[slot]]
 
@@ -194,7 +220,7 @@
 
 
 def gram_tiles_kernel(
-    here, rows, x2, y2, x1, y1, y3,
+    here, rows, y2, x2, y1, y3, x1,
     own, left0, left1, left2, left3, right0, right1, right2, right3,
     across, down, grams, sems,
 ):
@@ -293,22 +319,29 @@
 
 def sum_replicas(grad, here, holder, slot_total, order, beside, between):
     rows, width = grad.shape[1], grad.shape[2]
-    half = width // 2
+    split = width // order // 6 * order
+    rest = width - split
     grad = grad.reshape(SIDE, SIDE, rows, width)
-    line = (SIDE, rows, half)
+    column, row = (rows, SIDE * split + rest), (SIDE, rows, rest)
     sent = call(
-        first_send_kernel, "first_send", [(here, SMEM), (grad, HBM)], [(line, BF16, VMEM)] * 6,
-        [pltpu.SemaphoreType.DMA((6,))], 0, 5,
-    )
-    got = []
-    for k, by in enumerate((1, 3, 2)):
-        got += [along_x(sent[2 * k], by), along_y(sent[2 * k + 1], by)]
+        functools.partial(first_send_kernel, split), "first_send", [(here, SMEM), (grad, HBM)],
+        [(shape, BF16, VMEM) for shape in (column, row, column, row, column)],
+        [pltpu.SemaphoreType.DMA((3, SIDE + 1)), pltpu.SemaphoreType.DMA((2,))], 0, 5,
+    )
+    got = [along_x(sent[0], 1), along_y(sent[1], 1), along_x(sent[2], 3), along_y(sent[3], 3), along_x(sent[4], 2)]
     got, early = lax.optimization_barrier((got, beside()))
     early = between(early)
+    piece, piece_rest, both = (rows, split), (rows, rest), (rows, width)
     pieces = call(
-        second_send_kernel, "second_send", [(here, SMEM), (grad, HBM)] + [(value, VMEM) for value in got],
-        [((rows, half), BF16, None if by % SIDE == 0 else VMEM) for by in range(2 * SIDE)],
-        [pltpu.VMEM(line, BF16), pltpu.VMEM(line, BF16), pltpu.SemaphoreType.DMA((2,))], 0, 4,
+        functools.partial(second_send_kernel, split), "second_send",
+        [(here, SMEM), (grad, HBM)] + [(value, VMEM) for value in got],
+        [(piece, BF16, None), (piece, BF16, VMEM), (both, BF16, VMEM), (piece, BF16, VMEM), (piece_rest, BF16, None)]
+        + [(piece_rest, BF16, VMEM)] * 3,
+        [
+            pltpu.VMEM(column, BF16), pltpu.VMEM(row, BF16), pltpu.SemaphoreType.DMA((SIDE + 1,)),
+            pltpu.SemaphoreType.DMA((1,)),
+        ],
+        0, 4,
     )
     p, q = [pieces[0]], [pieces[4]]
     for by in (1, 3, 2):
@@ -383,10 +416,7 @@
     )
     rows, packed = lax.optimization_barrier((rows, packed))
     packed = exchange(packed, "dp")
-    near = []
-    for by in (2, 1):
-        near += [along_x(rows, by), along_y(rows, by)]
-    near.append(along_y(rows, 3))
+    near = [along_y(rows, 2), along_x(rows, 2), along_y(rows, 1), along_y(rows, 3), along_x(rows, 1)]
     turned = call(
         rotate_left_kernel, "rotate_left", [(packed, VMEM), (left_basis, HBM), (ready, VMEM)],
         [(chunks, BF16, VMEM)], basis_scratch, 9, 8,
@@ -406,6 +436,8 @@
     )
     lefts = [tiles[1]] + [along_y(tiles[1 + back], SIDE - back) for back in (1, 2, 3)]
     rights = [tiles[1 + SIDE]] + [along_x(tiles[1 + SIDE + by], by) for by in (1, 2, 3)]
+    early_lefts, turned = lax.optimization_barrier((lefts[1:3], turned))
+    lefts = [lefts[0], *early_lefts, lefts[3]]
     new_second, step = call(
         step_kernel, "step_rows", [(used, SMEM), (turned, VMEM), (right_basis, HBM)],
         [(slabs, BF16, None), ((owners, slots, part_rows, order), BF16, VMEM)], basis_scratch, 3, 8,

time: 144 us -> 142 us (0.986)
  starting transfers between devices: 63.9 us -> 59.3 us
  waiting for transfers between devices: 36.4 us -> 38.5 us
    ppermute x12 -> x11, waiting for transfers between devices: 12.1 us -> 24.6 us  [along_y(): return lax.ppermute(value, 'dp', pairs)]
    ppermute x11, waiting for transfers between devices: 15.8 us -> 8.71 us  [along_x(): return lax.ppermute(value, 'dp', pairs)]
    all_to_all x5, waiting for transfers between devices: 8.48 us -> 5.12 us  [exchange(): return lax.all_to_all(value, axis, split_axis=0, concat_axis=0, tiled=True)]
    all_to_all x5, starting transfers between devices: 29.9 us -> 26.9 us  [exchange(): return lax.all_to_all(value, axis, split_axis=0, concat_axis=0, tiled=True)]
    ppermute x12 -> x11, starting transfers between devices: 17 us -> 15.5 us  [along_y(): return lax.ppermute(value, 'dp', pairs)]
  transfers between devices with their start and end apart: 28 -> 27, of which waited for: 17 -> 10; matrix products, arithmetic and copies ran while one was open for 0% -> 0% of each run, Pallas kernels for 22% -> 22%
where the time goes in v4:
time: 142 us; the launch traced here: 141 us
  starting transfers between devices  59.3 us (42%)
  Pallas kernels  41 us (29%)
  waiting for transfers between devices  38.5 us (27%)
    pallas_call x10, Pallas kernels, call(): pl.pallas_call(kernel, in_specs=[pl.BlockSpec(memory_space=space) for _,...  41 us
    all_to_all x5, starting transfers between devices, exchange(): return lax.all_to_all(value, axis, split_axis=0, concat_axis=0, tiled=True)  26.9 us
    ppermute x11, waiting for transfers between devices, along_y(): return lax.ppermute(value, 'dp', pairs)  24.6 us
    ppermute x11, starting transfers between devices, along_x(): return lax.ppermute(value, 'dp', pairs)  16.9 us
    ppermute x11, starting transfers between devices, along_y(): return lax.ppermute(value, 'dp', pairs)  15.5 us
    ppermute x11, waiting for transfers between devices, along_x(): return lax.ppermute(value, 'dp', pairs)  8.71 us
    all_to_all x5, waiting for transfers between devices, exchange(): return lax.all_to_all(value, axis, split_axis=0, concat_axis=0, tiled=True)  5.12 us
  transfers between devices with their start and end apart: 27, of which 10 were waited for; matrix products, arithmetic and copies ran while one was open for 0% of the time, Pallas kernels for 22%

profile of v4, /device:TPU:1, one launch (start us, length us, event | category | flops | bytes accessed | tf_op | source)
XLA Modules:
  0.0 141.2 jit_solution(2109998347642852380)
XLA Ops:
  0.7 0.1 pad_add_fusion.here
  0.7 2.4 %first_send.1 = (bf16[8,18432]{1,0:T(8,128)(2,1)S(1)}, bf16[4,8,10240]{2,1,0:T(8,128)(2,1)S(1)}, bf16[8,18432]{1,0:T(8,128)(2,1)S(1)}, bf16[4,8,10240]{2,1,0:T(8,128)(2,1)S(1)}, bf16[8,18432]{1,0:T(8,128)(2,1)S(1)}) custom-call(s32[2]{0:T(128)S(1)} %pad_add_fusion.here, bf16[4,4,8,12288]{3,2,1,0:T(8,128)(2,1)} %bitcast.13), custom_call_target="tpu_custom_call" | custom-call | bytes 5242880 | tf_op jit(solution)/shard_map/first_send/pallas_call | solution.py:306
  3.1 2.2 %collective-permute-start.1 = (bf16[4,8,10240]{2,1,0:T(8,128)(2,1)S(1)}, bf16[4,8,10240]{2,1,0:T(8,128)(2,1)S(1)}, u32[]{:S(2)}, u32[]{:S(2)}) collective-permute-start(bf16[4,8,10240]{2,1,0:T(8,128)(2,1)S(1)} %get-tuple-element.66), channel_id=1, source_target_pairs={{0,32},{8,40},{16,48},{24,56},{32,64},{40,72},{48,80},{56,88},{64,... | collective-permute-start | bytes 1966088 | tf_op jit(solution)/shard_map/ppermute | solution.py:301
  5.3 1.5 %collective-permute-start.3 = (bf16[4,8,10240]{2,1,0:T(8,128)(2,1)S(1)}, bf16[4,8,10240]{2,1,0:T(8,128)(2,1)S(1)}, u32[]{:S(2)}, u32[]{:S(2)}) collective-permute-start(bf16[4,8,10240]{2,1,0:T(8,128)(2,1)S(1)} %get-tuple-element.68), channel_id=1, source_target_pairs={{0,96},{8,104},{16,112},{24,120},{32,0},{40,8},{48,16},{56,24},{64... | collective-permute-start | bytes 1966088 | tf_op jit(solution)/shard_map/ppermute | solution.py:301
  6.8 1.2 collective-permute-start
  8.0 1.5 %collective-permute-start.2 = (bf16[8,18432]{1,0:T(8,128)(2,1)S(1)}, bf16[8,18432]{1,0:T(8,128)(2,1)S(1)}, u32[]{:S(2)}, u32[]{:S(2)}) collective-permute-start(bf16[8,18432]{1,0:T(8,128)(2,1)S(1)} %get-tuple-element.67), channel_id=1, source_target_pairs={{0,24},{8,0},{16,8},{24,16},{32,56},{40,32},{48,40},{56,48},{64,88... | collective-permute-start | bytes 884744 | tf_op jit(solution)/shard_map/ppermute | solution.py:294
  9.5 1.5 %collective-permute-start.4 = (bf16[8,18432]{1,0:T(8,128)(2,1)S(1)}, bf16[8,18432]{1,0:T(8,128)(2,1)S(1)}, u32[]{:S(2)}, u32[]{:S(2)}) collective-permute-start(bf16[8,18432]{1,0:T(8,128)(2,1)S(1)} %get-tuple-element.69), channel_id=1, source_target_pairs={{0,16},{8,24},{16,0},{24,8},{32,48},{40,56},{48,32},{56,40},{64,80... | collective-permute-start | bytes 884744 | tf_op jit(solution)/shard_map/ppermute | solution.py:294
  11.0 5.0 %moment_right.1 = bf16[16,3,64,128]{3,2,1,0:T(8,128)(2,1)} custom-call(bf16[3,64,1024]{2,1,0:T(8,128)(2,1)} %moment_hbm.3, bf16[3,64,1024]{2,1,0:T(8,128)(2,1)} %second_hbm.1, bf16[3,1024,1024]{2,1,0:T(8,128)(2,1)} %basis_hbm.9), custom_call_target="tpu_custom_call" | custom-call | flops 402653184 | bytes 8388608 | tf_op jit(solution)/shard_map/moment_right/pallas_call | solution.py:306
  16.0 0.0 collective-permute-done.a1
  16.0 0.0 collective-permute-done.2.a3
  16.0 6.7 %collective-permute-done.4.a2 = bf16[8,18432]{1,0:T(8,128)(2,1)S(1)} collective-permute-done((bf16[8,18432]{1,0:T(8,128)(2,1)S(1)}, bf16[8,18432]{1,0:T(8,128)(2,1)S(1)}, u32[]{:S(2)}, u32[]{:S(2)}) %collective-permute-start.4) | collective-permute-done | bytes 294944 | tf_op jit(solution)/shard_map/ppermute | solution.py:294
  22.7 0.0 collective-permute-done.1.b1
  22.8 0.0 collective-permute-done.3.b3
  22.8 4.6 %all-to-all-start = ((bf16[16,3,64,128]{3,2,1,0:T(8,128)(2,1)}), bf16[16,3,64,128]{3,2,1,0:T(8,128)(2,1)S(1)}, u32[]{:S(2)}, u32[]{:S(2)}) async-start(bf16[16,3,64,128]{3,2,1,0:T(8,128)(2,1)} %moment_right.1), calls=%async_computation | async-start | bytes 1572864 | tf_op jit(solution)/shard_map/all_to_all | solution.py:387
  27.3 2.1 %second_send.1 = (bf16[8,2048]{1,0:T(8,128)(2,1)S(1)}, bf16[8,2048]{1,0:T(8,128)(2,1)S(1)}, bf16[8,12288]{1,0:T(8,128)(2,1)S(1)}, bf16[8,2048]{1,0:T(8,128)(2,1)...) custom-call(s32[2]{0:T(128)S(1)} %pad_add_fusion.here, ...), custom_call_target="tpu_custom_call" | custom-call | bytes 4194304 | tf_op jit(solution)/shard_map/second_send/pallas_call | solution.py:306
  29.4 2.9 %collective-permute-start.7 = (bf16[8,12288]{1,0:T(8,128)(2,1)S(1)}, bf16[8,12288]{1,0:T(8,128)(2,1)S(1)}, u32[]{:S(2)}, u32[]{:S(2)}) collective-permute-start(bf16[8,12288]{1,0:T(8,128)(2,1)S(1)} %get-tuple-element.78), channel_id=1, source_target_pairs={{0,64},{8,72},{16,80},{24,88},{32,96},{40,104},{48,112},{56,120},{... | collective-permute-start | bytes 589832 | tf_op jit(solution)/shard_map/ppermute | solution.py:301
  32.4 2.7 %collective-permute-start.10 = (bf16[8,10240]{1,0:T(8,128)(2,1)S(1)}, bf16[8,10240]{1,0:T(8,128)(2,1)S(1)}, u32[]{:S(2)}, u32[]{:S(2)}) collective-permute-start(bf16[8,10240]{1,0:T(8,128)(2,1)S(1)} %get-tuple-element.82), channel_id=1, source_target_pairs={{0,16},{8,24},{16,0},{24,8},{32,48},{40,56},{48,32},{56,40},{64,80... | collective-permute-start | bytes 491528 | tf_op jit(solution)/shard_map/ppermute | solution.py:294
  35.1 0.3 collective-permute-start.8
  35.3 2.4 %collective-permute-start.9 = (bf16[8,10240]{1,0:T(8,128)(2,1)S(1)}, bf16[8,10240]{1,0:T(8,128)(2,1)S(1)}, u32[]{:S(2)}, u32[]{:S(2)}) collective-permute-start(bf16[8,10240]{1,0:T(8,128)(2,1)S(1)} %get-tuple-element.81), channel_id=1, source_target_pairs={{0,24},{8,0},{16,8},{24,16},{32,56},{40,32},{48,40},{56,48},{64,88... | collective-permute-start | bytes 491528 | tf_op jit(solution)/shard_map/ppermute | solution.py:294
  37.7 0.3 collective-permute-start.5
  38.0 7.1 %collective-permute-done.5.p1 = bf16[8,2048]{1,0:T(8,128)(2,1)S(1)} collective-permute-done((bf16[8,2048]{1,0:T(8,128)(2,1)S(1)}, bf16[8,2048]{1,0:T(8,128)(2,1)S(1)}, u32[]{:S(2)}, u32[]{:S(2)}) %collective-permute-start.5) | collective-permute-done | bytes 32800 | tf_op jit(solution)/shard_map/ppermute | solution.py:301
  45.1 0.0 collective-permute-start.6
  45.1 0.1 select_reduce_fusion.holder
  45.2 2.7 %collective-permute-done.6.p3 = bf16[8,2048]{1,0:T(8,128)(2,1)S(1)} collective-permute-done((bf16[8,2048]{1,0:T(8,128)(2,1)S(1)}, bf16[8,2048]{1,0:T(8,128)(2,1)S(1)}, u32[]{:S(2)}, u32[]{:S(2)}) %collective-permute-start.6) | collective-permute-done | bytes 32800 | tf_op jit(solution)/shard_map/ppermute | solution.py:301
  47.9 0.0 collective-permute-done.10.q2
  47.9 0.0 collective-permute-done.8.q1
  47.9 0.0 collective-permute-done.9.q3
  47.9 0.0 collective-permute-done.7.p2
  47.9 0.0 all-to-all-done.packed
  47.9 1.4 %outgoing.1 = bf16[24,8,1024]{2,1,0:T(8,128)(2,1)} custom-call(s32[24]{0:T(128)S(1)} %select_reduce_fusion.holder, bf16[8,2048]{1,0:T(8,128)(2,1)S(1)} %get-tuple-element.84.p0, bf16[8,2048]{1,0:T(8,128)(2,1)S(1)} %collective-permute-done.5.p1, bf16[8,2048]{1,0:T(8,128)(2,1)S(1)} %collective-permute-done.6.p3, ...), custom_call_target="tpu_custom_call" | custom-call | bytes 1048576 | tf_op jit(solution)/shard_map/outgoing/pallas_call | solution.py:306
  49.3 7.7 %all-to-all-start.1 = ((bf16[8,3,8,1024]{3,2,1,0:T(8,128)(2,1)}), bf16[8,3,8,1024]{3,2,1,0:T(8,128)(2,1)S(1)}, u32[]{:S(2)}, u32[]{:S(2)}) async-start(bf16[8,3,8,1024]{3,2,1,0:T(8,128)(2,1)} %bitcast.3), calls=%async_computation.1 | async-start | bytes 786432 | tf_op jit(solution)/shard_map/all_to_all | solution.py:387
  57.1 0.1 fusion
  57.2 0.1 dynamic_slice.3.used
  57.3 3.4 %moment_left.1.ready = f32[3,128,1024]{2,1,0:T(8,128)S(1)} custom-call(bf16[16,3,64,128]{3,2,1,0:T(8,128)(2,1)S(1)} %all-to-all-done.packed, bf16[3,1024,1024]{2,1,0:T(8,128)(2,1)} %basis_hbm.8), custom_call_target="tpu_custom_call" | custom-call | flops 402653184 | bytes 8388608 | tf_op jit(solution)/shard_map/moment_left/pallas_call | solution.py:306
  60.7 4.5 %all-to-all-done.1 = bf16[8,3,8,1024]{3,2,1,0:T(8,128)(2,1)S(1)} async-done(((bf16[8,3,8,1024]{3,2,1,0:T(8,128)(2,1)}), bf16[8,3,8,1024]{3,2,1,0:T(8,128)(2,1)S(1)}, u32[]{:S(2)}, u32[]{:S(2)}) %all-to-all-start.1) | async-done | bytes 393248 | tf_op jit(solution)/shard_map/all_to_all | solution.py:387
  65.2 0.0 copy-start
  65.2 6.0 %rotate_right.1 = (bf16[3,64,1024]{2,1,0:T(8,128)(2,1)}, bf16[16,3,32,128]{3,2,1,0:T(8,128)(2,1)}) custom-call(s32[3]{0:T(128)S(1)} %dynamic_slice.3.used, bf16[3,64,1024]{2,1,0:T(8,128)(2,1)S(1)} %copy_bitcast_fusion.rows, bf16[3,64,1024]{2,1,0:T(8,128)(2,1)} %moment_hbm.3, bf16[3,1024,1024]{2,1,0:T(8,128)(2,1)} %basis_hbm.9), custom_call_target="tpu_custom_call" | custom-call | flops 402653184 | bytes 8388608 | tf_op jit(solution)/shard_map/rotate_right/pallas_call | solution.py:306
  71.2 4.3 %all-to-all-start.2 = ((bf16[16,3,32,128]{3,2,1,0:T(8,128)(2,1)}), bf16[16,3,32,128]{3,2,1,0:T(8,128)(2,1)S(1)}, u32[]{:S(2)}, u32[]{:S(2)}) async-start(bf16[16,3,32,128]{3,2,1,0:T(8,128)(2,1)} %get-tuple-element.96), calls=%async_computation.2 | async-start | bytes 786432 | tf_op jit(solution)/shard_map/all_to_all | solution.py:387
  75.5 2.9 %collective-permute-start.11 = (bf16[3,64,1024]{2,1,0:T(8,128)(2,1)S(1)}, bf16[3,64,1024]{2,1,0:T(8,128)(2,1)S(1)}, u32[]{:S(2)}, u32[]{:S(2)}) collective-permute-start(bf16[3,64,1024]{2,1,0:T(8,128)(2,1)S(1)} %copy_bitcast_fusion.rows), channel_id=1, source_target_pairs={{0,64},{8,72},{16,80},{24,88},{32,96},{40,104},{48,112},{56,120},{... | collective-permute-start | bytes 1179656 | tf_op jit(solution)/shard_map/ppermute | solution.py:301
  78.4 2.7 %collective-permute-start.12 = (bf16[3,64,1024]{2,1,0:T(8,128)(2,1)S(1)}, bf16[3,64,1024]{2,1,0:T(8,128)(2,1)S(1)}, u32[]{:S(2)}, u32[]{:S(2)}) collective-permute-start(bf16[3,64,1024]{2,1,0:T(8,128)(2,1)S(1)} %copy_bitcast_fusion.rows), channel_id=1, source_target_pairs={{0,16},{8,24},{16,0},{24,8},{32,48},{40,56},{48,32},{56,40},{64,80... | collective-permute-start | bytes 1179656 | tf_op jit(solution)/shard_map/ppermute | solution.py:294
  81.1 0.3 collective-permute-start.13
  81.4 2.4 %collective-permute-start.14 = (bf16[3,64,1024]{2,1,0:T(8,128)(2,1)S(1)}, bf16[3,64,1024]{2,1,0:T(8,128)(2,1)}, u32[]{:S(2)}, u32[]{:S(2)}) collective-permute-start(bf16[3,64,1024]{2,1,0:T(8,128)(2,1)S(1)} %copy_bitcast_fusion.rows), channel_id=1, source_target_pairs={{0,96},{8,104},{16,112},{24,120},{32,0},{40,8},{48,16},{56,24},{64... | collective-permute-start | bytes 1179656 | tf_op jit(solution)/shard_map/ppermute | solution.py:301
  83.8 0.3 collective-permute-start.15
  84.1 0.5 all-to-all-done.2.packed
  84.6 6.5 %rotate_left.1 = bf16[16,3,64,128]{3,2,1,0:T(8,128)(2,1)} custom-call(bf16[16,3,32,128]{3,2,1,0:T(8,128)(2,1)S(1)} %all-to-all-done.2.packed, bf16[3,1024,1024]{2,1,0:T(8,128)(2,1)} %basis_hbm.8, f32[3,128,1024]{2,1,0:T(8,128)S(1)} %moment_left.1.ready), custom_call_target="tpu_custom_call" | custom-call | flops 1207959552 | bytes 8388608 | tf_op jit(solution)/shard_map/rotate_left/pallas_call | solution.py:306
  91.1 0.0 collective-permute-done.12.x2
  91.2 9.8 %collective-permute-done.13.y1 = bf16[3,64,1024]{2,1,0:T(8,128)(2,1)} collective-permute-done((bf16[3,64,1024]{2,1,0:T(8,128)(2,1)S(1)}, bf16[3,64,1024]{2,1,0:T(8,128)(2,1)}, u32[]{:S(2)}, u32[]{:S(2)}) %collective-permute-start.13) | collective-permute-done | bytes 393248 | tf_op jit(solution)/shard_map/ppermute | solution.py:301
  101.0 0.0 collective-permute-done.14.y3
  101.0 0.0 collective-permute-done.15.x1
  101.0 4.4 %all-to-all-start.3 = ((bf16[16,3,64,128]{3,2,1,0:T(8,128)(2,1)}), bf16[16,3,64,128]{3,2,1,0:T(8,128)(2,1)S(1)}, u32[]{:S(2)}, u32[]{:S(2)}) async-start(bf16[16,3,64,128]{3,2,1,0:T(8,128)(2,1)} %rotate_left.1), calls=%async_computation.3 | async-start | bytes 1572864 | tf_op jit(solution)/shard_map/all_to_all | solution.py:387
  105.4 5.4 %gram_tiles.1 = (f32[3,64,256]{2,1,0:T(8,128)S(1)}, f32[3,64,128]{2,1,0:T(8,128)S(1)}, bf16[3,64,128]{2,1,0:T(8,128)(2,1)S(1)}, bf16[3,64,128]{2,1,0:T(8,128)(2,...) custom-call(s32[2]{0:T(128)S(1)} %pad_add_fusion.here, ...), custom_call_target="tpu_custom_call" | custom-call | flops 1207959552 | bytes 6291456 | tf_op jit(solution)/shard_map/gram_tiles/pallas_call | solution.py:306
  110.8 2.6 %collective-permute-start.21 = (bf16[3,64,1280]{2,1,0:T(8,128)(2,1)}, bf16[3,64,1280]{2,1,0:T(8,128)(2,1)S(1)}, u32[]{:S(2)}, u32[]{:S(2)}) collective-permute-start(bf16[3,64,1280]{2,1,0:T(8,128)(2,1)} %get-tuple-element.114), channel_id=1, source_target_pairs={{0,24},{8,0},{16,8},{24,16},{32,56},{40,32},{48,40},{56,48},{64,88... | collective-permute-start | bytes 1474568 | tf_op jit(solution)/shard_map/ppermute | solution.py:294
  113.5 2.4 %collective-permute-start.16 = (bf16[3,64,128]{2,1,0:T(8,128)(2,1)S(1)}, bf16[3,64,128]{2,1,0:T(8,128)(2,1)S(1)}, u32[]{:S(2)}, u32[]{:S(2)}) collective-permute-start(bf16[3,64,128]{2,1,0:T(8,128)(2,1)S(1)} %get-tuple-element.105), channel_id=1, source_target_pairs={{0,96},{8,104},{16,112},{24,120},{32,0},{40,8},{48,16},{56,24},{64... | collective-permute-start | bytes 147464 | tf_op jit(solution)/shard_map/ppermute | solution.py:301
  115.9 0.6 collective-permute-start.17
  116.5 1.8 %collective-permute-start.20 = (bf16[3,64,1024]{2,1,0:T(8,128)(2,1)}, bf16[3,64,1024]{2,1,0:T(8,128)(2,1)S(1)}, u32[]{:S(2)}, u32[]{:S(2)}) collective-permute-start(bf16[3,64,1024]{2,1,0:T(8,128)(2,1)} %get-tuple-element.113), channel_id=1, source_target_pairs={{0,16},{8,24},{16,0},{24,8},{32,48},{40,56},{48,32},{56,40},{64,80... | collective-permute-start | bytes 1179656 | tf_op jit(solution)/shard_map/ppermute | solution.py:294
  118.2 2.6 %collective-permute-done.17.left2 = bf16[3,64,128]{2,1,0:T(8,128)(2,1)S(1)} collective-permute-done((bf16[3,64,128]{2,1,0:T(8,128)(2,1)S(1)}, bf16[3,64,128]{2,1,0:T(8,128)(2,1)S(1)}, u32[]{:S(2)}, u32[]{:S(2)}) %collective-permute-start.17) | collective-permute-done | bytes 49184 | tf_op jit(solution)/shard_map/ppermute | solution.py:301
  120.8 5.2 %step_rows.1 = (bf16[3,64,1024]{2,1,0:T(8,128)(2,1)}, bf16[8,3,8,1024]{3,2,1,0:T(8,128)(2,1)}) custom-call(s32[3]{0:T(128)S(1)} %dynamic_slice.3.used, bf16[16,3,64,128]{3,2,1,0:T(8,128)(2,1)S(1)} %all-to-all-done.3.packed, bf16[3,1024,1024]{2,1,0:T(8,128)(2,1)} %basis_hbm.9), custom_call_target="tpu_custom_call" | custom-call | flops 402653184 | bytes 8388608 | tf_op jit(solution)/shard_map/step_rows/pallas_call | solution.py:306
  126.1 5.8 %all-to-all-start.4 = ((bf16[8,3,8,1024]{3,2,1,0:T(8,128)(2,1)}), bf16[8,3,8,1024]{3,2,1,0:T(8,128)(2,1)S(1)}, u32[]{:S(2)}, u32[]{:S(2)}) async-start(bf16[8,3,8,1024]{3,2,1,0:T(8,128)(2,1)} %get-tuple-element.116), calls=%async_computation.4 | async-start | bytes 786432 | tf_op jit(solution)/shard_map/all_to_all | solution.py:387
  131.9 0.0 collective-permute-start.18
  131.9 2.0 %collective-permute-done.20.right2 = bf16[3,64,1024]{2,1,0:T(8,128)(2,1)S(1)} collective-permute-done((bf16[3,64,1024]{2,1,0:T(8,128)(2,1)}, bf16[3,64,1024]{2,1,0:T(8,128)(2,1)S(1)}, u32[]{:S(2)}, u32[]{:S(2)}) %collective-permute-start.20) | collective-permute-done | bytes 393248 | tf_op jit(solution)/shard_map/ppermute | solution.py:294
  133.9 2.4 %collective-permute-done.18.left3 = bf16[3,64,128]{2,1,0:T(8,128)(2,1)S(1)} collective-permute-done((bf16[3,64,128]{2,1,0:T(8,128)(2,1)S(1)}, bf16[3,64,128]{2,1,0:T(8,128)(2,1)S(1)}, u32[]{:S(2)}, u32[]{:S(2)}) %collective-permute-start.18) | collective-permute-done | bytes 49184 | tf_op jit(solution)/shard_map/ppermute | solution.py:301
  136.4 3.5 %gram_sum.1 = (f32[3,64,1024]{2,1,0:T(8,128)}, f32[3,64,1024]{2,1,0:T(8,128)}) custom-call(s32[2]{0:T(128)S(1)} %pad_add_fusion.here, s32[3]{0:T(128)S(1)} %dynamic_slice.3.used, f32[3,64,256]{2,1,0:T(8,128)S(1)} %get-tuple-element.103.own, f32[3,64,128]{2,1,0:T(8,128)S(1)} %get-tuple-element.104.left0, ...), custom_call_target="tpu_custom_call" | custom-call | bytes 8388608 | tf_op jit(solution)/shard_map/gram_sum/pallas_call | solution.py:306
  139.9 0.1 all-to-all-done.4
  140.0 1.2 gather_fusion
  (17 shorter events, 0.1 us)
Async XLA Ops:
  3.1 19.6 %collective-permute-start.1 = (bf16[4,8,10240]{2,1,0:T(8,128)(2,1)S(1)}, bf16[4,8,10240]{2,1,0:T(8,128)(2,1)S(1)}, u32[]{:S(2)}, u32[]{:S(2)}) collective-permute-start(bf16[4,8,10240]{2,1,0:T(8,128)(2,1)S(1)} %get-tuple-element.66), channel_id=1, source_target_pairs={{0,32},{8,40},{16,48},{24,56},{32,64},{40,72},{48,80},{56,88},{64,... | collective-permute-start | bytes 1966088 | tf_op jit(solution)/shard_map/ppermute | solution.py:301
  5.3 17.4 %collective-permute-start.3 = (bf16[4,8,10240]{2,1,0:T(8,128)(2,1)S(1)}, bf16[4,8,10240]{2,1,0:T(8,128)(2,1)S(1)}, u32[]{:S(2)}, u32[]{:S(2)}) collective-permute-start(bf16[4,8,10240]{2,1,0:T(8,128)(2,1)S(1)} %get-tuple-element.68), channel_id=1, source_target_pairs={{0,96},{8,104},{16,112},{24,120},{32,0},{40,8},{48,16},{56,24},{64... | collective-permute-start | bytes 1966088 | tf_op jit(solution)/shard_map/ppermute | solution.py:301
  6.8 9.2 %collective-permute-start = (bf16[8,18432]{1,0:T(8,128)(2,1)S(1)}, bf16[8,18432]{1,0:T(8,128)(2,1)S(1)}, u32[]{:S(2)}, u32[]{:S(2)}) collective-permute-start(bf16[8,18432]{1,0:T(8,128)(2,1)S(1)} %get-tuple-element.65), channel_id=1, source_target_pairs={{0,8},{8,16},{16,24},{24,0},{32,40},{40,48},{48,56},{56,32},{64,72... | collective-permute-start | bytes 884744 | tf_op jit(solution)/shard_map/ppermute | solution.py:294
  8.0 8.0 %collective-permute-start.2 = (bf16[8,18432]{1,0:T(8,128)(2,1)S(1)}, bf16[8,18432]{1,0:T(8,128)(2,1)S(1)}, u32[]{:S(2)}, u32[]{:S(2)}) collective-permute-start(bf16[8,18432]{1,0:T(8,128)(2,1)S(1)} %get-tuple-element.67), channel_id=1, source_target_pairs={{0,24},{8,0},{16,8},{24,16},{32,56},{40,32},{48,40},{56,48},{64,88... | collective-permute-start | bytes 884744 | tf_op jit(solution)/shard_map/ppermute | solution.py:294
  9.5 35.6 %copy-start.3 = (s32[12]{0:T(128)S(1)}, s32[12]{0:T(128)}, u32[]{:S(2)}) copy-start(s32[12]{0:T(128)} %param.9) | copy-start | bytes 148
  9.5 13.2 %collective-permute-start.4 = (bf16[8,18432]{1,0:T(8,128)(2,1)S(1)}, bf16[8,18432]{1,0:T(8,128)(2,1)S(1)}, u32[]{:S(2)}, u32[]{:S(2)}) collective-permute-start(bf16[8,18432]{1,0:T(8,128)(2,1)S(1)} %get-tuple-element.69), channel_id=1, source_target_pairs={{0,16},{8,24},{16,0},{24,8},{32,48},{40,56},{48,32},{56,40},{64,80... | collective-permute-start | bytes 884744 | tf_op jit(solution)/shard_map/ppermute | solution.py:294
  22.8 25.1 %all-to-all-start = ((bf16[16,3,64,128]{3,2,1,0:T(8,128)(2,1)}), bf16[16,3,64,128]{3,2,1,0:T(8,128)(2,1)S(1)}, u32[]{:S(2)}, u32[]{:S(2)}) async-start(bf16[16,3,64,128]{3,2,1,0:T(8,128)(2,1)} %moment_right.1), calls=%async_computation | async-start | bytes 1572864 | tf_op jit(solution)/shard_map/all_to_all | solution.py:387
  29.4 18.5 %collective-permute-start.7 = (bf16[8,12288]{1,0:T(8,128)(2,1)S(1)}, bf16[8,12288]{1,0:T(8,128)(2,1)S(1)}, u32[]{:S(2)}, u32[]{:S(2)}) collective-permute-start(bf16[8,12288]{1,0:T(8,128)(2,1)S(1)} %get-tuple-element.78), channel_id=1, source_target_pairs={{0,64},{8,72},{16,80},{24,88},{32,96},{40,104},{48,112},{56,120},{... | collective-permute-start | bytes 589832 | tf_op jit(solution)/shard_map/ppermute | solution.py:301
  32.4 15.5 %collective-permute-start.10 = (bf16[8,10240]{1,0:T(8,128)(2,1)S(1)}, bf16[8,10240]{1,0:T(8,128)(2,1)S(1)}, u32[]{:S(2)}, u32[]{:S(2)}) collective-permute-start(bf16[8,10240]{1,0:T(8,128)(2,1)S(1)} %get-tuple-element.82), channel_id=1, source_target_pairs={{0,16},{8,24},{16,0},{24,8},{32,48},{40,56},{48,32},{56,40},{64,80... | collective-permute-start | bytes 491528 | tf_op jit(solution)/shard_map/ppermute | solution.py:294
  35.1 12.8 %collective-permute-start.8 = (bf16[8,10240]{1,0:T(8,128)(2,1)S(1)}, bf16[8,10240]{1,0:T(8,128)(2,1)S(1)}, u32[]{:S(2)}, u32[]{:S(2)}) collective-permute-start(bf16[8,10240]{1,0:T(8,128)(2,1)S(1)} %get-tuple-element.80), channel_id=1, source_target_pairs={{0,8},{8,16},{16,24},{24,0},{32,40},{40,48},{48,56},{56,32},{64,72... | collective-permute-start | bytes 491528 | tf_op jit(solution)/shard_map/ppermute | solution.py:294
  35.3 12.5 %collective-permute-start.9 = (bf16[8,10240]{1,0:T(8,128)(2,1)S(1)}, bf16[8,10240]{1,0:T(8,128)(2,1)S(1)}, u32[]{:S(2)}, u32[]{:S(2)}) collective-permute-start(bf16[8,10240]{1,0:T(8,128)(2,1)S(1)} %get-tuple-element.81), channel_id=1, source_target_pairs={{0,24},{8,0},{16,8},{24,16},{32,56},{40,32},{48,40},{56,48},{64,88... | collective-permute-start | bytes 491528 | tf_op jit(solution)/shard_map/ppermute | solution.py:294
  37.7 7.4 %collective-permute-start.5 = (bf16[8,2048]{1,0:T(8,128)(2,1)S(1)}, bf16[8,2048]{1,0:T(8,128)(2,1)S(1)}, u32[]{:S(2)}, u32[]{:S(2)}) collective-permute-start(bf16[8,2048]{1,0:T(8,128)(2,1)S(1)} %get-tuple-element.76), channel_id=1, source_target_pairs={{0,32},{8,40},{16,48},{24,56},{32,64},{40,72},{48,80},{56,88},{64,... | collective-permute-start | bytes 98312 | tf_op jit(solution)/shard_map/ppermute | solution.py:301
  45.1 2.8 %collective-permute-start.6 = (bf16[8,2048]{1,0:T(8,128)(2,1)S(1)}, bf16[8,2048]{1,0:T(8,128)(2,1)S(1)}, u32[]{:S(2)}, u32[]{:S(2)}) collective-permute-start(bf16[8,2048]{1,0:T(8,128)(2,1)S(1)} %get-tuple-element.77), channel_id=1, source_target_pairs={{0,96},{8,104},{16,112},{24,120},{32,0},{40,8},{48,16},{56,24},{64... | collective-permute-start | bytes 98312 | tf_op jit(solution)/shard_map/ppermute | solution.py:301
  49.3 15.8 %all-to-all-start.1 = ((bf16[8,3,8,1024]{3,2,1,0:T(8,128)(2,1)}), bf16[8,3,8,1024]{3,2,1,0:T(8,128)(2,1)S(1)}, u32[]{:S(2)}, u32[]{:S(2)}) async-start(bf16[8,3,8,1024]{3,2,1,0:T(8,128)(2,1)} %bitcast.3), calls=%async_computation.1 | async-start | bytes 786432 | tf_op jit(solution)/shard_map/all_to_all | solution.py:387
  65.2 25.9 %copy-start = (bf16[3,64,1024]{2,1,0:T(8,128)(2,1)}, bf16[3,64,1024]{2,1,0:T(8,128)(2,1)S(1)}, u32[]{:S(2)}) copy-start(bf16[3,64,1024]{2,1,0:T(8,128)(2,1)S(1)} %copy_bitcast_fusion.rows) | copy-start | bytes 1179652
  71.2 13.3 %all-to-all-start.2 = ((bf16[16,3,32,128]{3,2,1,0:T(8,128)(2,1)}), bf16[16,3,32,128]{3,2,1,0:T(8,128)(2,1)S(1)}, u32[]{:S(2)}, u32[]{:S(2)}) async-start(bf16[16,3,32,128]{3,2,1,0:T(8,128)(2,1)} %get-tuple-element.96), calls=%async_computation.2 | async-start | bytes 786432 | tf_op jit(solution)/shard_map/all_to_all | solution.py:387
  75.5 15.6 %collective-permute-start.11 = (bf16[3,64,1024]{2,1,0:T(8,128)(2,1)S(1)}, bf16[3,64,1024]{2,1,0:T(8,128)(2,1)S(1)}, u32[]{:S(2)}, u32[]{:S(2)}) collective-permute-start(bf16[3,64,1024]{2,1,0:T(8,128)(2,1)S(1)} %copy_bitcast_fusion.rows), channel_id=1, source_target_pairs={{0,64},{8,72},{16,80},{24,88},{32,96},{40,104},{48,112},{56,120},{... | collective-permute-start | bytes 1179656 | tf_op jit(solution)/shard_map/ppermute | solution.py:301
  78.4 12.7 %collective-permute-start.12 = (bf16[3,64,1024]{2,1,0:T(8,128)(2,1)S(1)}, bf16[3,64,1024]{2,1,0:T(8,128)(2,1)S(1)}, u32[]{:S(2)}, u32[]{:S(2)}) collective-permute-start(bf16[3,64,1024]{2,1,0:T(8,128)(2,1)S(1)} %copy_bitcast_fusion.rows), channel_id=1, source_target_pairs={{0,16},{8,24},{16,0},{24,8},{32,48},{40,56},{48,32},{56,40},{64,80... | collective-permute-start | bytes 1179656 | tf_op jit(solution)/shard_map/ppermute | solution.py:294
  81.1 19.9 %collective-permute-start.13 = (bf16[3,64,1024]{2,1,0:T(8,128)(2,1)S(1)}, bf16[3,64,1024]{2,1,0:T(8,128)(2,1)}, u32[]{:S(2)}, u32[]{:S(2)}) collective-permute-start(bf16[3,64,1024]{2,1,0:T(8,128)(2,1)S(1)} %copy_bitcast_fusion.rows), channel_id=1, source_target_pairs={{0,32},{8,40},{16,48},{24,56},{32,64},{40,72},{48,80},{56,88},{64,... | collective-permute-start | bytes 1179656 | tf_op jit(solution)/shard_map/ppermute | solution.py:301
  81.4 19.6 %collective-permute-start.14 = (bf16[3,64,1024]{2,1,0:T(8,128)(2,1)S(1)}, bf16[3,64,1024]{2,1,0:T(8,128)(2,1)}, u32[]{:S(2)}, u32[]{:S(2)}) collective-permute-start(bf16[3,64,1024]{2,1,0:T(8,128)(2,1)S(1)} %copy_bitcast_fusion.rows), channel_id=1, source_target_pairs={{0,96},{8,104},{16,112},{24,120},{32,0},{40,8},{48,16},{56,24},{64... | collective-permute-start | bytes 1179656 | tf_op jit(solution)/shard_map/ppermute | solution.py:301
  83.8 17.2 %collective-permute-start.15 = (bf16[3,64,1024]{2,1,0:T(8,128)(2,1)S(1)}, bf16[3,64,1024]{2,1,0:T(8,128)(2,1)}, u32[]{:S(2)}, u32[]{:S(2)}) collective-permute-start(bf16[3,64,1024]{2,1,0:T(8,128)(2,1)S(1)} %copy_bitcast_fusion.rows), channel_id=1, source_target_pairs={{0,8},{8,16},{16,24},{24,0},{32,40},{40,48},{48,56},{56,32},{64,72... | collective-permute-start | bytes 1179656 | tf_op jit(solution)/shard_map/ppermute | solution.py:294
  91.1 14.3 %copy-start.1 = (bf16[3,64,1024]{2,1,0:T(8,128)(2,1)}, bf16[3,64,1024]{2,1,0:T(8,128)(2,1)S(1)}, u32[]{:S(2)}) copy-start(bf16[3,64,1024]{2,1,0:T(8,128)(2,1)S(1)} %collective-permute-done.11.y2) | copy-start | bytes 1179652
  91.1 9.8 %copy-start.2 = (bf16[3,64,1024]{2,1,0:T(8,128)(2,1)}, bf16[3,64,1024]{2,1,0:T(8,128)(2,1)S(1)}, u32[]{:S(2)}) copy-start(bf16[3,64,1024]{2,1,0:T(8,128)(2,1)S(1)} %collective-permute-done.12.x2) | copy-start | bytes 1179652
  101.0 19.9 %all-to-all-start.3 = ((bf16[16,3,64,128]{3,2,1,0:T(8,128)(2,1)}), bf16[16,3,64,128]{3,2,1,0:T(8,128)(2,1)S(1)}, u32[]{:S(2)}, u32[]{:S(2)}) async-start(bf16[16,3,64,128]{3,2,1,0:T(8,128)(2,1)} %rotate_left.1), calls=%async_computation.3 | async-start | bytes 1572864 | tf_op jit(solution)/shard_map/all_to_all | solution.py:387
  110.8 23.1 %collective-permute-start.21 = (bf16[3,64,1280]{2,1,0:T(8,128)(2,1)}, bf16[3,64,1280]{2,1,0:T(8,128)(2,1)S(1)}, u32[]{:S(2)}, u32[]{:S(2)}) collective-permute-start(bf16[3,64,1280]{2,1,0:T(8,128)(2,1)} %get-tuple-element.114), channel_id=1, source_target_pairs={{0,24},{8,0},{16,8},{24,16},{32,56},{40,32},{48,40},{56,48},{64,88... | collective-permute-start | bytes 1474568 | tf_op jit(solution)/shard_map/ppermute | solution.py:294
  113.5 4.7 %collective-permute-start.16 = (bf16[3,64,128]{2,1,0:T(8,128)(2,1)S(1)}, bf16[3,64,128]{2,1,0:T(8,128)(2,1)S(1)}, u32[]{:S(2)}, u32[]{:S(2)}) collective-permute-start(bf16[3,64,128]{2,1,0:T(8,128)(2,1)S(1)} %get-tuple-element.105), channel_id=1, source_target_pairs={{0,96},{8,104},{16,112},{24,120},{32,0},{40,8},{48,16},{56,24},{64... | collective-permute-start | bytes 147464 | tf_op jit(solution)/shard_map/ppermute | solution.py:301
  115.9 4.9 %collective-permute-start.17 = (bf16[3,64,128]{2,1,0:T(8,128)(2,1)S(1)}, bf16[3,64,128]{2,1,0:T(8,128)(2,1)S(1)}, u32[]{:S(2)}, u32[]{:S(2)}) collective-permute-start(bf16[3,64,128]{2,1,0:T(8,128)(2,1)S(1)} %get-tuple-element.106), channel_id=1, source_target_pairs={{0,64},{8,72},{16,80},{24,88},{32,96},{40,104},{48,112},{56,120},{... | collective-permute-start | bytes 147464 | tf_op jit(solution)/shard_map/ppermute | solution.py:301
  116.5 15.5 %collective-permute-start.19 = (bf16[3,64,1024]{2,1,0:T(8,128)(2,1)}, bf16[3,64,1024]{2,1,0:T(8,128)(2,1)S(1)}, u32[]{:S(2)}, u32[]{:S(2)}) collective-permute-start(bf16[3,64,1024]{2,1,0:T(8,128)(2,1)} %get-tuple-element.112), channel_id=1, source_target_pairs={{0,8},{8,16},{16,24},{24,0},{32,40},{40,48},{48,56},{56,32},{64,72... | collective-permute-start | bytes 1179656 | tf_op jit(solution)/shard_map/ppermute | solution.py:294
  116.5 17.5 %collective-permute-start.20 = (bf16[3,64,1024]{2,1,0:T(8,128)(2,1)}, bf16[3,64,1024]{2,1,0:T(8,128)(2,1)S(1)}, u32[]{:S(2)}, u32[]{:S(2)}) collective-permute-start(bf16[3,64,1024]{2,1,0:T(8,128)(2,1)} %get-tuple-element.113), channel_id=1, source_target_pairs={{0,16},{8,24},{16,0},{24,8},{32,48},{40,56},{48,32},{56,40},{64,80... | collective-permute-start | bytes 1179656 | tf_op jit(solution)/shard_map/ppermute | solution.py:294
  126.1 13.9 %all-to-all-start.4 = ((bf16[8,3,8,1024]{3,2,1,0:T(8,128)(2,1)}), bf16[8,3,8,1024]{3,2,1,0:T(8,128)(2,1)S(1)}, u32[]{:S(2)}, u32[]{:S(2)}) async-start(bf16[8,3,8,1024]{3,2,1,0:T(8,128)(2,1)} %get-tuple-element.116), calls=%async_computation.4 | async-start | bytes 786432 | tf_op jit(solution)/shard_map/all_to_all | solution.py:387
  131.9 4.4 %collective-permute-start.18 = (bf16[3,64,128]{2,1,0:T(8,128)(2,1)S(1)}, bf16[3,64,128]{2,1,0:T(8,128)(2,1)S(1)}, u32[]{:S(2)}, u32[]{:S(2)}) collective-permute-start(bf16[3,64,128]{2,1,0:T(8,128)(2,1)S(1)} %get-tuple-element.110), channel_id=1, source_target_pairs={{0,32},{8,40},{16,48},{24,56},{32,64},{40,72},{48,80},{56,88},{64,... | collective-permute-start | bytes 147464 | tf_op jit(solution)/shard_map/ppermute | solution.py:301

commit v5 on v4

--- a/solution.py
+++ b/solution.py
@@ -161,7 +161,7 @@
         out[slot, :HALF] = dot(both[:, :HALF], basis[slot], TN)
 
 
-def rotate_right_kernel(used, rows, moment_hbm, basis_hbm, first, packed, moment, basis, small_sems, sems):
+def rotate_right_kernel(used, rows, moment_hbm, basis_hbm, first_hbm, packed, moment, first, basis, small_sems, sems):
     small = pltpu.make_async_copy(moment_hbm, moment, small_sems.at[0])
     arrivals = fetch(basis_hbm, basis, sems)
     small.start()
@@ -172,6 +172,8 @@
         grad = rows[slot]
         mixed = BETA_FIRST * moment[slot].astype(F32) + (1.0 - BETA_FIRST) * grad.astype(F32)
         first[slot] = jnp.where(used[slot] > 0, mixed, 0.0).astype(BF16)
+    done = pltpu.make_async_copy(first, first_hbm, small_sems.at[1])
+    done.start()
     for slot in range(rows.shape[0]):
         arrivals[slot].wait()
         turned = dot(rows[slot], basis[slot], NN)
@@ -181,6 +183,7 @@
             b = turned[half:, lanes]
             packed[2 * pair, slot] = jnp.where(low, a, swap_halves(b)).astype(BF16)
             packed[2 * pair + 1, slot] = jnp.where(low, swap_halves(a), b).astype(BF16)
+    done.wait()
 
 
 def rotate_left_kernel(packed, basis_hbm, ready, out, basis, sems):
@@ -202,9 +205,10 @@
         out[:, slot] = joined.reshape(parts, HALF, LANES)
 
 
-def step_kernel(used, packed, basis_hbm, second, step, basis, sems):
+def step_kernel(used, packed, basis_hbm, second_hbm, step, basis, second, sems, out_sems):
     arrivals = fetch(basis_hbm, basis, sems)
     low = low_lanes(HALF)
+    done = []
     for slot in range(second.shape[0]):
         lefts = []
         for pair in range(packed.shape[0] // 2):
@@ -214,9 +218,12 @@
             lefts.append(jnp.where(low, a, swap_halves(b)).astype(BF16))
             v = jnp.where(low, swap_halves(a), b)
             second[slot, :, lanes] = jnp.where(used[slot] > 0, v, 0.0).astype(BF16)
+        done.append(pltpu.make_async_copy(second.at[slot], second_hbm.at[slot], out_sems.at[slot]))
+        done[slot].start()
         arrivals[slot].wait()
         moved = dot(jnp.concatenate(lefts, axis=1), basis[slot], NT)
         step[:, slot] = moved.reshape(step.shape[0], step.shape[2], step.shape[3]).astype(BF16)
+    wait_all(done)
 
 
 def gram_tiles_kernel(
@@ -256,18 +263,25 @@
 
 def gram_sum_kernel(
     here, used, own, left0, left1, left2, left3, right0, right1, right2, right3, left_hbm, right_hbm,
-    new_left, new_right, left, right, sems,
+    new_left_hbm, new_right_hbm, left, right, sems, out_sems,
 ):
     y, x = here[0], here[1]
-    old = start_all(
-        [pltpu.make_async_copy(left_hbm, left, sems.at[0]), pltpu.make_async_copy(right_hbm, right, sems.at[1])]
-    )
     slots, slab, order = left.shape
+    old = [
+        start_all(
+            [
+                pltpu.make_async_copy(right_hbm.at[slot], right.at[slot], sems.at[slot, 0]),
+                pltpu.make_async_copy(left_hbm.at[slot], left.at[slot], sems.at[slot, 1]),
+            ]
+        )
+        for slot in range(slots)
+    ]
+    done = []
     lines = own.shape[2]
     column = lax.broadcasted_iota(jnp.int32, (slab, lines), 1) // HALF
-    wait_all(old)
     for slot in range(slots):
         is_used = used[slot] > 0
+        wait_all(old[slot])
         for ahead, tile in enumerate((left0, left1, left2, left3)):
             back = (SIDE - ahead) % SIDE
             same = spread(own[slot, :, back // 2 * LANES :][:, :LANES], back % 2)
@@ -278,13 +292,20 @@
             gram = jnp.where(column == turn(x, 3), spread(tile, 0), gram)
             gram = jnp.where(column == turn(x, 2), spread(tile, 1), gram)
             lanes = pl.ds(pl.multiple_of(turn(y, ahead) * lines, lines), lines)
-            new_left[slot, :, lanes] = jnp.where(
+            left[slot, :, lanes] = jnp.where(
                 is_used, BETA_FACTOR * left[slot, :, lanes] + (1.0 - BETA_FACTOR) * gram, 0.0
             )
         gram = right0[slot]
         for term in (right1, right2, right3):
             gram = gram + term[slot, :, :order].astype(F32)
-        new_right[slot] = jnp.where(is_used, BETA_FACTOR * right[slot] + (1.0 - BETA_FACTOR) * gram, 0.0)
+        right[slot] = jnp.where(is_used, BETA_FACTOR * right[slot] + (1.0 - BETA_FACTOR) * gram, 0.0)
+        done += start_all(
+            [
+                pltpu.make_async_copy(right.at[slot], new_right_hbm.at[slot], out_sems.at[slot, 0]),
+                pltpu.make_async_copy(left.at[slot], new_left_hbm.at[slot], out_sems.at[slot, 1]),
+            ]
+        )
+    wait_all(done)
 
 
 def along_x(value, by):
@@ -411,8 +432,9 @@
     new_first, packed = call(
         rotate_right_kernel, "rotate_right",
         [(used, SMEM), (rows, VMEM), (first_moment, HBM), (right_basis, HBM)],
-        [(slabs, BF16, None), ((replicas, slots, slab // 2, LANES), BF16, VMEM)],
-        [pltpu.VMEM(slabs, BF16), basis_scratch[0], pltpu.SemaphoreType.DMA((1,)), basis_scratch[1]], 3, 8,
+        [(slabs, BF16, HBM), ((replicas, slots, slab // 2, LANES), BF16, VMEM)],
+        [pltpu.VMEM(slabs, BF16), pltpu.VMEM(slabs, BF16), basis_scratch[0], pltpu.SemaphoreType.DMA((2,)), basis_scratch[1]],
+        3, 8,
     )
     rows, packed = lax.optimization_barrier((rows, packed))
     packed = exchange(packed, "dp")
@@ -436,11 +458,12 @@
     )
     lefts = [tiles[1]] + [along_y(tiles[1 + back], SIDE - back) for back in (1, 2, 3)]
     rights = [tiles[1 + SIDE]] + [along_x(tiles[1 + SIDE + by], by) for by in (1, 2, 3)]
-    early_lefts, turned = lax.optimization_barrier((lefts[1:3], turned))
-    lefts = [lefts[0], *early_lefts, lefts[3]]
+    early_lefts, turned = lax.optimization_barrier((lefts[1:2], turned))
+    lefts = [lefts[0], *early_lefts, *lefts[2:]]
     new_second, step = call(
         step_kernel, "step_rows", [(used, SMEM), (turned, VMEM), (right_basis, HBM)],
-        [(slabs, BF16, None), ((owners, slots, part_rows, order), BF16, VMEM)], basis_scratch, 3, 8,
+        [(slabs, BF16, HBM), ((owners, slots, part_rows, order), BF16, VMEM)],
+        [basis_scratch[0], pltpu.VMEM(slabs, BF16), basis_scratch[1], pltpu.SemaphoreType.DMA((slots,))], 3, 8,
     )
     returned = exchange(step, "owner")
     rights, step = lax.optimization_barrier((rights, step))
@@ -448,8 +471,12 @@
         gram_sum_kernel, "gram_sum",
         [(here, SMEM), (used, SMEM)] + [(value, VMEM) for value in [tiles[0]] + lefts + rights]
         + [(left_factor, HBM), (right_factor, HBM)],
-        [(slabs, F32, None)] * 2,
-        [pltpu.VMEM(slabs, F32), pltpu.VMEM(slabs, F32), pltpu.SemaphoreType.DMA((2,))], 0, 8,
+        [(slabs, F32, HBM)] * 2,
+        [
+            pltpu.VMEM(slabs, F32), pltpu.VMEM(slabs, F32), pltpu.SemaphoreType.DMA((slots, 2)),
+            pltpu.SemaphoreType.DMA((slots, 2)),
+        ],
+        0, 8,
     )
 
     picked = returned.reshape(owners * slots, part_rows, order).at[block_slot].get(mode="promise_in_bounds")

time: 142 us -> 141 us (level)
  waiting for transfers between devices: 38.5 us -> 36.4 us
  starting transfers between devices: 59.3 us -> 61 us
    ppermute x11, waiting for transfers between devices: 24.6 us -> 22.2 us  [along_y(): return lax.ppermute(value, 'dp', pairs)]
  transfers between devices with their start and end apart: 27 -> 27, of which waited for: 10 -> 11; matrix products, arithmetic and copies ran while one was open for 0% -> 0% of each run, Pallas kernels for 22% -> 22%
where the time goes in v5:
time: 141 us
  starting transfers between devices  61 us (43%)
  Pallas kernels  40.9 us (29%)
  waiting for transfers between devices  36.4 us (26%)
    pallas_call x10, Pallas kernels, call(): pl.pallas_call(kernel, in_specs=[pl.BlockSpec(memory_space=space) for _,...  40.9 us
    all_to_all x5, starting transfers between devices, exchange(): return lax.all_to_all(value, axis, split_axis=0, concat_axis=0, tiled=True)  27.3 us
    ppermute x11, waiting for transfers between devices, along_y(): return lax.ppermute(value, 'dp', pairs)  22.2 us
    ppermute x11, starting transfers between devices, along_x(): return lax.ppermute(value, 'dp', pairs)  16.9 us
    ppermute x11, starting transfers between devices, along_y(): return lax.ppermute(value, 'dp', pairs)  16.7 us
    ppermute x11, waiting for transfers between devices, along_x(): return lax.ppermute(value, 'dp', pairs)  8.37 us
    all_to_all x5, waiting for transfers between devices, exchange(): return lax.all_to_all(value, axis, split_axis=0, concat_axis=0, tiled=True)  5.85 us
  transfers between devices with their start and end apart: 27, of which 11 were waited for; matrix products, arithmetic and copies ran while one was open for 0% of the time, Pallas kernels for 22%

profile of v5, /device:TPU:1, one launch (start us, length us, event | category | flops | bytes accessed | tf_op | source)
XLA Modules:
  0.0 140.8 jit_solution(5060748468558425685)
XLA Ops:
  0.7 0.1 pad_add_fusion.here
  0.7 2.4 %first_send.1 = (bf16[8,18432]{1,0:T(8,128)(2,1)S(1)}, bf16[4,8,10240]{2,1,0:T(8,128)(2,1)S(1)}, bf16[8,18432]{1,0:T(8,128)(2,1)S(1)}, bf16[4,8,10240]{2,1,0:T(8,128)(2,1)S(1)}, bf16[8,18432]{1,0:T(8,128)(2,1)S(1)}) custom-call(s32[2]{0:T(128)S(1)} %pad_add_fusion.here, bf16[4,4,8,12288]{3,2,1,0:T(8,128)(2,1)} %bitcast.13), custom_call_target="tpu_custom_call" | custom-call | bytes 5242880 | tf_op jit(solution)/shard_map/first_send/pallas_call | solution.py:327
  3.1 2.2 %collective-permute-start.1 = (bf16[4,8,10240]{2,1,0:T(8,128)(2,1)S(1)}, bf16[4,8,10240]{2,1,0:T(8,128)(2,1)S(1)}, u32[]{:S(2)}, u32[]{:S(2)}) collective-permute-start(bf16[4,8,10240]{2,1,0:T(8,128)(2,1)S(1)} %get-tuple-element.65), channel_id=1, source_target_pairs={{0,32},{8,40},{16,48},{24,56},{32,64},{40,72},{48,80},{56,88},{64,... | collective-permute-start | bytes 1966088 | tf_op jit(solution)/shard_map/ppermute | solution.py:322
  5.3 1.5 %collective-permute-start.3 = (bf16[4,8,10240]{2,1,0:T(8,128)(2,1)S(1)}, bf16[4,8,10240]{2,1,0:T(8,128)(2,1)S(1)}, u32[]{:S(2)}, u32[]{:S(2)}) collective-permute-start(bf16[4,8,10240]{2,1,0:T(8,128)(2,1)S(1)} %get-tuple-element.67), channel_id=1, source_target_pairs={{0,96},{8,104},{16,112},{24,120},{32,0},{40,8},{48,16},{56,24},{64... | collective-permute-start | bytes 1966088 | tf_op jit(solution)/shard_map/ppermute | solution.py:322
  6.8 1.2 collective-permute-start
  8.0 1.5 %collective-permute-start.2 = (bf16[8,18432]{1,0:T(8,128)(2,1)S(1)}, bf16[8,18432]{1,0:T(8,128)(2,1)S(1)}, u32[]{:S(2)}, u32[]{:S(2)}) collective-permute-start(bf16[8,18432]{1,0:T(8,128)(2,1)S(1)} %get-tuple-element.66), channel_id=1, source_target_pairs={{0,24},{8,0},{16,8},{24,16},{32,56},{40,32},{48,40},{56,48},{64,88... | collective-permute-start | bytes 884744 | tf_op jit(solution)/shard_map/ppermute | solution.py:315
  9.5 1.5 %collective-permute-start.4 = (bf16[8,18432]{1,0:T(8,128)(2,1)S(1)}, bf16[8,18432]{1,0:T(8,128)(2,1)S(1)}, u32[]{:S(2)}, u32[]{:S(2)}) collective-permute-start(bf16[8,18432]{1,0:T(8,128)(2,1)S(1)} %get-tuple-element.68), channel_id=1, source_target_pairs={{0,16},{8,24},{16,0},{24,8},{32,48},{40,56},{48,32},{56,40},{64,80... | collective-permute-start | bytes 884744 | tf_op jit(solution)/shard_map/ppermute | solution.py:315
  11.0 5.0 %moment_right.1 = bf16[16,3,64,128]{3,2,1,0:T(8,128)(2,1)} custom-call(bf16[3,64,1024]{2,1,0:T(8,128)(2,1)} %moment_hbm.3, bf16[3,64,1024]{2,1,0:T(8,128)(2,1)} %second_hbm.1, bf16[3,1024,1024]{2,1,0:T(8,128)(2,1)} %basis_hbm.9), custom_call_target="tpu_custom_call" | custom-call | flops 402653184 | bytes 8388608 | tf_op jit(solution)/shard_map/moment_right/pallas_call | solution.py:327
  16.0 0.0 collective-permute-done.2.a3
  16.0 6.7 %collective-permute-done.4.a2 = bf16[8,18432]{1,0:T(8,128)(2,1)S(1)} collective-permute-done((bf16[8,18432]{1,0:T(8,128)(2,1)S(1)}, bf16[8,18432]{1,0:T(8,128)(2,1)S(1)}, u32[]{:S(2)}, u32[]{:S(2)}) %collective-permute-start.4) | collective-permute-done | bytes 294944 | tf_op jit(solution)/shard_map/ppermute | solution.py:315
  22.7 0.0 collective-permute-done.1.b1
  22.8 0.0 collective-permute-done.3.b3
  22.8 4.6 %all-to-all-start = ((bf16[16,3,64,128]{3,2,1,0:T(8,128)(2,1)}), bf16[16,3,64,128]{3,2,1,0:T(8,128)(2,1)S(1)}, u32[]{:S(2)}, u32[]{:S(2)}) async-start(bf16[16,3,64,128]{3,2,1,0:T(8,128)(2,1)} %moment_right.1), calls=%async_computation | async-start | bytes 1572864 | tf_op jit(solution)/shard_map/all_to_all | solution.py:408
  27.3 2.1 %second_send.1 = (bf16[8,2048]{1,0:T(8,128)(2,1)S(1)}, bf16[8,2048]{1,0:T(8,128)(2,1)S(1)}, bf16[8,12288]{1,0:T(8,128)(2,1)S(1)}, bf16[8,2048]{1,0:T(8,128)(2,1)...) custom-call(s32[2]{0:T(128)S(1)} %pad_add_fusion.here, ...), custom_call_target="tpu_custom_call" | custom-call | bytes 4194304 | tf_op jit(solution)/shard_map/second_send/pallas_call | solution.py:327
  29.4 2.9 %collective-permute-start.7 = (bf16[8,12288]{1,0:T(8,128)(2,1)S(1)}, bf16[8,12288]{1,0:T(8,128)(2,1)S(1)}, u32[]{:S(2)}, u32[]{:S(2)}) collective-permute-start(bf16[8,12288]{1,0:T(8,128)(2,1)S(1)} %get-tuple-element.77), channel_id=1, source_target_pairs={{0,64},{8,72},{16,80},{24,88},{32,96},{40,104},{48,112},{56,120},{... | collective-permute-start | bytes 589832 | tf_op jit(solution)/shard_map/ppermute | solution.py:322
  32.4 2.7 %collective-permute-start.10 = (bf16[8,10240]{1,0:T(8,128)(2,1)S(1)}, bf16[8,10240]{1,0:T(8,128)(2,1)S(1)}, u32[]{:S(2)}, u32[]{:S(2)}) collective-permute-start(bf16[8,10240]{1,0:T(8,128)(2,1)S(1)} %get-tuple-element.81), channel_id=1, source_target_pairs={{0,16},{8,24},{16,0},{24,8},{32,48},{40,56},{48,32},{56,40},{64,80... | collective-permute-start | bytes 491528 | tf_op jit(solution)/shard_map/ppermute | solution.py:315
  35.1 0.3 collective-permute-start.8
  35.3 2.4 %collective-permute-start.9 = (bf16[8,10240]{1,0:T(8,128)(2,1)S(1)}, bf16[8,10240]{1,0:T(8,128)(2,1)S(1)}, u32[]{:S(2)}, u32[]{:S(2)}) collective-permute-start(bf16[8,10240]{1,0:T(8,128)(2,1)S(1)} %get-tuple-element.80), channel_id=1, source_target_pairs={{0,24},{8,0},{16,8},{24,16},{32,56},{40,32},{48,40},{56,48},{64,88... | collective-permute-start | bytes 491528 | tf_op jit(solution)/shard_map/ppermute | solution.py:315
  37.7 0.3 collective-permute-start.5
  38.0 7.1 %collective-permute-done.5.p1 = bf16[8,2048]{1,0:T(8,128)(2,1)S(1)} collective-permute-done((bf16[8,2048]{1,0:T(8,128)(2,1)S(1)}, bf16[8,2048]{1,0:T(8,128)(2,1)S(1)}, u32[]{:S(2)}, u32[]{:S(2)}) %collective-permute-start.5) | collective-permute-done | bytes 32800 | tf_op jit(solution)/shard_map/ppermute | solution.py:322
  45.1 0.1 select_reduce_fusion.holder
  45.2 2.7 %collective-permute-done.6.p3 = bf16[8,2048]{1,0:T(8,128)(2,1)S(1)} collective-permute-done((bf16[8,2048]{1,0:T(8,128)(2,1)S(1)}, bf16[8,2048]{1,0:T(8,128)(2,1)S(1)}, u32[]{:S(2)}, u32[]{:S(2)}) %collective-permute-start.6) | collective-permute-done | bytes 32800 | tf_op jit(solution)/shard_map/ppermute | solution.py:322
  47.9 0.0 collective-permute-done.10.q2
  47.9 0.0 collective-permute-done.8.q1
  47.9 0.0 collective-permute-done.9.q3
  47.9 0.0 all-to-all-done.packed
  47.9 1.4 %outgoing.1 = bf16[24,8,1024]{2,1,0:T(8,128)(2,1)} custom-call(s32[24]{0:T(128)S(1)} %select_reduce_fusion.holder, bf16[8,2048]{1,0:T(8,128)(2,1)S(1)} %get-tuple-element.83.p0, bf16[8,2048]{1,0:T(8,128)(2,1)S(1)} %collective-permute-done.5.p1, bf16[8,2048]{1,0:T(8,128)(2,1)S(1)} %collective-permute-done.6.p3, ...), custom_call_target="tpu_custom_call" | custom-call | bytes 1048576 | tf_op jit(solution)/shard_map/outgoing/pallas_call | solution.py:327
  49.3 7.7 %all-to-all-start.1 = ((bf16[8,3,8,1024]{3,2,1,0:T(8,128)(2,1)}), bf16[8,3,8,1024]{3,2,1,0:T(8,128)(2,1)S(1)}, u32[]{:S(2)}, u32[]{:S(2)}) async-start(bf16[8,3,8,1024]{3,2,1,0:T(8,128)(2,1)} %bitcast.3), calls=%async_computation.1 | async-start | bytes 786432 | tf_op jit(solution)/shard_map/all_to_all | solution.py:408
  57.1 0.1 fusion
  57.2 0.1 dynamic_slice.3.used
  57.3 3.4 %moment_left.1.ready = f32[3,128,1024]{2,1,0:T(8,128)S(1)} custom-call(bf16[16,3,64,128]{3,2,1,0:T(8,128)(2,1)S(1)} %all-to-all-done.packed, bf16[3,1024,1024]{2,1,0:T(8,128)(2,1)} %basis_hbm.8), custom_call_target="tpu_custom_call" | custom-call | flops 402653184 | bytes 8388608 | tf_op jit(solution)/shard_map/moment_left/pallas_call | solution.py:327
  60.7 4.5 %all-to-all-done.1 = bf16[8,3,8,1024]{3,2,1,0:T(8,128)(2,1)S(1)} async-done(((bf16[8,3,8,1024]{3,2,1,0:T(8,128)(2,1)}), bf16[8,3,8,1024]{3,2,1,0:T(8,128)(2,1)S(1)}, u32[]{:S(2)}, u32[]{:S(2)}) %all-to-all-start.1) | async-done | bytes 393248 | tf_op jit(solution)/shard_map/all_to_all | solution.py:408
  65.2 0.0 copy-start
  65.2 6.0 %rotate_right.1 = (bf16[3,64,1024]{2,1,0:T(8,128)(2,1)}, bf16[16,3,32,128]{3,2,1,0:T(8,128)(2,1)}) custom-call(s32[3]{0:T(128)S(1)} %dynamic_slice.3.used, bf16[3,64,1024]{2,1,0:T(8,128)(2,1)S(1)} %copy_bitcast_fusion.rows, bf16[3,64,1024]{2,1,0:T(8,128)(2,1)} %moment_hbm.3, bf16[3,1024,1024]{2,1,0:T(8,128)(2,1)} %basis_hbm.9), custom_call_target="tpu_custom_call" | custom-call | flops 402653184 | bytes 8388608 | tf_op jit(solution)/shard_map/rotate_right/pallas_call | solution.py:327
  71.3 4.3 %all-to-all-start.2 = ((bf16[16,3,32,128]{3,2,1,0:T(8,128)(2,1)}), bf16[16,3,32,128]{3,2,1,0:T(8,128)(2,1)S(1)}, u32[]{:S(2)}, u32[]{:S(2)}) async-start(bf16[16,3,32,128]{3,2,1,0:T(8,128)(2,1)} %get-tuple-element.95), calls=%async_computation.2 | async-start | bytes 786432 | tf_op jit(solution)/shard_map/all_to_all | solution.py:408
  75.5 2.9 %collective-permute-start.11 = (bf16[3,64,1024]{2,1,0:T(8,128)(2,1)S(1)}, bf16[3,64,1024]{2,1,0:T(8,128)(2,1)S(1)}, u32[]{:S(2)}, u32[]{:S(2)}) collective-permute-start(bf16[3,64,1024]{2,1,0:T(8,128)(2,1)S(1)} %copy_bitcast_fusion.rows), channel_id=1, source_target_pairs={{0,64},{8,72},{16,80},{24,88},{32,96},{40,104},{48,112},{56,120},{... | collective-permute-start | bytes 1179656 | tf_op jit(solution)/shard_map/ppermute | solution.py:322
  78.4 2.7 %collective-permute-start.12 = (bf16[3,64,1024]{2,1,0:T(8,128)(2,1)S(1)}, bf16[3,64,1024]{2,1,0:T(8,128)(2,1)S(1)}, u32[]{:S(2)}, u32[]{:S(2)}) collective-permute-start(bf16[3,64,1024]{2,1,0:T(8,128)(2,1)S(1)} %copy_bitcast_fusion.rows), channel_id=1, source_target_pairs={{0,16},{8,24},{16,0},{24,8},{32,48},{40,56},{48,32},{56,40},{64,80... | collective-permute-start | bytes 1179656 | tf_op jit(solution)/shard_map/ppermute | solution.py:315
  81.1 0.3 collective-permute-start.13
  81.4 2.4 %collective-permute-start.14 = (bf16[3,64,1024]{2,1,0:T(8,128)(2,1)S(1)}, bf16[3,64,1024]{2,1,0:T(8,128)(2,1)}, u32[]{:S(2)}, u32[]{:S(2)}) collective-permute-start(bf16[3,64,1024]{2,1,0:T(8,128)(2,1)S(1)} %copy_bitcast_fusion.rows), channel_id=1, source_target_pairs={{0,96},{8,104},{16,112},{24,120},{32,0},{40,8},{48,16},{56,24},{64... | collective-permute-start | bytes 1179656 | tf_op jit(solution)/shard_map/ppermute | solution.py:322
  83.8 0.3 collective-permute-start.15
  84.1 0.5 all-to-all-done.2.packed
  84.6 6.5 %rotate_left.1 = bf16[16,3,64,128]{3,2,1,0:T(8,128)(2,1)} custom-call(bf16[16,3,32,128]{3,2,1,0:T(8,128)(2,1)S(1)} %all-to-all-done.2.packed, bf16[3,1024,1024]{2,1,0:T(8,128)(2,1)} %basis_hbm.8, f32[3,128,1024]{2,1,0:T(8,128)S(1)} %moment_left.1.ready), custom_call_target="tpu_custom_call" | custom-call | flops 1207959552 | bytes 8388608 | tf_op jit(solution)/shard_map/rotate_left/pallas_call | solution.py:327
  91.1 0.0 collective-permute-done.11.y2
  91.2 9.8 %collective-permute-done.13.y1 = bf16[3,64,1024]{2,1,0:T(8,128)(2,1)} collective-permute-done((bf16[3,64,1024]{2,1,0:T(8,128)(2,1)S(1)}, bf16[3,64,1024]{2,1,0:T(8,128)(2,1)}, u32[]{:S(2)}, u32[]{:S(2)}) %collective-permute-start.13) | collective-permute-done | bytes 393248 | tf_op jit(solution)/shard_map/ppermute | solution.py:322
  101.0 0.0 collective-permute-done.14.y3
  101.0 4.4 %all-to-all-start.3 = ((bf16[16,3,64,128]{3,2,1,0:T(8,128)(2,1)}), bf16[16,3,64,128]{3,2,1,0:T(8,128)(2,1)S(1)}, u32[]{:S(2)}, u32[]{:S(2)}) async-start(bf16[16,3,64,128]{3,2,1,0:T(8,128)(2,1)} %rotate_left.1), calls=%async_computation.3 | async-start | bytes 1572864 | tf_op jit(solution)/shard_map/all_to_all | solution.py:408
  105.4 5.4 %gram_tiles.1 = (f32[3,64,256]{2,1,0:T(8,128)S(1)}, f32[3,64,128]{2,1,0:T(8,128)S(1)}, bf16[3,64,128]{2,1,0:T(8,128)(2,1)S(1)}, bf16[3,64,128]{2,1,0:T(8,128)(2,...) custom-call(s32[2]{0:T(128)S(1)} %pad_add_fusion.here, ...), custom_call_target="tpu_custom_call" | custom-call | flops 1207959552 | bytes 6291456 | tf_op jit(solution)/shard_map/gram_tiles/pallas_call | solution.py:327
  110.8 2.6 %collective-permute-start.21 = (bf16[3,64,1280]{2,1,0:T(8,128)(2,1)}, bf16[3,64,1280]{2,1,0:T(8,128)(2,1)S(1)}, u32[]{:S(2)}, u32[]{:S(2)}) collective-permute-start(bf16[3,64,1280]{2,1,0:T(8,128)(2,1)} %get-tuple-element.112), channel_id=1, source_target_pairs={{0,24},{8,0},{16,8},{24,16},{32,56},{40,32},{48,40},{56,48},{64,88... | collective-permute-start | bytes 1474568 | tf_op jit(solution)/shard_map/ppermute | solution.py:315
  113.5 2.4 %collective-permute-start.16 = (bf16[3,64,128]{2,1,0:T(8,128)(2,1)S(1)}, bf16[3,64,128]{2,1,0:T(8,128)(2,1)S(1)}, u32[]{:S(2)}, u32[]{:S(2)}) collective-permute-start(bf16[3,64,128]{2,1,0:T(8,128)(2,1)S(1)} %get-tuple-element.104), channel_id=1, source_target_pairs={{0,96},{8,104},{16,112},{24,120},{32,0},{40,8},{48,16},{56,24},{64... | collective-permute-start | bytes 147464 | tf_op jit(solution)/shard_map/ppermute | solution.py:322
  115.9 0.0 collective-permute-start.19
  115.9 1.8 %collective-permute-start.20 = (bf16[3,64,1024]{2,1,0:T(8,128)(2,1)}, bf16[3,64,1024]{2,1,0:T(8,128)(2,1)S(1)}, u32[]{:S(2)}, u32[]{:S(2)}) collective-permute-start(bf16[3,64,1024]{2,1,0:T(8,128)(2,1)} %get-tuple-element.111), channel_id=1, source_target_pairs={{0,16},{8,24},{16,0},{24,8},{32,48},{40,56},{48,32},{56,40},{64,80... | collective-permute-start | bytes 1179656 | tf_op jit(solution)/shard_map/ppermute | solution.py:315
  117.7 0.1 collective-permute-done.16.left1
  117.7 0.8 all-to-all-done.3.packed
  118.6 5.3 %step_rows.1 = (bf16[3,64,1024]{2,1,0:T(8,128)(2,1)}, bf16[8,3,8,1024]{3,2,1,0:T(8,128)(2,1)}) custom-call(s32[3]{0:T(128)S(1)} %dynamic_slice.3.used, bf16[16,3,64,128]{3,2,1,0:T(8,128)(2,1)S(1)} %all-to-all-done.3.packed, bf16[3,1024,1024]{2,1,0:T(8,128)(2,1)} %basis_hbm.9), custom_call_target="tpu_custom_call" | custom-call | flops 402653184 | bytes 8388608 | tf_op jit(solution)/shard_map/step_rows/pallas_call | solution.py:327
  123.9 6.3 %all-to-all-start.4 = ((bf16[8,3,8,1024]{3,2,1,0:T(8,128)(2,1)}), bf16[8,3,8,1024]{3,2,1,0:T(8,128)(2,1)S(1)}, u32[]{:S(2)}, u32[]{:S(2)}) async-start(bf16[8,3,8,1024]{3,2,1,0:T(8,128)(2,1)} %get-tuple-element.114), calls=%async_computation.4 | async-start | bytes 786432 | tf_op jit(solution)/shard_map/all_to_all | solution.py:408
  130.2 0.9 collective-permute-start.17
  131.1 0.9 collective-permute-start.18
  132.0 0.0 collective-permute-done.19.right1
  132.0 1.6 %collective-permute-done.20.right2 = bf16[3,64,1024]{2,1,0:T(8,128)(2,1)S(1)} collective-permute-done((bf16[3,64,1024]{2,1,0:T(8,128)(2,1)}, bf16[3,64,1024]{2,1,0:T(8,128)(2,1)S(1)}, u32[]{:S(2)}, u32[]{:S(2)}) %collective-permute-start.20) | collective-permute-done | bytes 393248 | tf_op jit(solution)/shard_map/ppermute | solution.py:315
  133.7 0.0 collective-permute-done.21.right3
  133.7 1.3 collective-permute-done.17.left2
  135.0 1.2 collective-permute-done.18.left3
  136.2 3.3 %gram_sum.1 = (f32[3,64,1024]{2,1,0:T(8,128)}, f32[3,64,1024]{2,1,0:T(8,128)}) custom-call(s32[2]{0:T(128)S(1)} %pad_add_fusion.here, s32[3]{0:T(128)S(1)} %dynamic_slice.3.used, f32[3,64,256]{2,1,0:T(8,128)S(1)} %get-tuple-element.102.own, f32[3,64,128]{2,1,0:T(8,128)S(1)} %get-tuple-element.103.left0, ...), custom_call_target="tpu_custom_call" | custom-call | bytes 8388608 | tf_op jit(solution)/shard_map/gram_sum/pallas_call | solution.py:327
  139.5 1.2 gather_fusion
  (17 shorter events, 0.1 us)
Async XLA Ops:
  3.1 19.6 %collective-permute-start.1 = (bf16[4,8,10240]{2,1,0:T(8,128)(2,1)S(1)}, bf16[4,8,10240]{2,1,0:T(8,128)(2,1)S(1)}, u32[]{:S(2)}, u32[]{:S(2)}) collective-permute-start(bf16[4,8,10240]{2,1,0:T(8,128)(2,1)S(1)} %get-tuple-element.65), channel_id=1, source_target_pairs={{0,32},{8,40},{16,48},{24,56},{32,64},{40,72},{48,80},{56,88},{64,... | collective-permute-start | bytes 1966088 | tf_op jit(solution)/shard_map/ppermute | solution.py:322
  5.3 17.4 %collective-permute-start.3 = (bf16[4,8,10240]{2,1,0:T(8,128)(2,1)S(1)}, bf16[4,8,10240]{2,1,0:T(8,128)(2,1)S(1)}, u32[]{:S(2)}, u32[]{:S(2)}) collective-permute-start(bf16[4,8,10240]{2,1,0:T(8,128)(2,1)S(1)} %get-tuple-element.67), channel_id=1, source_target_pairs={{0,96},{8,104},{16,112},{24,120},{32,0},{40,8},{48,16},{56,24},{64... | collective-permute-start | bytes 1966088 | tf_op jit(solution)/shard_map/ppermute | solution.py:322
  6.8 9.2 %collective-permute-start = (bf16[8,18432]{1,0:T(8,128)(2,1)S(1)}, bf16[8,18432]{1,0:T(8,128)(2,1)S(1)}, u32[]{:S(2)}, u32[]{:S(2)}) collective-permute-start(bf16[8,18432]{1,0:T(8,128)(2,1)S(1)} %get-tuple-element.64), channel_id=1, source_target_pairs={{0,8},{8,16},{16,24},{24,0},{32,40},{40,48},{48,56},{56,32},{64,72... | collective-permute-start | bytes 884744 | tf_op jit(solution)/shard_map/ppermute | solution.py:315
  8.0 8.0 %collective-permute-start.2 = (bf16[8,18432]{1,0:T(8,128)(2,1)S(1)}, bf16[8,18432]{1,0:T(8,128)(2,1)S(1)}, u32[]{:S(2)}, u32[]{:S(2)}) collective-permute-start(bf16[8,18432]{1,0:T(8,128)(2,1)S(1)} %get-tuple-element.66), channel_id=1, source_target_pairs={{0,24},{8,0},{16,8},{24,16},{32,56},{40,32},{48,40},{56,48},{64,88... | collective-permute-start | bytes 884744 | tf_op jit(solution)/shard_map/ppermute | solution.py:315
  9.5 35.6 %copy-start.3 = (s32[12]{0:T(128)S(1)}, s32[12]{0:T(128)}, u32[]{:S(2)}) copy-start(s32[12]{0:T(128)} %param.9) | copy-start | bytes 148
  9.5 13.2 %collective-permute-start.4 = (bf16[8,18432]{1,0:T(8,128)(2,1)S(1)}, bf16[8,18432]{1,0:T(8,128)(2,1)S(1)}, u32[]{:S(2)}, u32[]{:S(2)}) collective-permute-start(bf16[8,18432]{1,0:T(8,128)(2,1)S(1)} %get-tuple-element.68), channel_id=1, source_target_pairs={{0,16},{8,24},{16,0},{24,8},{32,48},{40,56},{48,32},{56,40},{64,80... | collective-permute-start | bytes 884744 | tf_op jit(solution)/shard_map/ppermute | solution.py:315
  22.8 25.1 %all-to-all-start = ((bf16[16,3,64,128]{3,2,1,0:T(8,128)(2,1)}), bf16[16,3,64,128]{3,2,1,0:T(8,128)(2,1)S(1)}, u32[]{:S(2)}, u32[]{:S(2)}) async-start(bf16[16,3,64,128]{3,2,1,0:T(8,128)(2,1)} %moment_right.1), calls=%async_computation | async-start | bytes 1572864 | tf_op jit(solution)/shard_map/all_to_all | solution.py:408
  29.4 18.5 %collective-permute-start.7 = (bf16[8,12288]{1,0:T(8,128)(2,1)S(1)}, bf16[8,12288]{1,0:T(8,128)(2,1)S(1)}, u32[]{:S(2)}, u32[]{:S(2)}) collective-permute-start(bf16[8,12288]{1,0:T(8,128)(2,1)S(1)} %get-tuple-element.77), channel_id=1, source_target_pairs={{0,64},{8,72},{16,80},{24,88},{32,96},{40,104},{48,112},{56,120},{... | collective-permute-start | bytes 589832 | tf_op jit(solution)/shard_map/ppermute | solution.py:322
  32.4 15.5 %collective-permute-start.10 = (bf16[8,10240]{1,0:T(8,128)(2,1)S(1)}, bf16[8,10240]{1,0:T(8,128)(2,1)S(1)}, u32[]{:S(2)}, u32[]{:S(2)}) collective-permute-start(bf16[8,10240]{1,0:T(8,128)(2,1)S(1)} %get-tuple-element.81), channel_id=1, source_target_pairs={{0,16},{8,24},{16,0},{24,8},{32,48},{40,56},{48,32},{56,40},{64,80... | collective-permute-start | bytes 491528 | tf_op jit(solution)/shard_map/ppermute | solution.py:315
  35.1 12.8 %collective-permute-start.8 = (bf16[8,10240]{1,0:T(8,128)(2,1)S(1)}, bf16[8,10240]{1,0:T(8,128)(2,1)S(1)}, u32[]{:S(2)}, u32[]{:S(2)}) collective-permute-start(bf16[8,10240]{1,0:T(8,128)(2,1)S(1)} %get-tuple-element.79), channel_id=1, source_target_pairs={{0,8},{8,16},{16,24},{24,0},{32,40},{40,48},{48,56},{56,32},{64,72... | collective-permute-start | bytes 491528 | tf_op jit(solution)/shard_map/ppermute | solution.py:315
  35.3 12.5 %collective-permute-start.9 = (bf16[8,10240]{1,0:T(8,128)(2,1)S(1)}, bf16[8,10240]{1,0:T(8,128)(2,1)S(1)}, u32[]{:S(2)}, u32[]{:S(2)}) collective-permute-start(bf16[8,10240]{1,0:T(8,128)(2,1)S(1)} %get-tuple-element.80), channel_id=1, source_target_pairs={{0,24},{8,0},{16,8},{24,16},{32,56},{40,32},{48,40},{56,48},{64,88... | collective-permute-start | bytes 491528 | tf_op jit(solution)/shard_map/ppermute | solution.py:315
  37.7 7.4 %collective-permute-start.5 = (bf16[8,2048]{1,0:T(8,128)(2,1)S(1)}, bf16[8,2048]{1,0:T(8,128)(2,1)S(1)}, u32[]{:S(2)}, u32[]{:S(2)}) collective-permute-start(bf16[8,2048]{1,0:T(8,128)(2,1)S(1)} %get-tuple-element.75), channel_id=1, source_target_pairs={{0,32},{8,40},{16,48},{24,56},{32,64},{40,72},{48,80},{56,88},{64,... | collective-permute-start | bytes 98312 | tf_op jit(solution)/shard_map/ppermute | solution.py:322
  45.1 2.8 %collective-permute-start.6 = (bf16[8,2048]{1,0:T(8,128)(2,1)S(1)}, bf16[8,2048]{1,0:T(8,128)(2,1)S(1)}, u32[]{:S(2)}, u32[]{:S(2)}) collective-permute-start(bf16[8,2048]{1,0:T(8,128)(2,1)S(1)} %get-tuple-element.76), channel_id=1, source_target_pairs={{0,96},{8,104},{16,112},{24,120},{32,0},{40,8},{48,16},{56,24},{64... | collective-permute-start | bytes 98312 | tf_op jit(solution)/shard_map/ppermute | solution.py:322
  49.3 15.8 %all-to-all-start.1 = ((bf16[8,3,8,1024]{3,2,1,0:T(8,128)(2,1)}), bf16[8,3,8,1024]{3,2,1,0:T(8,128)(2,1)S(1)}, u32[]{:S(2)}, u32[]{:S(2)}) async-start(bf16[8,3,8,1024]{3,2,1,0:T(8,128)(2,1)} %bitcast.3), calls=%async_computation.1 | async-start | bytes 786432 | tf_op jit(solution)/shard_map/all_to_all | solution.py:408
  65.2 25.9 %copy-start = (bf16[3,64,1024]{2,1,0:T(8,128)(2,1)}, bf16[3,64,1024]{2,1,0:T(8,128)(2,1)S(1)}, u32[]{:S(2)}) copy-start(bf16[3,64,1024]{2,1,0:T(8,128)(2,1)S(1)} %copy_bitcast_fusion.rows) | copy-start | bytes 1179652
  71.3 13.3 %all-to-all-start.2 = ((bf16[16,3,32,128]{3,2,1,0:T(8,128)(2,1)}), bf16[16,3,32,128]{3,2,1,0:T(8,128)(2,1)S(1)}, u32[]{:S(2)}, u32[]{:S(2)}) async-start(bf16[16,3,32,128]{3,2,1,0:T(8,128)(2,1)} %get-tuple-element.95), calls=%async_computation.2 | async-start | bytes 786432 | tf_op jit(solution)/shard_map/all_to_all | solution.py:408
  75.5 15.6 %collective-permute-start.11 = (bf16[3,64,1024]{2,1,0:T(8,128)(2,1)S(1)}, bf16[3,64,1024]{2,1,0:T(8,128)(2,1)S(1)}, u32[]{:S(2)}, u32[]{:S(2)}) collective-permute-start(bf16[3,64,1024]{2,1,0:T(8,128)(2,1)S(1)} %copy_bitcast_fusion.rows), channel_id=1, source_target_pairs={{0,64},{8,72},{16,80},{24,88},{32,96},{40,104},{48,112},{56,120},{... | collective-permute-start | bytes 1179656 | tf_op jit(solution)/shard_map/ppermute | solution.py:322
  78.4 12.7 %collective-permute-start.12 = (bf16[3,64,1024]{2,1,0:T(8,128)(2,1)S(1)}, bf16[3,64,1024]{2,1,0:T(8,128)(2,1)S(1)}, u32[]{:S(2)}, u32[]{:S(2)}) collective-permute-start(bf16[3,64,1024]{2,1,0:T(8,128)(2,1)S(1)} %copy_bitcast_fusion.rows), channel_id=1, source_target_pairs={{0,16},{8,24},{16,0},{24,8},{32,48},{40,56},{48,32},{56,40},{64,80... | collective-permute-start | bytes 1179656 | tf_op jit(solution)/shard_map/ppermute | solution.py:315
  81.1 19.9 %collective-permute-start.13 = (bf16[3,64,1024]{2,1,0:T(8,128)(2,1)S(1)}, bf16[3,64,1024]{2,1,0:T(8,128)(2,1)}, u32[]{:S(2)}, u32[]{:S(2)}) collective-permute-start(bf16[3,64,1024]{2,1,0:T(8,128)(2,1)S(1)} %copy_bitcast_fusion.rows), channel_id=1, source_target_pairs={{0,32},{8,40},{16,48},{24,56},{32,64},{40,72},{48,80},{56,88},{64,... | collective-permute-start | bytes 1179656 | tf_op jit(solution)/shard_map/ppermute | solution.py:322
  81.4 19.6 %collective-permute-start.14 = (bf16[3,64,1024]{2,1,0:T(8,128)(2,1)S(1)}, bf16[3,64,1024]{2,1,0:T(8,128)(2,1)}, u32[]{:S(2)}, u32[]{:S(2)}) collective-permute-start(bf16[3,64,1024]{2,1,0:T(8,128)(2,1)S(1)} %copy_bitcast_fusion.rows), channel_id=1, source_target_pairs={{0,96},{8,104},{16,112},{24,120},{32,0},{40,8},{48,16},{56,24},{64... | collective-permute-start | bytes 1179656 | tf_op jit(solution)/shard_map/ppermute | solution.py:322
  83.8 17.2 %collective-permute-start.15 = (bf16[3,64,1024]{2,1,0:T(8,128)(2,1)S(1)}, bf16[3,64,1024]{2,1,0:T(8,128)(2,1)}, u32[]{:S(2)}, u32[]{:S(2)}) collective-permute-start(bf16[3,64,1024]{2,1,0:T(8,128)(2,1)S(1)} %copy_bitcast_fusion.rows), channel_id=1, source_target_pairs={{0,8},{8,16},{16,24},{24,0},{32,40},{40,48},{48,56},{56,32},{64,72... | collective-permute-start | bytes 1179656 | tf_op jit(solution)/shard_map/ppermute | solution.py:315
  91.1 14.3 %copy-start.1 = (bf16[3,64,1024]{2,1,0:T(8,128)(2,1)}, bf16[3,64,1024]{2,1,0:T(8,128)(2,1)S(1)}, u32[]{:S(2)}) copy-start(bf16[3,64,1024]{2,1,0:T(8,128)(2,1)S(1)} %collective-permute-done.11.y2) | copy-start | bytes 1179652
  91.2 9.8 %copy-start.2 = (bf16[3,64,1024]{2,1,0:T(8,128)(2,1)}, bf16[3,64,1024]{2,1,0:T(8,128)(2,1)S(1)}, u32[]{:S(2)}) copy-start(bf16[3,64,1024]{2,1,0:T(8,128)(2,1)S(1)} %collective-permute-done.12.x2) | copy-start | bytes 1179652
  101.0 17.6 %all-to-all-start.3 = ((bf16[16,3,64,128]{3,2,1,0:T(8,128)(2,1)}), bf16[16,3,64,128]{3,2,1,0:T(8,128)(2,1)S(1)}, u32[]{:S(2)}, u32[]{:S(2)}) async-start(bf16[16,3,64,128]{3,2,1,0:T(8,128)(2,1)} %rotate_left.1), calls=%async_computation.3 | async-start | bytes 1572864 | tf_op jit(solution)/shard_map/all_to_all | solution.py:408
  110.8 22.8 %collective-permute-start.21 = (bf16[3,64,1280]{2,1,0:T(8,128)(2,1)}, bf16[3,64,1280]{2,1,0:T(8,128)(2,1)S(1)}, u32[]{:S(2)}, u32[]{:S(2)}) collective-permute-start(bf16[3,64,1280]{2,1,0:T(8,128)(2,1)} %get-tuple-element.112), channel_id=1, source_target_pairs={{0,24},{8,0},{16,8},{24,16},{32,56},{40,32},{48,40},{56,48},{64,88... | collective-permute-start | bytes 1474568 | tf_op jit(solution)/shard_map/ppermute | solution.py:315
  113.5 4.2 %collective-permute-start.16 = (bf16[3,64,128]{2,1,0:T(8,128)(2,1)S(1)}, bf16[3,64,128]{2,1,0:T(8,128)(2,1)S(1)}, u32[]{:S(2)}, u32[]{:S(2)}) collective-permute-start(bf16[3,64,128]{2,1,0:T(8,128)(2,1)S(1)} %get-tuple-element.104), channel_id=1, source_target_pairs={{0,96},{8,104},{16,112},{24,120},{32,0},{40,8},{48,16},{56,24},{64... | collective-permute-start | bytes 147464 | tf_op jit(solution)/shard_map/ppermute | solution.py:322
  115.9 16.1 %collective-permute-start.19 = (bf16[3,64,1024]{2,1,0:T(8,128)(2,1)}, bf16[3,64,1024]{2,1,0:T(8,128)(2,1)S(1)}, u32[]{:S(2)}, u32[]{:S(2)}) collective-permute-start(bf16[3,64,1024]{2,1,0:T(8,128)(2,1)} %get-tuple-element.110), channel_id=1, source_target_pairs={{0,8},{8,16},{16,24},{24,0},{32,40},{40,48},{48,56},{56,32},{64,72... | collective-permute-start | bytes 1179656 | tf_op jit(solution)/shard_map/ppermute | solution.py:315
  115.9 17.8 %collective-permute-start.20 = (bf16[3,64,1024]{2,1,0:T(8,128)(2,1)}, bf16[3,64,1024]{2,1,0:T(8,128)(2,1)S(1)}, u32[]{:S(2)}, u32[]{:S(2)}) collective-permute-start(bf16[3,64,1024]{2,1,0:T(8,128)(2,1)} %get-tuple-element.111), channel_id=1, source_target_pairs={{0,16},{8,24},{16,0},{24,8},{32,48},{40,56},{48,32},{56,40},{64,80... | collective-permute-start | bytes 1179656 | tf_op jit(solution)/shard_map/ppermute | solution.py:315
  123.9 15.7 %all-to-all-start.4 = ((bf16[8,3,8,1024]{3,2,1,0:T(8,128)(2,1)}), bf16[8,3,8,1024]{3,2,1,0:T(8,128)(2,1)S(1)}, u32[]{:S(2)}, u32[]{:S(2)}) async-start(bf16[8,3,8,1024]{3,2,1,0:T(8,128)(2,1)} %get-tuple-element.114), calls=%async_computation.4 | async-start | bytes 786432 | tf_op jit(solution)/shard_map/all_to_all | solution.py:408
  130.2 4.7 %collective-permute-start.17 = (bf16[3,64,128]{2,1,0:T(8,128)(2,1)S(1)}, bf16[3,64,128]{2,1,0:T(8,128)(2,1)S(1)}, u32[]{:S(2)}, u32[]{:S(2)}) collective-permute-start(bf16[3,64,128]{2,1,0:T(8,128)(2,1)S(1)} %get-tuple-element.107), channel_id=1, source_target_pairs={{0,64},{8,72},{16,80},{24,88},{32,96},{40,104},{48,112},{56,120},{... | collective-permute-start | bytes 147464 | tf_op jit(solution)/shard_map/ppermute | solution.py:322
  131.1 5.1 %collective-permute-start.18 = (bf16[3,64,128]{2,1,0:T(8,128)(2,1)S(1)}, bf16[3,64,128]{2,1,0:T(8,128)(2,1)S(1)}, u32[]{:S(2)}, u32[]{:S(2)}) collective-permute-start(bf16[3,64,128]{2,1,0:T(8,128)(2,1)S(1)} %get-tuple-element.108), channel_id=1, source_target_pairs={{0,32},{8,40},{16,48},{24,56},{32,64},{40,72},{48,80},{56,88},{64,... | collective-permute-start | bytes 147464 | tf_op jit(solution)/shard_map/ppermute | solution.py:322

commit v6 on v5

--- a/solution.py
+++ b/solution.py
@@ -235,13 +235,16 @@
     slots, slab, order = rows.shape
     lines = SIDE * slab
     start = pl.multiple_of(y * lines, lines)
-    copies = []
-    for back, ref in enumerate((x1, x2)):
-        copies.append(pltpu.make_async_copy(ref, across.at[back], sems.at[0, back]))
-    for back, ref in enumerate((rows, y1, y2, y3)):
-        copies.append(pltpu.make_async_copy(ref, down.at[back], sems.at[1, back]))
-    wait_all(start_all(copies))
+    arrivals = []
     for slot in range(slots):
+        copies = []
+        for back, ref in enumerate((rows, y1, y2, y3)):
+            copies.append(pltpu.make_async_copy(ref.at[slot], down.at[back, slot], sems.at[slot, back]))
+        for back, ref in enumerate((x1, x2)):
+            copies.append(pltpu.make_async_copy(ref.at[slot], across.at[back, slot], sems.at[slot, SIDE + back]))
+        arrivals.append(start_all(copies))
+    for slot in range(slots):
+        wait_all(arrivals[slot])
         panel = down[:, slot].reshape(lines, order)
         tile = dot(panel, across[:, slot].reshape(2 * slab, order), NT)
         own[slot] = dot(down[0, slot], panel, NT)
@@ -452,7 +455,7 @@
         + [(slabs, F32, VMEM), (slabs, BF16, VMEM), (slabs, BF16, VMEM), ((slots, slab, order + SIDE * slab), BF16, VMEM)],
         [
             pltpu.VMEM((2, slots, slab, order), BF16), pltpu.VMEM((SIDE, slots, slab, order), BF16),
-            pltpu.VMEM((SIDE, slab, order), F32), pltpu.SemaphoreType.DMA((2, SIDE)),
+            pltpu.VMEM((SIDE, slab, order), F32), pltpu.SemaphoreType.DMA((slots, SIDE + 2)),
         ],
         9, 6,
     )

time: 141 us -> 141 us (level)
  no operation moved by 1% of the time
where the time goes in v6:
time: 141 us
  starting transfers between devices  61 us (43%)
  Pallas kernels  40.8 us (29%)
  waiting for transfers between devices  36.5 us (26%)
    pallas_call x10, Pallas kernels, call(): pl.pallas_call(kernel, in_specs=[pl.BlockSpec(memory_space=space) for _,...  40.8 us
    all_to_all x5, starting transfers between devices, exchange(): return lax.all_to_all(value, axis, split_axis=0, concat_axis=0, tiled=True)  27.4 us
    ppermute x11, waiting for transfers between devices, along_y(): return lax.ppermute(value, 'dp', pairs)  22.3 us
    ppermute x11, starting transfers between devices, along_x(): return lax.ppermute(value, 'dp', pairs)  16.9 us
    ppermute x11, starting transfers between devices, along_y(): return lax.ppermute(value, 'dp', pairs)  16.6 us
    ppermute x11, waiting for transfers between devices, along_x(): return lax.ppermute(value, 'dp', pairs)  8.38 us
    all_to_all x5, waiting for transfers between devices, exchange(): return lax.all_to_all(value, axis, split_axis=0, concat_axis=0, tiled=True)  5.85 us
  transfers between devices with their start and end apart: 27, of which 11 were waited for; matrix products, arithmetic and copies ran while one was open for 0% of the time, Pallas kernels for 22%

profile of v6, /device:TPU:1, one launch (start us, length us, event | category | flops | bytes accessed | tf_op | source)
XLA Modules:
  0.0 140.8 jit_solution(5476111166712314060)
XLA Ops:
  0.7 0.1 pad_add_fusion.here
  0.7 2.4 %first_send.1 = (bf16[8,18432]{1,0:T(8,128)(2,1)S(1)}, bf16[4,8,10240]{2,1,0:T(8,128)(2,1)S(1)}, bf16[8,18432]{1,0:T(8,128)(2,1)S(1)}, bf16[4,8,10240]{2,1,0:T(8,128)(2,1)S(1)}, bf16[8,18432]{1,0:T(8,128)(2,1)S(1)}) custom-call(s32[2]{0:T(128)S(1)} %pad_add_fusion.here, bf16[4,4,8,12288]{3,2,1,0:T(8,128)(2,1)} %bitcast.13), custom_call_target="tpu_custom_call" | custom-call | bytes 5242880 | tf_op jit(solution)/shard_map/first_send/pallas_call | solution.py:330
  3.1 2.2 %collective-permute-start.1 = (bf16[4,8,10240]{2,1,0:T(8,128)(2,1)S(1)}, bf16[4,8,10240]{2,1,0:T(8,128)(2,1)S(1)}, u32[]{:S(2)}, u32[]{:S(2)}) collective-permute-start(bf16[4,8,10240]{2,1,0:T(8,128)(2,1)S(1)} %get-tuple-element.65), channel_id=1, source_target_pairs={{0,32},{8,40},{16,48},{24,56},{32,64},{40,72},{48,80},{56,88},{64,... | collective-permute-start | bytes 1966088 | tf_op jit(solution)/shard_map/ppermute | solution.py:325
  5.3 1.5 %collective-permute-start.3 = (bf16[4,8,10240]{2,1,0:T(8,128)(2,1)S(1)}, bf16[4,8,10240]{2,1,0:T(8,128)(2,1)S(1)}, u32[]{:S(2)}, u32[]{:S(2)}) collective-permute-start(bf16[4,8,10240]{2,1,0:T(8,128)(2,1)S(1)} %get-tuple-element.67), channel_id=1, source_target_pairs={{0,96},{8,104},{16,112},{24,120},{32,0},{40,8},{48,16},{56,24},{64... | collective-permute-start | bytes 1966088 | tf_op jit(solution)/shard_map/ppermute | solution.py:325
  6.8 1.2 collective-permute-start
  8.0 1.5 %collective-permute-start.2 = (bf16[8,18432]{1,0:T(8,128)(2,1)S(1)}, bf16[8,18432]{1,0:T(8,128)(2,1)S(1)}, u32[]{:S(2)}, u32[]{:S(2)}) collective-permute-start(bf16[8,18432]{1,0:T(8,128)(2,1)S(1)} %get-tuple-element.66), channel_id=1, source_target_pairs={{0,24},{8,0},{16,8},{24,16},{32,56},{40,32},{48,40},{56,48},{64,88... | collective-permute-start | bytes 884744 | tf_op jit(solution)/shard_map/ppermute | solution.py:318
  9.5 1.5 %collective-permute-start.4 = (bf16[8,18432]{1,0:T(8,128)(2,1)S(1)}, bf16[8,18432]{1,0:T(8,128)(2,1)S(1)}, u32[]{:S(2)}, u32[]{:S(2)}) collective-permute-start(bf16[8,18432]{1,0:T(8,128)(2,1)S(1)} %get-tuple-element.68), channel_id=1, source_target_pairs={{0,16},{8,24},{16,0},{24,8},{32,48},{40,56},{48,32},{56,40},{64,80... | collective-permute-start | bytes 884744 | tf_op jit(solution)/shard_map/ppermute | solution.py:318
  11.0 5.0 %moment_right.1 = bf16[16,3,64,128]{3,2,1,0:T(8,128)(2,1)} custom-call(bf16[3,64,1024]{2,1,0:T(8,128)(2,1)} %moment_hbm.3, bf16[3,64,1024]{2,1,0:T(8,128)(2,1)} %second_hbm.1, bf16[3,1024,1024]{2,1,0:T(8,128)(2,1)} %basis_hbm.9), custom_call_target="tpu_custom_call" | custom-call | flops 402653184 | bytes 8388608 | tf_op jit(solution)/shard_map/moment_right/pallas_call | solution.py:330
  16.0 0.0 collective-permute-done.a1
  16.0 0.0 collective-permute-done.2.a3
  16.0 6.7 %collective-permute-done.4.a2 = bf16[8,18432]{1,0:T(8,128)(2,1)S(1)} collective-permute-done((bf16[8,18432]{1,0:T(8,128)(2,1)S(1)}, bf16[8,18432]{1,0:T(8,128)(2,1)S(1)}, u32[]{:S(2)}, u32[]{:S(2)}) %collective-permute-start.4) | collective-permute-done | bytes 294944 | tf_op jit(solution)/shard_map/ppermute | solution.py:318
  22.7 0.0 collective-permute-done.1.b1
  22.8 0.0 collective-permute-done.3.b3
  22.8 4.6 %all-to-all-start = ((bf16[16,3,64,128]{3,2,1,0:T(8,128)(2,1)}), bf16[16,3,64,128]{3,2,1,0:T(8,128)(2,1)S(1)}, u32[]{:S(2)}, u32[]{:S(2)}) async-start(bf16[16,3,64,128]{3,2,1,0:T(8,128)(2,1)} %moment_right.1), calls=%async_computation | async-start | bytes 1572864 | tf_op jit(solution)/shard_map/all_to_all | solution.py:411
  27.3 2.1 %second_send.1 = (bf16[8,2048]{1,0:T(8,128)(2,1)S(1)}, bf16[8,2048]{1,0:T(8,128)(2,1)S(1)}, bf16[8,12288]{1,0:T(8,128)(2,1)S(1)}, bf16[8,2048]{1,0:T(8,128)(2,1)...) custom-call(s32[2]{0:T(128)S(1)} %pad_add_fusion.here, ...), custom_call_target="tpu_custom_call" | custom-call | bytes 4194304 | tf_op jit(solution)/shard_map/second_send/pallas_call | solution.py:330
  29.4 2.9 %collective-permute-start.7 = (bf16[8,12288]{1,0:T(8,128)(2,1)S(1)}, bf16[8,12288]{1,0:T(8,128)(2,1)S(1)}, u32[]{:S(2)}, u32[]{:S(2)}) collective-permute-start(bf16[8,12288]{1,0:T(8,128)(2,1)S(1)} %get-tuple-element.77), channel_id=1, source_target_pairs={{0,64},{8,72},{16,80},{24,88},{32,96},{40,104},{48,112},{56,120},{... | collective-permute-start | bytes 589832 | tf_op jit(solution)/shard_map/ppermute | solution.py:325
  32.4 2.7 %collective-permute-start.10 = (bf16[8,10240]{1,0:T(8,128)(2,1)S(1)}, bf16[8,10240]{1,0:T(8,128)(2,1)S(1)}, u32[]{:S(2)}, u32[]{:S(2)}) collective-permute-start(bf16[8,10240]{1,0:T(8,128)(2,1)S(1)} %get-tuple-element.81), channel_id=1, source_target_pairs={{0,16},{8,24},{16,0},{24,8},{32,48},{40,56},{48,32},{56,40},{64,80... | collective-permute-start | bytes 491528 | tf_op jit(solution)/shard_map/ppermute | solution.py:318
  35.1 0.3 collective-permute-start.8
  35.3 2.4 %collective-permute-start.9 = (bf16[8,10240]{1,0:T(8,128)(2,1)S(1)}, bf16[8,10240]{1,0:T(8,128)(2,1)S(1)}, u32[]{:S(2)}, u32[]{:S(2)}) collective-permute-start(bf16[8,10240]{1,0:T(8,128)(2,1)S(1)} %get-tuple-element.80), channel_id=1, source_target_pairs={{0,24},{8,0},{16,8},{24,16},{32,56},{40,32},{48,40},{56,48},{64,88... | collective-permute-start | bytes 491528 | tf_op jit(solution)/shard_map/ppermute | solution.py:318
  37.7 0.3 collective-permute-start.5
  38.0 7.1 %collective-permute-done.5.p1 = bf16[8,2048]{1,0:T(8,128)(2,1)S(1)} collective-permute-done((bf16[8,2048]{1,0:T(8,128)(2,1)S(1)}, bf16[8,2048]{1,0:T(8,128)(2,1)S(1)}, u32[]{:S(2)}, u32[]{:S(2)}) %collective-permute-start.5) | collective-permute-done | bytes 32800 | tf_op jit(solution)/shard_map/ppermute | solution.py:325
  45.1 0.0 collective-permute-start.6
  45.1 0.1 select_reduce_fusion.holder
  45.2 2.7 %collective-permute-done.6.p3 = bf16[8,2048]{1,0:T(8,128)(2,1)S(1)} collective-permute-done((bf16[8,2048]{1,0:T(8,128)(2,1)S(1)}, bf16[8,2048]{1,0:T(8,128)(2,1)S(1)}, u32[]{:S(2)}, u32[]{:S(2)}) %collective-permute-start.6) | collective-permute-done | bytes 32800 | tf_op jit(solution)/shard_map/ppermute | solution.py:325
  47.9 0.0 collective-permute-done.10.q2
  47.9 0.0 collective-permute-done.8.q1
  47.9 0.0 collective-permute-done.9.q3
  47.9 0.0 collective-permute-done.7.p2
  47.9 1.4 %outgoing.1 = bf16[24,8,1024]{2,1,0:T(8,128)(2,1)} custom-call(s32[24]{0:T(128)S(1)} %select_reduce_fusion.holder, bf16[8,2048]{1,0:T(8,128)(2,1)S(1)} %get-tuple-element.83.p0, bf16[8,2048]{1,0:T(8,128)(2,1)S(1)} %collective-permute-done.5.p1, bf16[8,2048]{1,0:T(8,128)(2,1)S(1)} %collective-permute-done.6.p3, ...), custom_call_target="tpu_custom_call" | custom-call | bytes 1048576 | tf_op jit(solution)/shard_map/outgoing/pallas_call | solution.py:330
  49.3 7.7 %all-to-all-start.1 = ((bf16[8,3,8,1024]{3,2,1,0:T(8,128)(2,1)}), bf16[8,3,8,1024]{3,2,1,0:T(8,128)(2,1)S(1)}, u32[]{:S(2)}, u32[]{:S(2)}) async-start(bf16[8,3,8,1024]{3,2,1,0:T(8,128)(2,1)} %bitcast.3), calls=%async_computation.1 | async-start | bytes 786432 | tf_op jit(solution)/shard_map/all_to_all | solution.py:411
  57.1 0.1 fusion
  57.2 0.1 dynamic_slice.3.used
  57.3 3.4 %moment_left.1.ready = f32[3,128,1024]{2,1,0:T(8,128)S(1)} custom-call(bf16[16,3,64,128]{3,2,1,0:T(8,128)(2,1)S(1)} %all-to-all-done.packed, bf16[3,1024,1024]{2,1,0:T(8,128)(2,1)} %basis_hbm.8), custom_call_target="tpu_custom_call" | custom-call | flops 402653184 | bytes 8388608 | tf_op jit(solution)/shard_map/moment_left/pallas_call | solution.py:330
  60.7 4.5 %all-to-all-done.1 = bf16[8,3,8,1024]{3,2,1,0:T(8,128)(2,1)S(1)} async-done(((bf16[8,3,8,1024]{3,2,1,0:T(8,128)(2,1)}), bf16[8,3,8,1024]{3,2,1,0:T(8,128)(2,1)S(1)}, u32[]{:S(2)}, u32[]{:S(2)}) %all-to-all-start.1) | async-done | bytes 393248 | tf_op jit(solution)/shard_map/all_to_all | solution.py:411
  65.2 0.0 copy-start
  65.2 6.0 %rotate_right.1 = (bf16[3,64,1024]{2,1,0:T(8,128)(2,1)}, bf16[16,3,32,128]{3,2,1,0:T(8,128)(2,1)}) custom-call(s32[3]{0:T(128)S(1)} %dynamic_slice.3.used, bf16[3,64,1024]{2,1,0:T(8,128)(2,1)S(1)} %copy_bitcast_fusion.rows, bf16[3,64,1024]{2,1,0:T(8,128)(2,1)} %moment_hbm.3, bf16[3,1024,1024]{2,1,0:T(8,128)(2,1)} %basis_hbm.9), custom_call_target="tpu_custom_call" | custom-call | flops 402653184 | bytes 8388608 | tf_op jit(solution)/shard_map/rotate_right/pallas_call | solution.py:330
  71.3 4.3 %all-to-all-start.2 = ((bf16[16,3,32,128]{3,2,1,0:T(8,128)(2,1)}), bf16[16,3,32,128]{3,2,1,0:T(8,128)(2,1)S(1)}, u32[]{:S(2)}, u32[]{:S(2)}) async-start(bf16[16,3,32,128]{3,2,1,0:T(8,128)(2,1)} %get-tuple-element.95), calls=%async_computation.2 | async-start | bytes 786432 | tf_op jit(solution)/shard_map/all_to_all | solution.py:411
  75.5 2.9 %collective-permute-start.11 = (bf16[3,64,1024]{2,1,0:T(8,128)(2,1)S(1)}, bf16[3,64,1024]{2,1,0:T(8,128)(2,1)S(1)}, u32[]{:S(2)}, u32[]{:S(2)}) collective-permute-start(bf16[3,64,1024]{2,1,0:T(8,128)(2,1)S(1)} %copy_bitcast_fusion.rows), channel_id=1, source_target_pairs={{0,64},{8,72},{16,80},{24,88},{32,96},{40,104},{48,112},{56,120},{... | collective-permute-start | bytes 1179656 | tf_op jit(solution)/shard_map/ppermute | solution.py:325
  78.4 2.7 %collective-permute-start.12 = (bf16[3,64,1024]{2,1,0:T(8,128)(2,1)S(1)}, bf16[3,64,1024]{2,1,0:T(8,128)(2,1)S(1)}, u32[]{:S(2)}, u32[]{:S(2)}) collective-permute-start(bf16[3,64,1024]{2,1,0:T(8,128)(2,1)S(1)} %copy_bitcast_fusion.rows), channel_id=1, source_target_pairs={{0,16},{8,24},{16,0},{24,8},{32,48},{40,56},{48,32},{56,40},{64,80... | collective-permute-start | bytes 1179656 | tf_op jit(solution)/shard_map/ppermute | solution.py:318
  81.1 0.3 collective-permute-start.13
  81.4 2.4 %collective-permute-start.14 = (bf16[3,64,1024]{2,1,0:T(8,128)(2,1)S(1)}, bf16[3,64,1024]{2,1,0:T(8,128)(2,1)}, u32[]{:S(2)}, u32[]{:S(2)}) collective-permute-start(bf16[3,64,1024]{2,1,0:T(8,128)(2,1)S(1)} %copy_bitcast_fusion.rows), channel_id=1, source_target_pairs={{0,96},{8,104},{16,112},{24,120},{32,0},{40,8},{48,16},{56,24},{64... | collective-permute-start | bytes 1179656 | tf_op jit(solution)/shard_map/ppermute | solution.py:325
  83.8 0.3 collective-permute-start.15
  84.1 0.5 all-to-all-done.2.packed
  84.6 6.5 %rotate_left.1 = bf16[16,3,64,128]{3,2,1,0:T(8,128)(2,1)} custom-call(bf16[16,3,32,128]{3,2,1,0:T(8,128)(2,1)S(1)} %all-to-all-done.2.packed, bf16[3,1024,1024]{2,1,0:T(8,128)(2,1)} %basis_hbm.8, f32[3,128,1024]{2,1,0:T(8,128)S(1)} %moment_left.1.ready), custom_call_target="tpu_custom_call" | custom-call | flops 1207959552 | bytes 8388608 | tf_op jit(solution)/shard_map/rotate_left/pallas_call | solution.py:330
  91.1 0.0 collective-permute-done.12.x2
  91.2 9.8 %collective-permute-done.13.y1 = bf16[3,64,1024]{2,1,0:T(8,128)(2,1)} collective-permute-done((bf16[3,64,1024]{2,1,0:T(8,128)(2,1)S(1)}, bf16[3,64,1024]{2,1,0:T(8,128)(2,1)}, u32[]{:S(2)}, u32[]{:S(2)}) %collective-permute-start.13) | collective-permute-done | bytes 393248 | tf_op jit(solution)/shard_map/ppermute | solution.py:325
  101.0 0.0 collective-permute-done.14.y3
  101.0 0.0 collective-permute-done.15.x1
  101.0 4.4 %all-to-all-start.3 = ((bf16[16,3,64,128]{3,2,1,0:T(8,128)(2,1)}), bf16[16,3,64,128]{3,2,1,0:T(8,128)(2,1)S(1)}, u32[]{:S(2)}, u32[]{:S(2)}) async-start(bf16[16,3,64,128]{3,2,1,0:T(8,128)(2,1)} %rotate_left.1), calls=%async_computation.3 | async-start | bytes 1572864 | tf_op jit(solution)/shard_map/all_to_all | solution.py:411
  105.4 5.4 %gram_tiles.1 = (f32[3,64,256]{2,1,0:T(8,128)S(1)}, f32[3,64,128]{2,1,0:T(8,128)S(1)}, bf16[3,64,128]{2,1,0:T(8,128)(2,1)S(1)}, bf16[3,64,128]{2,1,0:T(8,128)(2,...) custom-call(s32[2]{0:T(128)S(1)} %pad_add_fusion.here, ...), custom_call_target="tpu_custom_call" | custom-call | flops 1207959552 | bytes 6291456 | tf_op jit(solution)/shard_map/gram_tiles/pallas_call | solution.py:330
  110.8 2.6 %collective-permute-start.21 = (bf16[3,64,1280]{2,1,0:T(8,128)(2,1)}, bf16[3,64,1280]{2,1,0:T(8,128)(2,1)S(1)}, u32[]{:S(2)}, u32[]{:S(2)}) collective-permute-start(bf16[3,64,1280]{2,1,0:T(8,128)(2,1)} %get-tuple-element.112), channel_id=1, source_target_pairs={{0,24},{8,0},{16,8},{24,16},{32,56},{40,32},{48,40},{56,48},{64,88... | collective-permute-start | bytes 1474568 | tf_op jit(solution)/shard_map/ppermute | solution.py:318
  113.5 2.4 %collective-permute-start.16 = (bf16[3,64,128]{2,1,0:T(8,128)(2,1)S(1)}, bf16[3,64,128]{2,1,0:T(8,128)(2,1)S(1)}, u32[]{:S(2)}, u32[]{:S(2)}) collective-permute-start(bf16[3,64,128]{2,1,0:T(8,128)(2,1)S(1)} %get-tuple-element.104), channel_id=1, source_target_pairs={{0,96},{8,104},{16,112},{24,120},{32,0},{40,8},{48,16},{56,24},{64... | collective-permute-start | bytes 147464 | tf_op jit(solution)/shard_map/ppermute | solution.py:325
  115.9 1.8 %collective-permute-start.20 = (bf16[3,64,1024]{2,1,0:T(8,128)(2,1)}, bf16[3,64,1024]{2,1,0:T(8,128)(2,1)S(1)}, u32[]{:S(2)}, u32[]{:S(2)}) collective-permute-start(bf16[3,64,1024]{2,1,0:T(8,128)(2,1)} %get-tuple-element.111), channel_id=1, source_target_pairs={{0,16},{8,24},{16,0},{24,8},{32,48},{40,56},{48,32},{56,40},{64,80... | collective-permute-start | bytes 1179656 | tf_op jit(solution)/shard_map/ppermute | solution.py:318
  117.6 0.1 collective-permute-done.16.left1
  117.7 0.8 all-to-all-done.3.packed
  118.6 5.3 %step_rows.1 = (bf16[3,64,1024]{2,1,0:T(8,128)(2,1)}, bf16[8,3,8,1024]{3,2,1,0:T(8,128)(2,1)}) custom-call(s32[3]{0:T(128)S(1)} %dynamic_slice.3.used, bf16[16,3,64,128]{3,2,1,0:T(8,128)(2,1)S(1)} %all-to-all-done.3.packed, bf16[3,1024,1024]{2,1,0:T(8,128)(2,1)} %basis_hbm.9), custom_call_target="tpu_custom_call" | custom-call | flops 402653184 | bytes 8388608 | tf_op jit(solution)/shard_map/step_rows/pallas_call | solution.py:330
  123.9 6.4 %all-to-all-start.4 = ((bf16[8,3,8,1024]{3,2,1,0:T(8,128)(2,1)}), bf16[8,3,8,1024]{3,2,1,0:T(8,128)(2,1)S(1)}, u32[]{:S(2)}, u32[]{:S(2)}) async-start(bf16[8,3,8,1024]{3,2,1,0:T(8,128)(2,1)} %get-tuple-element.114), calls=%async_computation.4 | async-start | bytes 786432 | tf_op jit(solution)/shard_map/all_to_all | solution.py:411
  130.3 0.9 collective-permute-start.17
  131.2 0.8 collective-permute-start.18
  132.0 1.7 %collective-permute-done.20.right2 = bf16[3,64,1024]{2,1,0:T(8,128)(2,1)S(1)} collective-permute-done((bf16[3,64,1024]{2,1,0:T(8,128)(2,1)}, bf16[3,64,1024]{2,1,0:T(8,128)(2,1)S(1)}, u32[]{:S(2)}, u32[]{:S(2)}) %collective-permute-start.20) | collective-permute-done | bytes 393248 | tf_op jit(solution)/shard_map/ppermute | solution.py:318
  133.6 1.4 collective-permute-done.17.left2
  135.0 1.2 collective-permute-done.18.left3
  136.2 3.3 %gram_sum.1 = (f32[3,64,1024]{2,1,0:T(8,128)}, f32[3,64,1024]{2,1,0:T(8,128)}) custom-call(s32[2]{0:T(128)S(1)} %pad_add_fusion.here, s32[3]{0:T(128)S(1)} %dynamic_slice.3.used, f32[3,64,256]{2,1,0:T(8,128)S(1)} %get-tuple-element.102.own, f32[3,64,128]{2,1,0:T(8,128)S(1)} %get-tuple-element.103.left0, ...), custom_call_target="tpu_custom_call" | custom-call | bytes 8388608 | tf_op jit(solution)/shard_map/gram_sum/pallas_call | solution.py:330
  139.6 1.2 gather_fusion
  (17 shorter events, 0.1 us)
Async XLA Ops:
  3.1 19.6 %collective-permute-start.1 = (bf16[4,8,10240]{2,1,0:T(8,128)(2,1)S(1)}, bf16[4,8,10240]{2,1,0:T(8,128)(2,1)S(1)}, u32[]{:S(2)}, u32[]{:S(2)}) collective-permute-start(bf16[4,8,10240]{2,1,0:T(8,128)(2,1)S(1)} %get-tuple-element.65), channel_id=1, source_target_pairs={{0,32},{8,40},{16,48},{24,56},{32,64},{40,72},{48,80},{56,88},{64,... | collective-permute-start | bytes 1966088 | tf_op jit(solution)/shard_map/ppermute | solution.py:325
  5.3 17.4 %collective-permute-start.3 = (bf16[4,8,10240]{2,1,0:T(8,128)(2,1)S(1)}, bf16[4,8,10240]{2,1,0:T(8,128)(2,1)S(1)}, u32[]{:S(2)}, u32[]{:S(2)}) collective-permute-start(bf16[4,8,10240]{2,1,0:T(8,128)(2,1)S(1)} %get-tuple-element.67), channel_id=1, source_target_pairs={{0,96},{8,104},{16,112},{24,120},{32,0},{40,8},{48,16},{56,24},{64... | collective-permute-start | bytes 1966088 | tf_op jit(solution)/shard_map/ppermute | solution.py:325
  6.8 9.2 %collective-permute-start = (bf16[8,18432]{1,0:T(8,128)(2,1)S(1)}, bf16[8,18432]{1,0:T(8,128)(2,1)S(1)}, u32[]{:S(2)}, u32[]{:S(2)}) collective-permute-start(bf16[8,18432]{1,0:T(8,128)(2,1)S(1)} %get-tuple-element.64), channel_id=1, source_target_pairs={{0,8},{8,16},{16,24},{24,0},{32,40},{40,48},{48,56},{56,32},{64,72... | collective-permute-start | bytes 884744 | tf_op jit(solution)/shard_map/ppermute | solution.py:318
  8.0 8.0 %collective-permute-start.2 = (bf16[8,18432]{1,0:T(8,128)(2,1)S(1)}, bf16[8,18432]{1,0:T(8,128)(2,1)S(1)}, u32[]{:S(2)}, u32[]{:S(2)}) collective-permute-start(bf16[8,18432]{1,0:T(8,128)(2,1)S(1)} %get-tuple-element.66), channel_id=1, source_target_pairs={{0,24},{8,0},{16,8},{24,16},{32,56},{40,32},{48,40},{56,48},{64,88... | collective-permute-start | bytes 884744 | tf_op jit(solution)/shard_map/ppermute | solution.py:318
  9.5 35.6 %copy-start.3 = (s32[12]{0:T(128)S(1)}, s32[12]{0:T(128)}, u32[]{:S(2)}) copy-start(s32[12]{0:T(128)} %param.9) | copy-start | bytes 148
  9.5 13.2 %collective-permute-start.4 = (bf16[8,18432]{1,0:T(8,128)(2,1)S(1)}, bf16[8,18432]{1,0:T(8,128)(2,1)S(1)}, u32[]{:S(2)}, u32[]{:S(2)}) collective-permute-start(bf16[8,18432]{1,0:T(8,128)(2,1)S(1)} %get-tuple-element.68), channel_id=1, source_target_pairs={{0,16},{8,24},{16,0},{24,8},{32,48},{40,56},{48,32},{56,40},{64,80... | collective-permute-start | bytes 884744 | tf_op jit(solution)/shard_map/ppermute | solution.py:318
  22.8 25.1 %all-to-all-start = ((bf16[16,3,64,128]{3,2,1,0:T(8,128)(2,1)}), bf16[16,3,64,128]{3,2,1,0:T(8,128)(2,1)S(1)}, u32[]{:S(2)}, u32[]{:S(2)}) async-start(bf16[16,3,64,128]{3,2,1,0:T(8,128)(2,1)} %moment_right.1), calls=%async_computation | async-start | bytes 1572864 | tf_op jit(solution)/shard_map/all_to_all | solution.py:411
  29.4 18.5 %collective-permute-start.7 = (bf16[8,12288]{1,0:T(8,128)(2,1)S(1)}, bf16[8,12288]{1,0:T(8,128)(2,1)S(1)}, u32[]{:S(2)}, u32[]{:S(2)}) collective-permute-start(bf16[8,12288]{1,0:T(8,128)(2,1)S(1)} %get-tuple-element.77), channel_id=1, source_target_pairs={{0,64},{8,72},{16,80},{24,88},{32,96},{40,104},{48,112},{56,120},{... | collective-permute-start | bytes 589832 | tf_op jit(solution)/shard_map/ppermute | solution.py:325
  32.4 15.5 %collective-permute-start.10 = (bf16[8,10240]{1,0:T(8,128)(2,1)S(1)}, bf16[8,10240]{1,0:T(8,128)(2,1)S(1)}, u32[]{:S(2)}, u32[]{:S(2)}) collective-permute-start(bf16[8,10240]{1,0:T(8,128)(2,1)S(1)} %get-tuple-element.81), channel_id=1, source_target_pairs={{0,16},{8,24},{16,0},{24,8},{32,48},{40,56},{48,32},{56,40},{64,80... | collective-permute-start | bytes 491528 | tf_op jit(solution)/shard_map/ppermute | solution.py:318
  35.1 12.8 %collective-permute-start.8 = (bf16[8,10240]{1,0:T(8,128)(2,1)S(1)}, bf16[8,10240]{1,0:T(8,128)(2,1)S(1)}, u32[]{:S(2)}, u32[]{:S(2)}) collective-permute-start(bf16[8,10240]{1,0:T(8,128)(2,1)S(1)} %get-tuple-element.79), channel_id=1, source_target_pairs={{0,8},{8,16},{16,24},{24,0},{32,40},{40,48},{48,56},{56,32},{64,72... | collective-permute-start | bytes 491528 | tf_op jit(solution)/shard_map/ppermute | solution.py:318
  35.3 12.5 %collective-permute-start.9 = (bf16[8,10240]{1,0:T(8,128)(2,1)S(1)}, bf16[8,10240]{1,0:T(8,128)(2,1)S(1)}, u32[]{:S(2)}, u32[]{:S(2)}) collective-permute-start(bf16[8,10240]{1,0:T(8,128)(2,1)S(1)} %get-tuple-element.80), channel_id=1, source_target_pairs={{0,24},{8,0},{16,8},{24,16},{32,56},{40,32},{48,40},{56,48},{64,88... | collective-permute-start | bytes 491528 | tf_op jit(solution)/shard_map/ppermute | solution.py:318
  37.7 7.4 %collective-permute-start.5 = (bf16[8,2048]{1,0:T(8,128)(2,1)S(1)}, bf16[8,2048]{1,0:T(8,128)(2,1)S(1)}, u32[]{:S(2)}, u32[]{:S(2)}) collective-permute-start(bf16[8,2048]{1,0:T(8,128)(2,1)S(1)} %get-tuple-element.75), channel_id=1, source_target_pairs={{0,32},{8,40},{16,48},{24,56},{32,64},{40,72},{48,80},{56,88},{64,... | collective-permute-start | bytes 98312 | tf_op jit(solution)/shard_map/ppermute | solution.py:325
  45.1 2.8 %collective-permute-start.6 = (bf16[8,2048]{1,0:T(8,128)(2,1)S(1)}, bf16[8,2048]{1,0:T(8,128)(2,1)S(1)}, u32[]{:S(2)}, u32[]{:S(2)}) collective-permute-start(bf16[8,2048]{1,0:T(8,128)(2,1)S(1)} %get-tuple-element.76), channel_id=1, source_target_pairs={{0,96},{8,104},{16,112},{24,120},{32,0},{40,8},{48,16},{56,24},{64... | collective-permute-start | bytes 98312 | tf_op jit(solution)/shard_map/ppermute | solution.py:325
  49.3 15.8 %all-to-all-start.1 = ((bf16[8,3,8,1024]{3,2,1,0:T(8,128)(2,1)}), bf16[8,3,8,1024]{3,2,1,0:T(8,128)(2,1)S(1)}, u32[]{:S(2)}, u32[]{:S(2)}) async-start(bf16[8,3,8,1024]{3,2,1,0:T(8,128)(2,1)} %bitcast.3), calls=%async_computation.1 | async-start | bytes 786432 | tf_op jit(solution)/shard_map/all_to_all | solution.py:411
  65.2 25.9 %copy-start = (bf16[3,64,1024]{2,1,0:T(8,128)(2,1)}, bf16[3,64,1024]{2,1,0:T(8,128)(2,1)S(1)}, u32[]{:S(2)}) copy-start(bf16[3,64,1024]{2,1,0:T(8,128)(2,1)S(1)} %copy_bitcast_fusion.rows) | copy-start | bytes 1179652
  71.3 13.3 %all-to-all-start.2 = ((bf16[16,3,32,128]{3,2,1,0:T(8,128)(2,1)}), bf16[16,3,32,128]{3,2,1,0:T(8,128)(2,1)S(1)}, u32[]{:S(2)}, u32[]{:S(2)}) async-start(bf16[16,3,32,128]{3,2,1,0:T(8,128)(2,1)} %get-tuple-element.95), calls=%async_computation.2 | async-start | bytes 786432 | tf_op jit(solution)/shard_map/all_to_all | solution.py:411
  75.5 15.6 %collective-permute-start.11 = (bf16[3,64,1024]{2,1,0:T(8,128)(2,1)S(1)}, bf16[3,64,1024]{2,1,0:T(8,128)(2,1)S(1)}, u32[]{:S(2)}, u32[]{:S(2)}) collective-permute-start(bf16[3,64,1024]{2,1,0:T(8,128)(2,1)S(1)} %copy_bitcast_fusion.rows), channel_id=1, source_target_pairs={{0,64},{8,72},{16,80},{24,88},{32,96},{40,104},{48,112},{56,120},{... | collective-permute-start | bytes 1179656 | tf_op jit(solution)/shard_map/ppermute | solution.py:325
  78.4 12.7 %collective-permute-start.12 = (bf16[3,64,1024]{2,1,0:T(8,128)(2,1)S(1)}, bf16[3,64,1024]{2,1,0:T(8,128)(2,1)S(1)}, u32[]{:S(2)}, u32[]{:S(2)}) collective-permute-start(bf16[3,64,1024]{2,1,0:T(8,128)(2,1)S(1)} %copy_bitcast_fusion.rows), channel_id=1, source_target_pairs={{0,16},{8,24},{16,0},{24,8},{32,48},{40,56},{48,32},{56,40},{64,80... | collective-permute-start | bytes 1179656 | tf_op jit(solution)/shard_map/ppermute | solution.py:318
  81.1 19.9 %collective-permute-start.13 = (bf16[3,64,1024]{2,1,0:T(8,128)(2,1)S(1)}, bf16[3,64,1024]{2,1,0:T(8,128)(2,1)}, u32[]{:S(2)}, u32[]{:S(2)}) collective-permute-start(bf16[3,64,1024]{2,1,0:T(8,128)(2,1)S(1)} %copy_bitcast_fusion.rows), channel_id=1, source_target_pairs={{0,32},{8,40},{16,48},{24,56},{32,64},{40,72},{48,80},{56,88},{64,... | collective-permute-start | bytes 1179656 | tf_op jit(solution)/shard_map/ppermute | solution.py:325
  81.4 19.6 %collective-permute-start.14 = (bf16[3,64,1024]{2,1,0:T(8,128)(2,1)S(1)}, bf16[3,64,1024]{2,1,0:T(8,128)(2,1)}, u32[]{:S(2)}, u32[]{:S(2)}) collective-permute-start(bf16[3,64,1024]{2,1,0:T(8,128)(2,1)S(1)} %copy_bitcast_fusion.rows), channel_id=1, source_target_pairs={{0,96},{8,104},{16,112},{24,120},{32,0},{40,8},{48,16},{56,24},{64... | collective-permute-start | bytes 1179656 | tf_op jit(solution)/shard_map/ppermute | solution.py:325
  83.8 17.2 %collective-permute-start.15 = (bf16[3,64,1024]{2,1,0:T(8,128)(2,1)S(1)}, bf16[3,64,1024]{2,1,0:T(8,128)(2,1)}, u32[]{:S(2)}, u32[]{:S(2)}) collective-permute-start(bf16[3,64,1024]{2,1,0:T(8,128)(2,1)S(1)} %copy_bitcast_fusion.rows), channel_id=1, source_target_pairs={{0,8},{8,16},{16,24},{24,0},{32,40},{40,48},{48,56},{56,32},{64,72... | collective-permute-start | bytes 1179656 | tf_op jit(solution)/shard_map/ppermute | solution.py:318
  91.1 14.3 %copy-start.1 = (bf16[3,64,1024]{2,1,0:T(8,128)(2,1)}, bf16[3,64,1024]{2,1,0:T(8,128)(2,1)S(1)}, u32[]{:S(2)}) copy-start(bf16[3,64,1024]{2,1,0:T(8,128)(2,1)S(1)} %collective-permute-done.11.y2) | copy-start | bytes 1179652
  91.2 9.8 %copy-start.2 = (bf16[3,64,1024]{2,1,0:T(8,128)(2,1)}, bf16[3,64,1024]{2,1,0:T(8,128)(2,1)S(1)}, u32[]{:S(2)}) copy-start(bf16[3,64,1024]{2,1,0:T(8,128)(2,1)S(1)} %collective-permute-done.12.x2) | copy-start | bytes 1179652
  101.0 17.6 %all-to-all-start.3 = ((bf16[16,3,64,128]{3,2,1,0:T(8,128)(2,1)}), bf16[16,3,64,128]{3,2,1,0:T(8,128)(2,1)S(1)}, u32[]{:S(2)}, u32[]{:S(2)}) async-start(bf16[16,3,64,128]{3,2,1,0:T(8,128)(2,1)} %rotate_left.1), calls=%async_computation.3 | async-start | bytes 1572864 | tf_op jit(solution)/shard_map/all_to_all | solution.py:411
  110.8 22.8 %collective-permute-start.21 = (bf16[3,64,1280]{2,1,0:T(8,128)(2,1)}, bf16[3,64,1280]{2,1,0:T(8,128)(2,1)S(1)}, u32[]{:S(2)}, u32[]{:S(2)}) collective-permute-start(bf16[3,64,1280]{2,1,0:T(8,128)(2,1)} %get-tuple-element.112), channel_id=1, source_target_pairs={{0,24},{8,0},{16,8},{24,16},{32,56},{40,32},{48,40},{56,48},{64,88... | collective-permute-start | bytes 1474568 | tf_op jit(solution)/shard_map/ppermute | solution.py:318
  113.5 4.3 %collective-permute-start.16 = (bf16[3,64,128]{2,1,0:T(8,128)(2,1)S(1)}, bf16[3,64,128]{2,1,0:T(8,128)(2,1)S(1)}, u32[]{:S(2)}, u32[]{:S(2)}) collective-permute-start(bf16[3,64,128]{2,1,0:T(8,128)(2,1)S(1)} %get-tuple-element.104), channel_id=1, source_target_pairs={{0,96},{8,104},{16,112},{24,120},{32,0},{40,8},{48,16},{56,24},{64... | collective-permute-start | bytes 147464 | tf_op jit(solution)/shard_map/ppermute | solution.py:325
  115.9 16.1 %collective-permute-start.19 = (bf16[3,64,1024]{2,1,0:T(8,128)(2,1)}, bf16[3,64,1024]{2,1,0:T(8,128)(2,1)S(1)}, u32[]{:S(2)}, u32[]{:S(2)}) collective-permute-start(bf16[3,64,1024]{2,1,0:T(8,128)(2,1)} %get-tuple-element.110), channel_id=1, source_target_pairs={{0,8},{8,16},{16,24},{24,0},{32,40},{40,48},{48,56},{56,32},{64,72... | collective-permute-start | bytes 1179656 | tf_op jit(solution)/shard_map/ppermute | solution.py:318
  115.9 17.8 %collective-permute-start.20 = (bf16[3,64,1024]{2,1,0:T(8,128)(2,1)}, bf16[3,64,1024]{2,1,0:T(8,128)(2,1)S(1)}, u32[]{:S(2)}, u32[]{:S(2)}) collective-permute-start(bf16[3,64,1024]{2,1,0:T(8,128)(2,1)} %get-tuple-element.111), channel_id=1, source_target_pairs={{0,16},{8,24},{16,0},{24,8},{32,48},{40,56},{48,32},{56,40},{64,80... | collective-permute-start | bytes 1179656 | tf_op jit(solution)/shard_map/ppermute | solution.py:318
  123.9 15.7 %all-to-all-start.4 = ((bf16[8,3,8,1024]{3,2,1,0:T(8,128)(2,1)}), bf16[8,3,8,1024]{3,2,1,0:T(8,128)(2,1)S(1)}, u32[]{:S(2)}, u32[]{:S(2)}) async-start(bf16[8,3,8,1024]{3,2,1,0:T(8,128)(2,1)} %get-tuple-element.114), calls=%async_computation.4 | async-start | bytes 786432 | tf_op jit(solution)/shard_map/all_to_all | solution.py:411
  130.3 4.7 %collective-permute-start.17 = (bf16[3,64,128]{2,1,0:T(8,128)(2,1)S(1)}, bf16[3,64,128]{2,1,0:T(8,128)(2,1)S(1)}, u32[]{:S(2)}, u32[]{:S(2)}) collective-permute-start(bf16[3,64,128]{2,1,0:T(8,128)(2,1)S(1)} %get-tuple-element.107), channel_id=1, source_target_pairs={{0,64},{8,72},{16,80},{24,88},{32,96},{40,104},{48,112},{56,120},{... | collective-permute-start | bytes 147464 | tf_op jit(solution)/shard_map/ppermute | solution.py:325
  131.2 5.0 %collective-permute-start.18 = (bf16[3,64,128]{2,1,0:T(8,128)(2,1)S(1)}, bf16[3,64,128]{2,1,0:T(8,128)(2,1)S(1)}, u32[]{:S(2)}, u32[]{:S(2)}) collective-permute-start(bf16[3,64,128]{2,1,0:T(8,128)(2,1)S(1)} %get-tuple-element.108), channel_id=1, source_target_pairs={{0,32},{8,40},{16,48},{24,56},{32,64},{40,72},{48,80},{56,88},{64,... | collective-permute-start | bytes 147464 | tf_op jit(solution)/shard_map/ppermute | solution.py:325
